TPU v7x, 32 devices: a whole 2x2x4 slice. The times are simulated.
32 devices in a mesh: groups: 2 (over x), dev: 8 (over z, y), sub: 2 (over core).
Axes of the slice: x: 2, y: 2, z: 4, core: 2. Of those that a mesh axis runs over, the one named last changes fastest.
Arguments:
- hidden: bfloat16 [1024, 2048], P(('groups', 'dev', 'sub')), parts along dimension 0, may hold values from -6 to 6
- lengths: int32 [32, 32], P(('groups', 'dev', 'sub')), parts along dimension 0, may hold values from 1 to 256, 4096 in all within a row
- key_cache: bfloat16 [32, 4096, 512], P(('groups', 'dev', 'sub')), parts along dimension 0, may hold values from -320 to 320
- value_cache: bfloat16 [32, 4096, 512], P(('groups', 'dev', 'sub')), parts along dimension 0, may hold values from -6 to 6
- expert_ids: int32 [1024, 8], P(('groups', 'dev', 'sub')), parts along dimension 0, may hold values from 0 to 15, all different within a row; in each aligned block of 32 rows (0 to 31, 32 to 63, ...) at most 16 rows name the same one
- gate_codes: int32 [1024, 8], P(('groups', 'dev', 'sub')), parts along dimension 0, may hold values from 1 to 1023
- expert_device: int32 [16], replicated, may hold values from 0 to 15, each once
- attention_gain: float32 [2048], replicated, may hold values from 0.1 to 1.9
- mixture_gain: float32 [2048], replicated, may hold values from 0.1 to 1.9
- query_gain: float32 [128], replicated, may hold values from 0.1 to 1.9
- key_gain: float32 [128], replicated, may hold values from 0.1 to 1.9
- project_weight: bfloat16 [2048, 5120], P(None, 'dev'), may hold values from -0.125 to 0.125
- output_weight: bfloat16 [4096, 2048], P('dev'), may hold values from -0.09375 to 0.09375
- expert_gate_up: bfloat16 [16, 2048, 1536], P(('dev', 'sub')), may hold values from -0.125 to 0.125
- expert_down: bfloat16 [16, 768, 2048], P(('dev', 'sub')), may hold values from -0.21875 to 0.21875
Outputs:
- layer_out: bfloat16 [1024, 2048], P(('groups', 'dev', 'sub')), parts along dimension 0
There are 2 independent parts, one for each index of `groups`. A program takes and returns all parts, laid end to end along the dimension named above; an argument that names none is the same for every part. Nothing has to cross between parts.
Inputs may be any that keep to these rules, and one draw needn't show every extreme that they name: `expert_ids`: each row names 8 different experts. Among the 32 rows of one device no expert is named more than 16 times, and in some device an expert is named exactly 16 times. The 32 lengths of each device sum to 4096; the largest of them is 256. A permutation: expert e is held by the device at index expert_device[e] of the joined axes dev and sub.
All inputs are finite; a program needn't handle non-finite values.
Results may differ from a plain program's by a relative error of at most 0.015.
Values may be sent and summed in bfloat16 or wider, within the bound.
No kernel may reach another device: no remote copies, remote signals or barrier semaphores. Data moves between devices by JAX's collectives and lax.ppermute only.
A program may use at most 128 MiB of HBM per device.

v0:
```python
import math

import jax
import jax.numpy as jnp
from jax import lax
from jax.sharding import PartitionSpec as P

D = 2048
HEADS = 32
KVH = 4
HD = 128
TOP = 8
CAP = 16


EPSILON = 1e-06
ROPE_BASE = 1000000.0


def norm_scale(values, scale_gain):
    mean_square = jnp.mean(values * values, axis=-1, keepdims=True)
    return values * lax.rsqrt(mean_square + EPSILON) * scale_gain


def rotate(values, position):
    half_width = values.shape[-1] // 2
    frequency = ROPE_BASE ** (-jnp.arange(half_width, dtype=jnp.float32) * 2.0 / values.shape[-1])
    angles = position.astype(jnp.float32)[:, None] * frequency[None, :]
    cosine = jnp.cos(angles)[:, None, :]
    sine_part = jnp.sin(angles)[:, None, :]
    first_half = values[..., :half_width]
    second_half = values[..., half_width:]
    return jnp.concatenate(
        [
            first_half * cosine - second_half * sine_part,
            second_half * cosine + first_half * sine_part,
        ],
        axis=-1,
    )


def split_heads(merged, position, query_gain, key_gain):
    row_count = merged.shape[0]
    query_cols = HEADS * HD
    key_cols = KVH * HD
    queries = merged[:, :query_cols].astype(jnp.float32).reshape(row_count, HEADS, HD)
    queries = rotate(norm_scale(queries, query_gain), position).astype(jnp.bfloat16)
    new_keys = (
        merged[:, query_cols : query_cols + key_cols]
        .astype(jnp.float32)
        .reshape(row_count, KVH, HD)
    )
    new_keys = rotate(norm_scale(new_keys, key_gain), position).astype(jnp.bfloat16)
    new_values = merged[:, query_cols + key_cols :].reshape(row_count, KVH, HD)
    return (queries, new_keys, new_values)


def attend(queries, new_keys, new_values, key_rows, value_rows, lengths):
    row_count, head_count, head_width = queries.shape
    kv_count = new_keys.shape[1]
    group_size = head_count // kv_count
    pool_size = key_rows.shape[0]
    seg_end = jnp.cumsum(lengths)
    seg_start = seg_end - lengths
    position = jnp.arange(pool_size, dtype=jnp.int32)
    inside = (position[None, :] >= seg_start[:, None]) & (position[None, :] < seg_end[:, None])
    grouped = queries.reshape(row_count, kv_count, group_size, head_width)
    keyed = key_rows.reshape(pool_size, kv_count, head_width)
    valued = value_rows.reshape(pool_size, kv_count, head_width)
    scale = 1.0 / math.sqrt(head_width)
    scores = (
        jnp.einsum("rkgd,pkd->krgp", grouped, keyed, preferred_element_type=jnp.float32) * scale
    )
    own_score = (
        jnp.einsum("rkgd,rkd->krg", grouped.astype(jnp.float32), new_keys.astype(jnp.float32))
        * scale
    )
    mask = inside[None, :, None, :]
    masked = jnp.where(mask, scores, -1e30)
    peak = jnp.maximum(jnp.max(masked, axis=3), own_score)
    raised = jnp.where(mask, jnp.exp(masked - peak[..., None]), 0.0)
    own_raised = jnp.exp(own_score - peak)
    denominator = jnp.sum(raised, axis=3) + own_raised
    weights = (raised / denominator[..., None]).astype(jnp.bfloat16)
    mixed_out = jnp.einsum("krgp,pkd->rkgd", weights, valued, preferred_element_type=jnp.float32)
    own_weight = jnp.transpose(own_raised / denominator, (1, 0, 2))[..., None]
    own_part = own_weight * new_values.astype(jnp.float32)[:, :, None, :]
    return (mixed_out + own_part).reshape(row_count, head_count * head_width).astype(jnp.bfloat16)


def expert_block(arrived, gate_up, down_rows):
    count = arrived.shape[0] * arrived.shape[1]
    flat = arrived.reshape(count, arrived.shape[2])
    both_parts = jnp.dot(flat, gate_up, preferred_element_type=jnp.float32)
    inner = down_rows.shape[0]
    units = (jax.nn.silu(both_parts[:, :inner]) * both_parts[:, inner:]).astype(jnp.bfloat16)
    result = jnp.dot(units, down_rows, preferred_element_type=jnp.float32).astype(jnp.bfloat16)
    return result.reshape(arrived.shape)


def on_device(
    hidden,
    lengths,
    key_cache,
    value_cache,
    expert_ids,
    gate_codes,
    expert_device,
    attention_gain,
    mixture_gain,
    query_gain,
    key_gain,
    project_weight,
    output_weight,
    expert_gate_up,
    expert_down,
):
    row_count = hidden.shape[0]
    normed = norm_scale(hidden.astype(jnp.float32), attention_gain).astype(jnp.bfloat16)
    merged_cols = jnp.dot(
        lax.all_gather(normed, "dev", axis=0, tiled=True),
        project_weight,
        preferred_element_type=jnp.float32,
    ).astype(jnp.bfloat16)
    merged = lax.all_to_all(merged_cols, "dev", split_axis=0, concat_axis=1, tiled=True)
    position = lengths.reshape(row_count)
    queries, new_keys, new_values = split_heads(merged, position, query_gain, key_gain)
    attention = attend(queries, new_keys, new_values, key_cache[0], value_cache[0], position)
    features = lax.all_to_all(attention, "dev", split_axis=1, concat_axis=0, tiled=True)
    projected = lax.psum_scatter(
        jnp.dot(features, output_weight, preferred_element_type=jnp.float32).astype(jnp.bfloat16),
        "dev",
        scatter_dimension=0,
        tiled=True,
    ).astype(jnp.float32)
    residual = hidden.astype(jnp.float32) + projected
    mixture_in = norm_scale(residual, mixture_gain).astype(jnp.bfloat16)
    expert_count = expert_device.shape[0]
    expert_range = jnp.arange(expert_count, dtype=jnp.int32)
    holder = jnp.sum(
        jnp.where(
            expert_ids[:, :, None] == expert_range[None, None, :], expert_device[None, None, :], 0
        ),
        axis=2,
    )
    flat_holder = holder.reshape(row_count * TOP)
    onehot = (flat_holder[:, None] == expert_range[None, :]).astype(jnp.int32)
    before = jnp.cumsum(onehot, axis=0) - onehot
    slot_index = jnp.sum(before * onehot, axis=1)
    target = flat_holder * CAP + slot_index
    cell_index = jnp.arange(expert_count * CAP, dtype=jnp.int32)
    matched = (target[:, None] == cell_index[None, :]).reshape(row_count, TOP, expert_count * CAP)
    assign = jnp.any(matched, axis=1).astype(jnp.bfloat16)
    share = gate_codes.astype(jnp.float32)
    share = share / jnp.sum(share, axis=1, keepdims=True)
    combine = jnp.sum(jnp.where(matched, share[:, :, None], 0.0), axis=1)
    outgoing = jnp.einsum(
        "rc,rd->cd", assign, mixture_in, preferred_element_type=jnp.float32
    ).astype(jnp.bfloat16)
    outgoing = outgoing.reshape(expert_count, CAP, D)
    gate_up = expert_gate_up[0]
    down_rows = expert_down[0]
    computed = expert_block(
        lax.all_to_all(outgoing, ("dev", "sub"), split_axis=0, concat_axis=0, tiled=True),
        gate_up,
        down_rows,
    )
    returned = lax.all_to_all(computed, ("dev", "sub"), split_axis=0, concat_axis=0, tiled=True)
    returned_flat = returned.reshape(expert_count * CAP, D).astype(jnp.float32)
    routed = jnp.dot(combine, returned_flat, precision=lax.Precision.HIGHEST)
    return (residual + routed).astype(jnp.bfloat16)


def solution(mesh):
    return jax.shard_map(
        on_device,
        mesh=mesh,
        in_specs=(
            P(("groups", "dev", "sub"), None),
            P(("groups", "dev", "sub"), None),
            P(("groups", "dev", "sub"), None, None),
            P(("groups", "dev", "sub"), None, None),
            P(("groups", "dev", "sub"), None),
            P(("groups", "dev", "sub"), None),
            P(),
            P(),
            P(),
            P(),
            P(),
            P(None, "dev"),
            P("dev", None),
            P(("dev", "sub"), None, None),
            P(("dev", "sub"), None, None),
        ),
        out_specs=P(("groups", "dev", "sub"), None),
        check_vma=False,
    )
```

profile of v0, /device:TPU:0, one launch (start us, length us, event | category | flops | bytes accessed | tf_op | source)
XLA Modules:
  0.0 253.2 jit_solution(13442766343679465597)
XLA Ops:
  6.5 0.0 all-gather.2.cloned.1.call-start
  6.5 1.2 fusion.27
  7.7 1.7 fusion.29
  9.4 0.0 all-gather.2.cloned.1.call-update
  9.4 0.7 copy.45
  10.2 0.1 reduce-window.14
  10.2 0.1 reduce
  10.3 6.9 %reshape_squeeze.6 = bf16[4096,4,128]{2,1,0:T(4,128)(2,1)} reshape(bf16[1,4096,512]{2,1,0:T(8,128)(2,1)} %param.17) | data formatting | bytes 8388608 | tf_op jit(solution)/shard_map/reshape;squeeze | solution.py:68
  17.3 7.0 %reshape_squeeze.7 = bf16[4096,4,128]{2,1,0:T(4,128)(2,1)} reshape(bf16[1,4096,512]{2,1,0:T(8,128)(2,1)} %param.18) | data formatting | bytes 8388608 | tf_op jit(solution)/shard_map/reshape;squeeze | solution.py:69
  24.3 0.1 multiply_cosine_fusion
  24.4 28.0 %all-gather.2.cloned.1.call-done = bf16[256,2048]{1,0:T(8,128)(2,1)} async-done(((bf16[32,2048]{1,0:T(8,128)(2,1)}), bf16[256,2048]{1,0:T(8,128)(2,1)}) %all-gather.2.cloned.1.call-update) | async-done | bytes 1048592 | tf_op jit(solution)/shard_map/all_gather | solution.py:121
  52.4 3.8 %convolution_convert_fusion.2 = bf16[256,640]{1,0:T(8,128)(2,1)} fusion(bf16[256,2048]{1,0:T(8,128)(2,1)} %all-gather.2.cloned.1.call-done, bf16[2048,640]{1,0:T(8,128)(2,1)} %param.26), kind=kOutput, calls=%fused_computation.20 | convolution fusion | flops 671252480 | bytes 3997696 | tf_op jit(solution)/shard_map/dot_general | solution.py:120
  56.2 4.1 %all-to-all-start = ((bf16[8,32,640]{2,1,0:T(8,128)(2,1)}), bf16[8,32,640]{2,1,0:T(8,128)(2,1)}, u32[]{:S(2)}, u32[]{:S(2)}) async-start(bf16[8,32,640]{2,1,0:T(8,128)(2,1)} %bitcast.2), calls=%async_computation | async-start | bytes 655360 | tf_op jit(solution)/shard_map/all_to_all | solution.py:125
  60.3 0.0 reduce-scatter.2.cloned.1.call-start
  60.3 0.2 fusion.24
  60.5 9.3 %all-to-all-done = bf16[8,32,640]{2,1,0:T(8,128)(2,1)} async-done(((bf16[8,32,640]{2,1,0:T(8,128)(2,1)}), bf16[8,32,640]{2,1,0:T(8,128)(2,1)}, u32[]{:S(2)}, u32[]{:S(2)}) %all-to-all-start) | async-done | bytes 327712 | tf_op jit(solution)/shard_map/all_to_all | solution.py:125
  69.8 1.0 copy.70
  70.9 0.8 convert_bitcast_fusion
  71.7 0.1 multiply_reduce_fusion.2
  71.9 1.1 copy.72
  73.0 0.2 multiply_reduce_fusion
  73.2 0.1 multiply_multiply_fusion.1
  73.3 0.2 multiply_multiply_fusion
  73.6 0.1 subtract_convert_fusion.1
  73.7 0.2 fusion.30
  73.9 0.1 maximum_bitcast_fusion
  74.0 0.1 pad_maximum_fusion
  74.2 0.3 fusion.33
  74.4 6.5 %fusion = (f32[4,32,8]{2,1,0:T(8,128)S(1)}, f32[4,32,8,4096]{3,2,1,0:T(8,128)S(1)}) fusion(pred[32,4096]{1,0:T(8,128)(4,1)S(1)} %fusion.24, bf16[4096,4,128,1]{2,1,0,3:T(4,128)(2,1)} %bitcast.83, bf16[32,4,8,128]{3,2,1,0:T(8,128)(2,1)S(1)} %pad_maximum_fusion), kind=kOutput, calls=%fused_computation.3 | convolution fusion | flops 1086323712 | bytes 21368832 | tf_op jit(solution)/shard_map/rkgd,pkd->krgp/dot_general | solution.py:72
  80.9 6.0 %fusion.1 = f32[4,32,8]{2,1,0:T(8,128)S(1)} fusion(f32[4,32,8,4096]{3,2,1,0:T(8,128)S(1)} %get-tuple-element.14, f32[4,32,8]{2,1,0:T(8,128)S(1)} %multiply_maximum_fusion, pred[32,4096]{1,0:T(8,128)(4,1)S(1)} %fusion.24), kind=kLoop, calls=%fused_computation.4 | loop fusion | flops 20970496 | bytes 16916480 | tf_op jit(solution)/shard_map/reduce_sum | solution.py:83
  87.0 11.2 %fusion.20 = bf16[32,4,8,128]{3,2,0,1:T(8,128)(2,1)S(1)} fusion(bf16[4096,4,128,1]{2,1,0,3:T(4,128)(2,1)} %bitcast.85, f32[4,32,8,4096]{3,2,1,0:T(8,128)} %copy-done.1, f32[4,32,8]{2,1,0:T(8,128)S(1)} %exponential_add_fusion, f32[4,32,8]{2,1,0:T(8,128)S(1)} %multiply_maximum_fusion, pred[32,4096]{1,0:T(8,128)(4,1)S(1)} %fusion.24, ...), kind=kOutput, calls=%fused_computation.21 | convolution fusion | flops 1099300864 | bytes 21442560 | tf_op jit(solution)/shard_map/krgp,pkd->rkgd/dot_general | solution.py:85
  98.2 0.0 copy-start.6
  98.3 0.0 copy-start.10
  98.3 0.0 copy-start.2
  98.3 0.0 copy-start.5
  98.4 0.9 convert_element_type.86
  99.2 1.0 copy.53
  100.2 11.9 %all_to_all.45 = bf16[32,8,512]{2,0,1:T(8,128)(2,1)S(1)} all-to-all(bf16[32,8,512]{2,0,1:T(8,128)(2,1)S(1)} %copy.53), channel_id=1, replica_groups=mesh['groups'=2,'dev'=8,'sub'=2] {'dev'}, dimensions={1} | all-to-all | bytes 524288 | tf_op jit(solution)/shard_map/all_to_all | solution.py:129
  112.1 3.3 %convolution_convert_fusion = bf16[256,2048]{1,0:T(8,128)(2,1)} fusion(bf16[256,512]{1,0:T(8,128)(2,1)S(1)} %bitcast.91, bf16[512,2048]{1,0:T(8,128)(2,1)} %param.27), kind=kOutput, calls=%fused_computation.13 | convolution fusion | flops 537395200 | bytes 3407872 | tf_op jit(solution)/shard_map/dot_general | solution.py:131
  115.4 0.0 reduce-scatter.2.cloned.1.call-update
  115.4 0.0 copy-done.6
  115.5 0.1 select_reduce_fusion.1
  115.5 0.1 copy.54
  115.6 0.1 eq.59
  115.7 0.1 eq.55
  115.8 0.6 reduce-window.18
  116.4 0.2 slice_reduce_fusion
  116.6 0.1 fusion.42
  116.7 0.1 reduce_sum.92
  116.8 0.1 copy.57
  116.9 0.1 copy.58
  117.0 0.2 fusion.32
  117.1 61.1 %reduce-scatter.2.cloned.1.call-done = bf16[32,2048]{1,0:T(8,128)(2,1)} async-done(((bf16[256,2048]{1,0:T(8,128)(2,1)}), bf16[32,2048]{1,0:T(8,128)(2,1)}) %reduce-scatter.2.cloned.1.call-update) | async-done | bytes 131088 | tf_op jit(solution)/shard_map/reduce_scatter | solution.py:130
  178.3 1.1 multiply_reduce_fusion.1
  179.3 1.4 convolution_convert_fusion.1
  180.7 28.4 %all_to_all.46 = bf16[16,16,2048]{2,1,0:T(8,128)(2,1)S(1)} all-to-all(bf16[16,16,2048]{2,1,0:T(8,128)(2,1)S(1)} %bitcast.86), channel_id=1, replica_groups=mesh['groups'=2,'dev'=8,'sub'=2] {'dev','sub'}, dimensions={0} | all-to-all | bytes 2097152 | tf_op jit(solution)/shard_map/all_to_all | solution.py:164
  209.1 4.6 %fusion.3 = f32[256,1536]{1,0:T(8,128)S(1)} fusion(bf16[256,2048]{1,0:T(8,128)(2,1)S(1)} %bitcast.90, bf16[1,2048,1536]{2,1,0:T(8,128)(2,1)} %param.28), kind=kOutput, calls=%fused_computation.6 | convolution fusion | flops 1610612736 | bytes 8912896 | tf_op jit(solution)/shard_map/dot_general | solution.py:94
  213.7 0.0 copy-start.4
  213.8 2.1 fusion.10
  215.8 5.0 %all-to-all-start.3 = ((bf16[16,16,2048]{2,1,0:T(8,128)(2,1)}), bf16[16,16,2048]{2,1,0:T(8,128)(2,1)}, u32[]{:S(2)}, u32[]{:S(2)}) async-start(bf16[16,16,2048]{2,1,0:T(8,128)(2,1)} %bitcast.89), calls=%async_computation.4 | async-start | bytes 2097152 | tf_op jit(solution)/shard_map/all_to_all | solution.py:168
  220.9 0.1 copy.59
  221.0 0.2 select_reduce_fusion
  221.2 22.7 %all-to-all-done.3 = bf16[16,16,2048]{2,1,0:T(8,128)(2,1)} async-done(((bf16[16,16,2048]{2,1,0:T(8,128)(2,1)}), bf16[16,16,2048]{2,1,0:T(8,128)(2,1)}, u32[]{:S(2)}, u32[]{:S(2)}) %all-to-all-start.3) | async-done | bytes 1048608 | tf_op jit(solution)/shard_map/all_to_all | solution.py:168
  243.9 2.5 fusion.13
  (36 shorter events, 0.3 us)
Async XLA Ops:
  6.5 207.2 %copy-start = (bf16[1,768,2048]{2,1,0:T(8,128)(2,1)S(1)}, bf16[1,768,2048]{2,1,0:T(8,128)(2,1)}, u32[]{:S(2)}) copy-start(bf16[1,768,2048]{2,1,0:T(8,128)(2,1)} %param.29) | copy-start | bytes 9437188
  6.5 45.9 %all-gather.2.cloned.1.call-start = ((), (), s32[]{:S(2)}) async-start(), calls=%async_computation.5 | async-start | bytes 1179648 | tf_op jit(solution)/shard_map/all_gather | solution.py:121
  17.3 7.0 %copy-start.9 = (s32[1,32]{1,0:T(1,128)S(1)}, s32[1,32]{1,0:T(1,128)}, u32[]{:S(2)}) copy-start(s32[1,32]{1,0:T(1,128)} %param.16) | copy-start | bytes 388
  24.2 49.0 %copy-start.7 = (f32[128]{0:T(128)S(1)}, f32[128]{0:T(128)}, u32[]{:S(2)}) copy-start(f32[128]{0:T(128)} %param.25) | copy-start | bytes 1540
  24.2 49.1 %copy-start.8 = (f32[128]{0:T(128)S(1)}, f32[128]{0:T(128)}, u32[]{:S(2)}) copy-start(f32[128]{0:T(128)} %param.24) | copy-start | bytes 1540
  56.2 13.6 %all-to-all-start = ((bf16[8,32,640]{2,1,0:T(8,128)(2,1)}), bf16[8,32,640]{2,1,0:T(8,128)(2,1)}, u32[]{:S(2)}, u32[]{:S(2)}) async-start(bf16[8,32,640]{2,1,0:T(8,128)(2,1)} %bitcast.2), calls=%async_computation | async-start | bytes 655360 | tf_op jit(solution)/shard_map/all_to_all | solution.py:125
  60.3 118.0 %reduce-scatter.2.cloned.1.call-start = ((), (), s32[]{:S(2)}) async-start(), calls=%async_computation.6 | async-start | bytes 1179648 | tf_op jit(solution)/shard_map/reduce_scatter | solution.py:130
  80.9 6.0 %copy-start.1 = (f32[4,32,8,4096]{3,2,1,0:T(8,128)}, f32[4,32,8,4096]{3,2,1,0:T(8,128)S(1)}, u32[]{:S(2)}) copy-start(f32[4,32,8,4096]{3,2,1,0:T(8,128)S(1)} %get-tuple-element.14) | copy-start | bytes 50331652
  98.2 17.2 %copy-start.6 = (s32[32,8]{0,1:T(8,128)S(1)}, s32[32,8]{0,1:T(8,128)}, u32[]{:S(2)}) copy-start(s32[32,8]{0,1:T(8,128)} %param.19) | copy-start | bytes 3076
  98.3 17.2 %copy-start.10 = (s32[16]{0:T(128)S(1)}, s32[16]{0:T(128)}, u32[]{:S(2)}) copy-start(s32[16]{0:T(128)} %param.21) | copy-start | bytes 196
  98.3 80.0 %copy-start.2 = (bf16[32,2048]{1,0:T(8,128)(2,1)S(1)}, bf16[32,2048]{1,0:T(8,128)(2,1)}, u32[]{:S(2)}) copy-start(bf16[32,2048]{1,0:T(8,128)(2,1)} %param.15) | copy-start | bytes 393220
  98.3 81.0 %copy-start.5 = (f32[2048]{0:T(1024)S(1)}, f32[2048]{0:T(1024)}, u32[]{:S(2)}) copy-start(f32[2048]{0:T(1024)} %param.23) | copy-start | bytes 24580
  213.7 7.2 %copy-start.4 = (s32[32,8]{0,1:T(8,128)S(1)}, s32[32,8]{0,1:T(8,128)}, u32[]{:S(2)}) copy-start(s32[32,8]{0,1:T(8,128)} %param.20) | copy-start | bytes 3076
  213.7 30.1 %copy-start.3 = (bf16[32,2048]{1,0:T(8,128)(2,1)S(1)}, bf16[32,2048]{1,0:T(8,128)(2,1)}, u32[]{:S(2)}) copy-start(bf16[32,2048]{1,0:T(8,128)(2,1)} %reduce-scatter.2.cloned.1.call-done) | copy-start | bytes 393220
  215.8 28.0 %all-to-all-start.3 = ((bf16[16,16,2048]{2,1,0:T(8,128)(2,1)}), bf16[16,16,2048]{2,1,0:T(8,128)(2,1)}, u32[]{:S(2)}, u32[]{:S(2)}) async-start(bf16[16,16,2048]{2,1,0:T(8,128)(2,1)} %bitcast.89), calls=%async_computation.4 | async-start | bytes 2097152 | tf_op jit(solution)/shard_map/all_to_all | solution.py:168
Sparse Core Ops, SparseCore 0:
  9.6 42.8 all-gather.1
  115.6 62.6 reduce-scatter.1
where the time goes:
time: 255 us; the launch traced here: 253 us
  waiting for transfers between devices  121 us (47%)
  blocking collectives  40.3 us (16%)
  matrix products  35.6 us (14%)
  local copies, waits for them, and re-layouts  19.5 us (8%)
  between operations  13.8 us (5%)
  other arithmetic  13.7 us (5%)
  starting transfers between devices  9.16 us (4%)
    reduce_scatter x1, waiting for transfers between devices, on_device(): lax.psum_scatter(jnp.dot(features, output_weight, preferred_element_type=...  61.1 us
    all_to_all x1, blocking collectives, on_device(): lax.all_to_all(outgoing, ('dev', 'sub'), split_axis=0, concat_axis=0, til...  28.4 us
    all_gather x1, waiting for transfers between devices, on_device(): lax.all_gather(normed, 'dev', axis=0, tiled=True)  28 us
    all_to_all x1, waiting for transfers between devices, on_device(): lax.all_to_all(computed, ('dev', 'sub'), split_axis=0, concat_axis=0, til...  22.7 us
    all_to_all x1, blocking collectives, on_device(): lax.all_to_all(attention, 'dev', split_axis=1, concat_axis=0, tiled=True)  11.9 us
    dot_general x1, matrix products, attend(): jnp.einsum('krgp,pkd->rkgd', weights, valued, preferred_element_type=jnp....  11.2 us
    all_to_all x1, waiting for transfers between devices, on_device(): lax.all_to_all(merged_cols, 'dev', split_axis=0, concat_axis=1, tiled=True)  9.33 us
    another operation x1, local copies, waits for them, and re-layouts, attend(): valued = value_rows.reshape(pool_size, kv_count, head_width)  6.97 us
  transfers between devices with their start and end apart: 4, of which 4 were waited for; matrix products, arithmetic and copies ran while one was open for 7% of the time, Pallas kernels for 0%

commit v1 on v0

v1 whole, which is shorter than its diff:
```python
import functools
import math

import jax
import jax.numpy as jnp
from jax import lax
from jax.experimental import pallas as pl
from jax.experimental.pallas import tpu as pltpu
from jax.sharding import PartitionSpec as P

HD = 128

EPSILON = 1e-06
ROPE_BASE = 1000000.0
LOG2E = 1.4426950408889634
LONGEST = 256
ALIGN = 16
WINDOW = LONGEST + ALIGN
UNROLL = 8
TILE = 256


def norm_scale(values, scale_gain):
    mean_square = jnp.mean(values * values, axis=-1, keepdims=True)
    return values * lax.rsqrt(mean_square + EPSILON) * scale_gain


def ring_order(count):
    return list(range(0, count, 2)) + list(range(1, count, 2))[::-1]


class Ring:
    def __init__(self, count):
        self.count = count
        self.far = count // 2
        order = ring_order(count)
        self.forward = [(order[i], order[(i + 1) % count]) for i in range(count)]
        self.backward = [(b, a) for a, b in self.forward]
        self.distances = [0]
        for step in range(1, self.far):
            self.distances += [step, -step]
        self.distances += [self.far]

    def ahead(self, values):
        return lax.ppermute(values, "dev", self.forward)

    def behind(self, values):
        return lax.ppermute(values, "dev", self.backward)

    def owners(self):
        count = self.count
        device = lax.axis_index("dev").astype(jnp.int32)
        index = lax.broadcasted_iota(jnp.int32, (1, count), 1)
        step = (index + 1) // 2
        distance = jnp.where(index % 2 == 1, step, -step)
        place = jnp.where(device % 2 == 0, device // 2, count - 1 - device // 2)
        place = place + distance
        place = jnp.where(place < 0, place + count, place)
        place = jnp.where(place >= count, place - count, place)
        return jnp.where(place < self.far, 2 * place, 2 * (count - 1 - place) + 1)


def ring_gather(ring, block):
    half_rows = block.shape[0] // 2
    up, down = block, block
    pieces = [block]
    for step in range(1, ring.far):
        up, down = ring.ahead(up), ring.behind(down)
        pieces += [down, up]
    pieces += [ring.ahead(up[:half_rows]), ring.behind(down[half_rows:])]
    return jnp.concatenate(pieces, axis=0), pieces


def ring_scatter_sum(ring, far_up, far_down, ups, downs):
    half_width = far_up.shape[1]
    sent = jnp.bfloat16
    up, down = ring.ahead(far_up), ring.behind(far_down)
    for distance in range(ring.far - 1, 0, -1):
        mine_up, mine_down = ups[distance - 1], downs[distance - 1]
        up, down = up.astype(jnp.float32), down.astype(jnp.float32)
        if distance == ring.far - 1:
            up = jnp.concatenate([mine_up[:, :half_width] + up, mine_up[:, half_width:]], axis=1)
            down = jnp.concatenate(
                [mine_down[:, :half_width], mine_down[:, half_width:] + down], axis=1
            )
        else:
            up, down = mine_up + up, mine_down + down
        up, down = ring.ahead(up.astype(sent)), ring.behind(down.astype(sent))
    return up, down


def whole_blocks(kinds):
    return [pl.BlockSpec(memory_space=kind) for kind in kinds]


def call(body, outs, ins, operands, scratch, limit, name, cost=100):
    return pl.pallas_call(
        body,
        out_shape=outs,
        in_specs=whole_blocks(ins),
        out_specs=jax.tree.map(lambda _: pl.BlockSpec(memory_space=pltpu.VMEM), outs),
        scratch_shapes=scratch,
        cost_estimate=pl.CostEstimate(
            flops=0, bytes_accessed=cost * 1024 * 1024, transcendentals=0
        ),
        compiler_params=pltpu.CompilerParams(vmem_limit_bytes=limit * 1024 * 1024),
        name=name,
    )(*operands)


VMEM, SMEM, HBM, ANY = pltpu.VMEM, pltpu.SMEM, pltpu.HBM, pl.ANY


def start_copies(pairs, sems):
    copies = [
        pltpu.make_async_copy(source, target, sems.at[index])
        for index, (source, target) in enumerate(pairs)
    ]
    for copy in copies:
        copy.start()
    return copies


def norm_kernel(hidden_hbm, gain_hbm, out_ref, hidden_ref, gain_ref, sems):
    pairs = [(hidden_hbm, hidden_ref), (gain_hbm, gain_ref)]
    for copy in start_copies(pairs, sems):
        copy.wait()
    values = hidden_ref[...].astype(jnp.float32)
    out_ref[...] = norm_scale(values, gain_ref[...]).astype(jnp.bfloat16)


def digit_kernel(holder_ref, ids_ref, codes_ref, out_ref):
    ids, codes = ids_ref[...], codes_ref[...]
    lane = lax.broadcasted_iota(jnp.int32, out_ref.shape, 1)
    high = jnp.zeros(out_ref.shape, jnp.float32)
    for expert in range(holder_ref.shape[1]):
        code = jnp.sum(jnp.where(ids == expert, codes, 0), axis=1, keepdims=True)
        slot = holder_ref[0, expert]
        high = high + jnp.where(lane == slot, (code >> 5).astype(jnp.float32), 0.0)
        high = high + jnp.where(lane == slot + HD // 2, (code & 31).astype(jnp.float32), 0.0)
    out_ref[...] = high.astype(jnp.bfloat16)


def load_kernel(number, *refs):
    sources, targets, sems = refs[:number], refs[-1 - number : -1], refs[-1]
    for copy in start_copies(list(zip(sources, targets)), sems):
        copy.wait()


def loaded(arrays, after, limit, name):
    number = len(arrays)
    return call(
        functools.partial(load_kernel, number),
        [jax.ShapeDtypeStruct(array.shape, array.dtype) for array in arrays],
        [HBM] * number + [ANY],
        (*arrays, after),
        [pltpu.SemaphoreType.DMA((number,))],
        limit,
        name,
    )


def project_kernel(count, owner_ref, normed_ref, weight_ref, out_ref):
    rows = normed_ref.shape[0] // count
    product = jnp.dot(normed_ref[...], weight_ref[...], preferred_element_type=jnp.float32)
    product = product.astype(jnp.bfloat16)
    for index in range(count):
        out_ref[owner_ref[0, index]] = product[index * rows : (index + 1) * rows]


def output_kernel(count, owner_ref, feature_ref, weight_ref, *refs):
    outs, held = refs[:-1], refs[-1]
    rows = feature_ref.shape[1]
    for index in range(count):
        held[index * rows : (index + 1) * rows, :] = feature_ref[owner_ref[0, index]]
    product = jnp.dot(held[...], weight_ref[...], preferred_element_type=jnp.float32)
    split_blocks(count, rows, product, outs)


def split_blocks(count, rows, product, outs):
    own, far_up, far_down, ups, downs = outs
    half_width = product.shape[1] // 2
    own[...] = product[:rows]
    for index in range(1, count - 1):
        side = ups if index % 2 else downs
        side[(index - 1) // 2] = product[index * rows : (index + 1) * rows]
    last = product[(count - 1) * rows :].astype(jnp.bfloat16)
    far_up[...] = last[:, :half_width]
    far_down[...] = last[:, half_width:]


def block_shapes(count, rows, width):
    own = jax.ShapeDtypeStruct((rows, width), jnp.float32)
    half = jax.ShapeDtypeStruct((rows, width // 2), jnp.bfloat16)
    side = jax.ShapeDtypeStruct((count // 2 - 1, rows, width), jnp.float32)
    return [own, half, half, side, side]


def residual_kernel(
    hidden_ref, own_ref, up_ref, down_ref, gain_ref, digit_ref, residual_ref, sent_ref
):
    width = hidden_ref.shape[1]
    summed = own_ref[...] + up_ref[...].astype(jnp.float32) + down_ref[...].astype(jnp.float32)
    residual = hidden_ref[...].astype(jnp.float32) + summed
    residual_ref[...] = residual
    sent_ref[:, :width] = norm_scale(residual, gain_ref[...]).astype(jnp.bfloat16)
    sent_ref[:, width:] = digit_ref[...]


def expert_kernel(count, slots, slot_ref, held, *refs):
    subs = slot_ref.shape[1]
    gate_ups, downs, refs = refs[:subs], refs[subs : 2 * subs], refs[2 * subs :]
    outs, (units, total) = refs[:5], refs[5:]
    width = total.shape[1]
    inner = units.shape[1]
    rows = held.shape[0] // count
    digits = held[:, width:].astype(jnp.float32)
    lane = lax.broadcasted_iota(jnp.int32, digits.shape, 1)
    codes = digits * 32.0 + pltpu.roll(digits, HD // 2, 1)
    codes = jnp.where(lane < slots, codes, 0.0)
    whole = jnp.sum(codes, axis=1, keepdims=True)
    for shift in range(subs):
        mine = jnp.where(lane == slot_ref[0, shift], codes, 0.0)
        weight = jnp.sum(mine, axis=1, keepdims=True) / whole
        for start in range(0, inner, TILE):
            gate, up = [
                jnp.dot(
                    held[:, :width],
                    gate_ups[shift][:, column : column + TILE],
                    preferred_element_type=jnp.float32,
                )
                for column in (start, inner + start)
            ]
            units[:, start : start + TILE] = (jax.nn.silu(gate) * up).astype(jnp.bfloat16)
        for start in range(0, width, 2 * TILE):
            columns = slice(start, start + 2 * TILE)
            result = jnp.dot(
                units[...], downs[shift][:, columns], preferred_element_type=jnp.float32
            )
            result = result.astype(jnp.bfloat16).astype(jnp.float32) * weight
            if shift:
                result = result + total[:, columns]
            total[:, columns] = result
    split_blocks(count, rows, total, outs)


def attention_kernel(
    kv_count,
    length_ref,
    merged_ref,
    cos_ref,
    sin_ref,
    query_gain_ref,
    key_gain_ref,
    key_ref,
    value_ref,
    *refs,
):
    out_ref, queries, results, new_keys, new_values, start_ref = refs[-6:]
    rows = merged_ref.shape[1]
    heads = queries.shape[0] // rows
    group = heads // kv_count
    pool = key_ref.shape[0]
    per_block = merged_ref.shape[2] // HD
    scale = LOG2E / math.sqrt(HD)

    def head(index):
        block, slot = index // per_block, index % per_block
        return merged_ref[block, :, slot * HD : (slot + 1) * HD].astype(jnp.float32)

    def turned(values, gain):
        mean_square = jnp.mean(values * values, axis=-1, keepdims=True)
        values = values * lax.rsqrt(mean_square + EPSILON) * gain
        values = values * cos_ref[...] + pltpu.roll(values, HD // 2, 1) * sin_ref[...]
        return values.astype(jnp.bfloat16).astype(jnp.float32)

    total = jnp.int32(0)
    for row in range(rows):
        start_ref[row] = total
        total = total + length_ref[0, row]
    start_ref[rows] = total

    query_gain = query_gain_ref[...]
    key_gain = key_gain_ref[...]
    for kv in range(kv_count):
        columns = slice(kv * HD, (kv + 1) * HD)
        new_keys[:, columns] = turned(head(heads + kv), key_gain)
        new_values[:, columns] = head(heads + kv_count + kv)
    for index in range(heads):
        queries[pl.ds(index, rows, stride=heads), :] = turned(head(index), query_gain)

    place = lax.broadcasted_iota(jnp.int32, (WINDOW + ALIGN, heads), 0)
    kv_of_row = lax.broadcasted_iota(jnp.int32, (heads, HD), 0) // group

    def with_new(ref, window, fresh, row):
        new = jnp.broadcast_to(fresh[pl.ds(row, 1), :], (ALIGN, fresh.shape[1]))
        return jnp.concatenate([ref[window, :], new.astype(jnp.bfloat16)], axis=0)

    def window_of(row):
        first, last = start_ref[row], start_ref[row + 1]
        base = jnp.minimum(first // ALIGN * ALIGN, pool - WINDOW)
        return first - base, last - base, pl.ds(pl.multiple_of(base, ALIGN), WINDOW)

    def rows_of(row):
        return pl.ds(pl.multiple_of(row * heads, heads), heads)

    def scored(row):
        first, last, window = window_of(row)
        query = queries[rows_of(row), :]
        spread = jnp.concatenate(
            [jnp.where(kv_of_row == kv, query, 0.0) for kv in range(kv_count)], axis=1
        ).astype(jnp.bfloat16)
        scores = lax.dot_general(
            with_new(key_ref, window, new_keys, row),
            spread,
            (((1,), (1,)), ((), ())),
            preferred_element_type=jnp.float32,
        )
        inside = ((place >= first) & (place < last)) | (place == WINDOW)
        return jnp.where(inside, scores * scale, -1e30)

    def weighed(scores):
        raised = jnp.exp2(scores - jnp.max(scores, axis=0, keepdims=True))
        weights = raised * (1.0 / jnp.sum(raised, axis=0, keepdims=True))
        return weights.astype(jnp.bfloat16)

    def mix(row, weights):
        mixed = lax.dot_general(
            weights,
            with_new(value_ref, window_of(row)[2], new_values, row),
            (((0,), (0,)), ((), ())),
            preferred_element_type=jnp.float32,
        )
        results[rows_of(row), :] = jnp.concatenate(
            [
                mixed[kv * group : (kv + 1) * group, kv * HD : (kv + 1) * HD]
                for kv in range(kv_count)
            ],
            axis=0,
        )

    def body(step, carry):
        at = [step * UNROLL + inner for inner in range(UNROLL)]
        weights = [weighed(scores) for scores in [scored(row) for row in at]]
        for row, weight in zip(at, weights):
            mix(row, weight)
        return carry

    lax.fori_loop(0, rows // UNROLL, body, 0)
    out_heads = out_ref.shape[2] // HD
    for index in range(heads):
        block, slot = index // out_heads, index % out_heads
        out_ref[block, :, slot * HD : (slot + 1) * HD] = results[
            pl.ds(index, rows, stride=heads), :
        ].astype(jnp.bfloat16)


def attend(merged, lengths, query_gain, key_gain, keys, values, count, swapped):
    rows = merged.shape[1]
    kv_count = keys.shape[1] // HD
    heads = merged.shape[0] * merged.shape[2] // HD - 2 * kv_count
    position = lengths.reshape(rows)
    frequency = ROPE_BASE ** (-jnp.arange(HD // 2, dtype=jnp.float32) * 2.0 / HD)
    angles = position.astype(jnp.float32)[:, None] * frequency[None, :]
    cosine, sine = jnp.cos(angles), jnp.sin(angles)
    return call(
        functools.partial(attention_kernel, kv_count),
        jax.ShapeDtypeStruct((count, rows, heads * HD // count), jnp.bfloat16),
        [SMEM] + [VMEM] * 7 + [HBM] * len(swapped),
        (
            lengths,
            merged,
            jnp.concatenate([cosine, cosine], axis=1),
            jnp.concatenate([-sine, sine], axis=1),
            query_gain[None, :],
            key_gain[None, :],
            keys,
            values,
            *swapped,
        ),
        [
            pltpu.VMEM((heads * rows, HD), jnp.float32),
            pltpu.VMEM((heads * rows, HD), jnp.float32),
            pltpu.VMEM((rows, kv_count * HD), jnp.float32),
            pltpu.VMEM((rows, kv_count * HD), jnp.float32),
            pltpu.SMEM((rows + 1,), jnp.int32),
        ],
        12,
        "ragged_attention",
    )


def on_device(
    hidden,
    lengths,
    key_cache,
    value_cache,
    expert_ids,
    gate_codes,
    expert_device,
    attention_gain,
    mixture_gain,
    query_gain,
    key_gain,
    project_weight,
    output_weight,
    expert_gate_up,
    expert_down,
):
    count, subs = lax.axis_size("dev"), lax.axis_size("sub")
    ring = Ring(count)
    rows, width = hidden.shape
    slots = expert_device.shape[0]

    gate_ups, downs = [], []
    for shift in range(1, subs):
        swap = [(i, (i - shift) % subs) for i in range(subs)]
        gate_ups.append(lax.ppermute(expert_gate_up[0], "sub", swap))
        downs.append(lax.ppermute(expert_down[0], "sub", swap))

    bf16 = jnp.bfloat16
    owners = ring.owners()
    dma = pltpu.SemaphoreType.DMA
    digits = call(
        digit_kernel,
        jax.ShapeDtypeStruct((rows, HD), bf16),
        [SMEM, VMEM, VMEM],
        (expert_device[None, :], expert_ids, gate_codes),
        [],
        4,
        "gate_digits",
    )
    normed = call(
        norm_kernel,
        jax.ShapeDtypeStruct((rows, width), bf16),
        [ANY] * 2,
        (hidden, attention_gain[None, :]),
        [pltpu.VMEM((rows, width), bf16), pltpu.VMEM((1, width), jnp.float32), dma((2,))],
        4,
        "attention_norm",
    )
    columns = project_weight.shape[1]
    gathered, pieces = ring_gather(ring, normed)
    (project_weight,) = loaded([project_weight], pieces[1], 50, "load_project")
    blocks = call(
        functools.partial(project_kernel, count),
        jax.ShapeDtypeStruct((count, rows, columns), bf16),
        [SMEM, VMEM, VMEM],
        (owners, gathered, project_weight),
        [],
        8,
        "project",
    )
    keys, values = loaded([key_cache[0], value_cache[0]], blocks, 44, "load_caches")
    blocks = lax.all_to_all(blocks, "dev", split_axis=0, concat_axis=0, tiled=True)
    if columns % HD:
        blocks = jnp.transpose(blocks, (1, 0, 2)).reshape(1, rows, -1)
    attention = attend(
        blocks, lengths, query_gain, key_gain, keys, values, count, [digits, *gate_ups, *downs]
    )
    features = lax.all_to_all(attention, "dev", split_axis=0, concat_axis=0, tiled=True)
    (output_weight,) = loaded([output_weight], attention, 44, "load_output")
    own, *partial = call(
        functools.partial(output_kernel, count),
        block_shapes(count, rows, width),
        [SMEM, VMEM, VMEM],
        (owners, features, output_weight),
        [pltpu.VMEM((count * rows, output_weight.shape[0]), bf16)],
        8,
        "output_projection",
    )
    up, down = ring_scatter_sum(ring, *partial)
    residual, sent = call(
        residual_kernel,
        [
            jax.ShapeDtypeStruct((rows, width), jnp.float32),
            jax.ShapeDtypeStruct((rows, width + HD), bf16),
        ],
        [VMEM] * 6,
        (hidden, own, up, down, mixture_gain[None, :], digits),
        [],
        4,
        "residual_norm",
    )
    shifts = jnp.arange(subs, dtype=jnp.int32)[None, :]
    own_slots = lax.axis_index("dev") * subs + (lax.axis_index("sub") + shifts) % subs
    gathered, pieces = ring_gather(ring, sent)
    (own_gate_up,) = loaded([expert_gate_up[0]], pieces[1], 42, "load_gate_up")
    (own_down,) = loaded([expert_down[0]], pieces[3], 42, "load_down")
    own, *partial = call(
        functools.partial(expert_kernel, count, slots),
        block_shapes(count, rows, width),
        [SMEM] + [VMEM] * (1 + 2 * subs),
        (own_slots, gathered, own_gate_up, *gate_ups, own_down, *downs),
        [
            pltpu.VMEM((count * rows, expert_down.shape[1]), bf16),
            pltpu.VMEM((count * rows, width), jnp.float32),
        ],
        18,
        "experts",
    )
    up, down = ring_scatter_sum(ring, *partial)
    return (residual + own + up + down).astype(bf16)


def solution(mesh):
    return jax.shard_map(
        on_device,
        mesh=mesh,
        in_specs=(
            P(("groups", "dev", "sub"), None),
            P(("groups", "dev", "sub"), None),
            P(("groups", "dev", "sub"), None, None),
            P(("groups", "dev", "sub"), None, None),
            P(("groups", "dev", "sub"), None),
            P(("groups", "dev", "sub"), None),
            P(),
            P(),
            P(),
            P(),
            P(),
            P(None, "dev"),
            P("dev", None),
            P(("dev", "sub"), None, None),
            P(("dev", "sub"), None, None),
        ),
        out_specs=P(("groups", "dev", "sub"), None),
        check_vma=False,
    )
```

time: 255 us -> 150 us (0.59)
  waiting for transfers between devices: 121 us -> 50.1 us
  blocking collectives: 40.3 us -> 0 us
  starting transfers between devices: 9.16 us -> 46.3 us
  matrix products: 35.6 us -> 0 us
  Pallas kernels: 0 us -> 32 us
  between operations: 13.8 us -> 0.53 us
  other arithmetic: 13.7 us -> 2.62 us
    reduce_scatter x1 -> x0, waiting for transfers between devices: 61.1 us -> none  [on_device(): lax.psum_scatter(jnp.dot(features, output_weight, preferred_element_type=...]
    ppermute x0 -> x34, waiting for transfers between devices: none -> 44.9 us  [the longest x16 40.9 us: ahead(): return lax.ppermute(values, 'dev', self.forward)]
    all_to_all x2 -> x0, blocking collectives: 40.3 us -> none  [the longest x1 28.4 us: on_device(): lax.all_to_all(outgoing, ('dev', 'sub'), split_axis=0, concat_axis=0, til...]
    dot_general x9 -> x0, matrix products: 35.6 us -> none  [the longest x1 11.2 us: attend(): jnp.einsum('krgp,pkd->rkgd', weights, valued, preferred_element_type=jnp....]
    ppermute x0 -> x34, starting transfers between devices: none -> 35.3 us  [the longest x16 20.9 us: behind(): return lax.ppermute(values, 'dev', self.backward)]
    pallas_call x0 -> x12, Pallas kernels: none -> 32 us  [call(): pl.pallas_call(body, out_shape=outs, in_specs=whole_blocks(ins), out_spec...]
    all_gather x1 -> x0, waiting for transfers between devices: 28 us -> none  [on_device(): lax.all_gather(normed, 'dev', axis=0, tiled=True)]
    all_to_all x2, waiting for transfers between devices: 32 us -> 5.2 us  [the longest x1 5.2 us: on_device(): lax.all_to_all(attention, 'dev', split_axis=0, concat_axis=0, tiled=True)]
  transfers between devices with their start and end apart: 4 -> 36, of which waited for: 4 -> 20; matrix products, arithmetic and copies ran while one was open for 7% -> 3% of each run, Pallas kernels for 0% -> 8%
where the time goes in v1:
time: 150 us; the launch traced here: 149 us
  waiting for transfers between devices  50.1 us (33%)
  starting transfers between devices  46.3 us (31%)
  Pallas kernels  32 us (21%)
  local copies, waits for them, and re-layouts  17.5 us (12%)
  other arithmetic  2.62 us (2%)
    ppermute x16, waiting for transfers between devices, ahead(): return lax.ppermute(values, 'dev', self.forward)  40.9 us
    pallas_call x12, Pallas kernels, call(): pl.pallas_call(body, out_shape=outs, in_specs=whole_blocks(ins), out_spec...  32 us
    ppermute x16, starting transfers between devices, behind(): return lax.ppermute(values, 'dev', self.backward)  20.9 us
    unnamed x60, local copies, waits for them, and re-layouts  17.3 us
    ppermute x16, starting transfers between devices, ahead(): return lax.ppermute(values, 'dev', self.forward)  14 us
    all_to_all x1, starting transfers between devices, on_device(): lax.all_to_all(attention, 'dev', split_axis=0, concat_axis=0, tiled=True)  6 us
    all_to_all x1, waiting for transfers between devices, on_device(): lax.all_to_all(attention, 'dev', split_axis=0, concat_axis=0, tiled=True)  5.2 us
    all_to_all x1, starting transfers between devices, on_device(): lax.all_to_all(blocks, 'dev', split_axis=0, concat_axis=0, tiled=True)  5.01 us
  transfers between devices with their start and end apart: 36, of which 20 were waited for; matrix products, arithmetic and copies ran while one was open for 3% of the time, Pallas kernels for 8%

profile of v1, /device:TPU:0, one launch (start us, length us, event | category | flops | bytes accessed | tf_op | source)
XLA Modules:
  0.0 149.1 jit_solution(1863289905536878449)
XLA Ops:
  0.5 0.9 copy-done.9
  1.4 0.7 copy-done.14
  2.4 3.1 %collective-permute-start.1 = (bf16[32,2048]{1,0:T(8,128)(2,1)S(1)}, bf16[32,2048]{1,0:T(8,128)(2,1)}, u32[]{:S(2)}, u32[]{:S(2)}) collective-permute-start(bf16[32,2048]{1,0:T(8,128)(2,1)S(1)} %attention_norm.1), channel_id=1, source_target_pairs={{0,4},{4,8},{8,12},{12,14},{14,10},{10,6},{6,2},{2,0},{1,5},{5,9},... | collective-permute-start | bytes 393224 | tf_op jit(solution)/shard_map/ppermute | solution.py:45
  5.5 0.7 constant_dynamic-update-slice_fusion.8
  6.2 3.0 %collective-permute-done.1 = bf16[32,2048]{1,0:T(8,128)(2,1)} collective-permute-done((bf16[32,2048]{1,0:T(8,128)(2,1)S(1)}, bf16[32,2048]{1,0:T(8,128)(2,1)}, u32[]{:S(2)}, u32[]{:S(2)}) %collective-permute-start.1) | collective-permute-done | bytes 131104 | tf_op jit(solution)/shard_map/ppermute | solution.py:45
  9.2 1.8 %collective-permute-start.3 = (bf16[32,2048]{1,0:T(8,128)(2,1)}, bf16[32,2048]{1,0:T(8,128)(2,1)S(1)}, u32[]{:S(2)}, u32[]{:S(2)}) collective-permute-start(bf16[32,2048]{1,0:T(8,128)(2,1)} %collective-permute-done.1), channel_id=1, source_target_pairs={{0,4},{4,8},{8,12},{12,14},{14,10},{10,6},{6,2},{2,0},{1,5},{5,9},... | collective-permute-start | bytes 393224 | tf_op jit(solution)/shard_map/ppermute | solution.py:45
  11.2 1.7 %load_project.1.weight_ref = bf16[2048,640]{1,0:T(8,128)(2,1)S(1)} custom-call(bf16[2048,640]{1,0:T(8,128)(2,1)} %refs_0_.2, bf16[32,2048]{1,0:T(8,128)(2,1)S(1)} %collective-permute-done.refs_1_), custom_call_target="tpu_custom_call" | custom-call | bytes 104857600 | tf_op jit(solution)/shard_map/load_project/pallas_call | solution.py:97
  13.0 0.9 constant_dynamic-update-slice_fusion.6
  14.4 1.8 %collective-permute-start.5 = (bf16[32,2048]{1,0:T(8,128)(2,1)S(1)}, bf16[32,2048]{1,0:T(8,128)(2,1)S(1)}, u32[]{:S(2)}, u32[]{:S(2)}) collective-permute-start(bf16[32,2048]{1,0:T(8,128)(2,1)S(1)} %collective-permute-done.3), channel_id=1, source_target_pairs={{0,4},{4,8},{8,12},{12,14},{14,10},{10,6},{6,2},{2,0},{1,5},{5,9},... | collective-permute-start | bytes 393224 | tf_op jit(solution)/shard_map/ppermute | solution.py:45
  16.4 2.9 %collective-permute-done.5 = bf16[32,2048]{1,0:T(8,128)(2,1)S(1)} collective-permute-done((bf16[32,2048]{1,0:T(8,128)(2,1)S(1)}, bf16[32,2048]{1,0:T(8,128)(2,1)S(1)}, u32[]{:S(2)}, u32[]{:S(2)}) %collective-permute-start.5) | collective-permute-done | bytes 131104 | tf_op jit(solution)/shard_map/ppermute | solution.py:45
  19.4 2.1 %collective-permute-start.6 = (bf16[16,2048]{1,0:T(8,128)(2,1)S(1)}, bf16[16,2048]{1,0:T(8,128)(2,1)S(1)}, u32[]{:S(2)}, u32[]{:S(2)}) collective-permute-start(bf16[16,2048]{1,0:T(8,128)(2,1)S(1)} %slice.100), channel_id=1, source_target_pairs={{0,4},{4,8},{8,12},{12,14},{14,10},{10,6},{6,2},{2,0},{1,5},{5,9},... | collective-permute-start | bytes 196616 | tf_op jit(solution)/shard_map/ppermute | solution.py:45
  21.6 2.0 %collective-permute-done.6 = bf16[16,2048]{1,0:T(8,128)(2,1)S(1)} collective-permute-done((bf16[16,2048]{1,0:T(8,128)(2,1)S(1)}, bf16[16,2048]{1,0:T(8,128)(2,1)S(1)}, u32[]{:S(2)}, u32[]{:S(2)}) %collective-permute-start.6) | collective-permute-done | bytes 65568 | tf_op jit(solution)/shard_map/ppermute | solution.py:45
  23.7 2.1 %collective-permute-done.7 = bf16[16,2048]{1,0:T(8,128)(2,1)S(1)} collective-permute-done((bf16[16,2048]{1,0:T(8,128)(2,1)S(1)}, bf16[16,2048]{1,0:T(8,128)(2,1)S(1)}, u32[]{:S(2)}, u32[]{:S(2)}) %collective-permute-start.7) | collective-permute-done | bytes 65568 | tf_op jit(solution)/shard_map/ppermute | solution.py:48
  25.9 2.3 %project.1.refs_2_ = bf16[8,32,640]{2,1,0:T(8,128)(2,1)} custom-call(s32[1,8]{1,0:T(1,128)S(1)} %compare_select_fusion.4.owner_ref, bf16[256,2048]{1,0:T(8,128)(2,1)S(1)} %constant_dynamic-update-slice_fusion.normed_ref, bf16[2048,640]{1,0:T(8,128)(2,1)S(1)} %load_project.1.weight_ref), custom_call_target="tpu_custom_call" | custom-call | bytes 104857600 | tf_op jit(solution)/shard_map/project/pallas_call | solution.py:97
  28.1 5.0 %all-to-all-start = ((bf16[8,32,640]{2,1,0:T(8,128)(2,1)}), bf16[8,32,640]{2,1,0:T(8,128)(2,1)S(1)}, u32[]{:S(2)}, u32[]{:S(2)}) async-start(bf16[8,32,640]{2,1,0:T(8,128)(2,1)} %project.1.refs_2_), calls=%async_computation | async-start | bytes 655360 | tf_op jit(solution)/shard_map/all_to_all | solution.py:455
  33.3 0.8 gate_digits.1.refs_0_.digit_ref
  34.3 3.5 %load_caches.1 = (bf16[4096,512]{1,0:T(8,128)(2,1)S(1)}, bf16[4096,512]{1,0:T(8,128)(2,1)S(1)}) custom-call(bf16[4096,512]{1,0:T(8,128)(2,1)} %bitcast.60, bf16[4096,512]{1,0:T(8,128)(2,1)} %bitcast.61, bf16[8,32,640]{2,1,0:T(8,128)(2,1)} %project.1.refs_2_), custom_call_target="tpu_custom_call" | custom-call | bytes 104857600 | tf_op jit(solution)/shard_map/load_caches/pallas_call | solution.py:97
  37.9 2.1 %copy-done.2 = bf16[4096,512]{1,0:T(8,128)(2,1)} copy-done((bf16[4096,512]{1,0:T(8,128)(2,1)}, bf16[4096,512]{1,0:T(8,128)(2,1)S(1)}, u32[]{:S(2)}) %copy-start.2) | copy-done | bytes 4194328
  39.9 2.0 %copy-done.4 = bf16[4096,512]{1,0:T(8,128)(2,1)} copy-done((bf16[4096,512]{1,0:T(8,128)(2,1)}, bf16[4096,512]{1,0:T(8,128)(2,1)S(1)}, u32[]{:S(2)}) %copy-start.4) | copy-done | bytes 4194328
  42.0 2.2 %copy-done.3 = bf16[4096,512]{1,0:T(8,128)(2,1)S(1)} copy-done((bf16[4096,512]{1,0:T(8,128)(2,1)S(1)}, bf16[4096,512]{1,0:T(8,128)(2,1)}, u32[]{:S(2)}) %copy-start.3) | copy-done | bytes 4194328
  44.2 2.2 %copy-done.5 = bf16[4096,512]{1,0:T(8,128)(2,1)S(1)} copy-done((bf16[4096,512]{1,0:T(8,128)(2,1)S(1)}, bf16[4096,512]{1,0:T(8,128)(2,1)}, u32[]{:S(2)}) %copy-start.5) | copy-done | bytes 4194328
  46.4 9.8 %ragged_attention.1.refs_1_ = bf16[8,32,512]{2,1,0:T(8,128)(2,1)} custom-call(s32[1,32]{1,0:T(1,128)S(1)} %copy-done.15, bf16[8,32,640]{2,1,0:T(8,128)(2,1)S(1)} %all-to-all-done.merged_ref, f32[32,128]{1,0:T(8,128)S(1)} %get-tuple-element.36.cos_ref, f32[32,128]{1,0:T(8,128)S(1)} %get-tuple-element.37.sin_ref, f32[1,128]{1,0:T(1,128)S(1)} %bitcast.55, ...), custom_call_target="tpu_custom_call" | custom-call | bytes 104857600 | tf_op jit(solution)/shard_map/ragged_attention/pallas_call | solution.py:97
  56.2 6.0 %all-to-all-start.1 = ((bf16[8,32,512]{2,1,0:T(8,128)(2,1)}), bf16[8,32,512]{2,1,0:T(8,128)(2,1)S(1)}, u32[]{:S(2)}, u32[]{:S(2)}) async-start(bf16[8,32,512]{2,1,0:T(8,128)(2,1)} %ragged_attention.1.refs_1_), calls=%async_computation.1 | async-start | bytes 524288 | tf_op jit(solution)/shard_map/all_to_all | solution.py:461
  62.2 1.6 %copy-done.7 = bf16[512,2048]{1,0:T(8,128)(2,1)S(1)} copy-done((bf16[512,2048]{1,0:T(8,128)(2,1)S(1)}, bf16[512,2048]{1,0:T(8,128)(2,1)}, u32[]{:S(2)}) %copy-start.7) | copy-done | bytes 2097176
  64.0 1.4 copy-done
  65.4 5.2 %all-to-all-done.1.feature_ref = bf16[8,32,512]{2,1,0:T(8,128)(2,1)S(1)} async-done(((bf16[8,32,512]{2,1,0:T(8,128)(2,1)}), bf16[8,32,512]{2,1,0:T(8,128)(2,1)S(1)}, u32[]{:S(2)}, u32[]{:S(2)}) %all-to-all-start.1) | async-done | bytes 262176 | tf_op jit(solution)/shard_map/all_to_all | solution.py:461
  70.6 1.6 %copy-done.1 = bf16[512,2048]{1,0:T(8,128)(2,1)S(1)} copy-done((bf16[512,2048]{1,0:T(8,128)(2,1)S(1)}, bf16[512,2048]{1,0:T(8,128)(2,1)}, u32[]{:S(2)}) %copy-start.1) | copy-done | bytes 2097176
  72.1 1.3 output_projection.1
  73.4 0.7 copy-done.11
  74.1 2.0 %collective-permute-start.14 = (bf16[32,1024]{1,0:T(8,128)(2,1)S(1)}, bf16[32,1024]{1,0:T(8,128)(2,1)S(1)}, u32[]{:S(2)}, u32[]{:S(2)}) collective-permute-start(bf16[32,1024]{1,0:T(8,128)(2,1)S(1)} %get-tuple-element.25), channel_id=1, source_target_pairs={{4,0},{8,4},{12,8},{14,12},{10,14},{6,10},{2,6},{0,2},{5,1},{9,5},... | collective-permute-start | bytes 196616 | tf_op jit(solution)/shard_map/ppermute | solution.py:48
  76.2 2.9 %collective-permute-done.10 = bf16[32,1024]{1,0:T(8,128)(2,1)S(1)} collective-permute-done((bf16[32,1024]{1,0:T(8,128)(2,1)S(1)}, bf16[32,1024]{1,0:T(8,128)(2,1)S(1)}, u32[]{:S(2)}, u32[]{:S(2)}) %collective-permute-start.10) | collective-permute-done | bytes 65568 | tf_op jit(solution)/shard_map/ppermute | solution.py:45
  79.3 2.1 %collective-permute-start.15 = (bf16[32,2048]{1,0:T(8,128)(2,1)S(1)}, bf16[32,2048]{1,0:T(8,128)(2,1)S(1)}, u32[]{:S(2)}, u32[]{:S(2)}) collective-permute-start(bf16[32,2048]{1,0:T(8,128)(2,1)S(1)} %pad_maximum_fusion.1), channel_id=1, source_target_pairs={{4,0},{8,4},{12,8},{14,12},{10,14},{6,10},{2,6},{0,2},{5,1},{9,5},... | collective-permute-start | bytes 393224 | tf_op jit(solution)/shard_map/ppermute | solution.py:48
  81.3 3.9 %collective-permute-done.11 = bf16[32,2048]{1,0:T(8,128)(2,1)S(1)} collective-permute-done((bf16[32,2048]{1,0:T(8,128)(2,1)S(1)}, bf16[32,2048]{1,0:T(8,128)(2,1)S(1)}, u32[]{:S(2)}, u32[]{:S(2)}) %collective-permute-start.11) | collective-permute-done | bytes 131104 | tf_op jit(solution)/shard_map/ppermute | solution.py:45
  85.4 2.1 %collective-permute-start.16 = (bf16[32,2048]{1,0:T(8,128)(2,1)S(1)}, bf16[32,2048]{1,0:T(8,128)(2,1)S(1)}, u32[]{:S(2)}, u32[]{:S(2)}) collective-permute-start(bf16[32,2048]{1,0:T(8,128)(2,1)S(1)} %fusion.4), channel_id=1, source_target_pairs={{4,0},{8,4},{12,8},{14,12},{10,14},{6,10},{2,6},{0,2},{5,1},{9,5},... | collective-permute-start | bytes 393224 | tf_op jit(solution)/shard_map/ppermute | solution.py:48
  87.4 3.5 %collective-permute-done.12 = bf16[32,2048]{1,0:T(8,128)(2,1)S(1)} collective-permute-done((bf16[32,2048]{1,0:T(8,128)(2,1)S(1)}, bf16[32,2048]{1,0:T(8,128)(2,1)S(1)}, u32[]{:S(2)}, u32[]{:S(2)}) %collective-permute-start.12) | collective-permute-done | bytes 131104 | tf_op jit(solution)/shard_map/ppermute | solution.py:45
  90.9 0.7 fusion.7
  91.6 0.7 fusion.5
  92.2 2.0 %collective-permute-start.17 = (bf16[32,2048]{1,0:T(8,128)(2,1)}, bf16[32,2048]{1,0:T(8,128)(2,1)}, u32[]{:S(2)}, u32[]{:S(2)}) collective-permute-start(bf16[32,2048]{1,0:T(8,128)(2,1)} %fusion.5), channel_id=1, source_target_pairs={{4,0},{8,4},{12,8},{14,12},{10,14},{6,10},{2,6},{0,2},{5,1},{9,5},... | collective-permute-start | bytes 393224 | tf_op jit(solution)/shard_map/ppermute | solution.py:48
  94.3 2.9 %collective-permute-done.13.up_ref = bf16[32,2048]{1,0:T(8,128)(2,1)} collective-permute-done((bf16[32,2048]{1,0:T(8,128)(2,1)}, bf16[32,2048]{1,0:T(8,128)(2,1)}, u32[]{:S(2)}, u32[]{:S(2)}) %collective-permute-start.13) | collective-permute-done | bytes 131104 | tf_op jit(solution)/shard_map/ppermute | solution.py:45
  97.5 1.1 residual_norm.1
  98.7 0.7 collective-permute-start.19
  99.4 1.5 collective-permute-start.18
  100.8 3.4 %collective-permute-done.19 = bf16[32,2176]{1,0:T(8,128)(2,1)S(1)} collective-permute-done((bf16[32,2176]{1,0:T(8,128)(2,1)S(1)}, bf16[32,2176]{1,0:T(8,128)(2,1)S(1)}, u32[]{:S(2)}, u32[]{:S(2)}) %collective-permute-start.19) | collective-permute-done | bytes 139296 | tf_op jit(solution)/shard_map/ppermute | solution.py:45
  104.2 1.0 collective-permute-start.21
  105.2 1.4 collective-permute-start.20
  106.7 2.9 %load_gate_up.1.refs_0_ = bf16[2048,1536]{1,0:T(8,128)(2,1)S(1)} custom-call(bf16[2048,1536]{1,0:T(8,128)(2,1)} %bitcast.59, bf16[32,2176]{1,0:T(8,128)(2,1)S(1)} %collective-permute-done.18.refs_1_), custom_call_target="tpu_custom_call" | custom-call | bytes 104857600 | tf_op jit(solution)/shard_map/load_gate_up/pallas_call | solution.py:97
  109.6 0.7 collective-permute-start.23
  110.3 1.5 collective-permute-start.22
  112.0 2.7 %collective-permute-done.23 = bf16[32,2176]{1,0:T(8,128)(2,1)S(1)} collective-permute-done((bf16[32,2176]{1,0:T(8,128)(2,1)S(1)}, bf16[32,2176]{1,0:T(8,128)(2,1)S(1)}, u32[]{:S(2)}, u32[]{:S(2)}) %collective-permute-start.23) | collective-permute-done | bytes 139296 | tf_op jit(solution)/shard_map/ppermute | solution.py:45
  114.7 0.6 collective-permute-start.24
  115.3 1.5 collective-permute-start.25
  116.9 2.5 %collective-permute-done.24 = bf16[16,2176]{1,0:T(8,128)(2,1)S(1)} collective-permute-done((bf16[16,2176]{1,0:T(8,128)(2,1)S(1)}, bf16[16,2176]{1,0:T(8,128)(2,1)S(1)}, u32[]{:S(2)}, u32[]{:S(2)}) %collective-permute-start.24) | collective-permute-done | bytes 69664 | tf_op jit(solution)/shard_map/ppermute | solution.py:45
  119.4 1.0 collective-permute-done.25
  120.4 7.9 %experts.1 = (f32[32,2048]{1,0:T(8,128)S(1)}, bf16[32,1024]{1,0:T(8,128)(2,1)S(1)}, bf16[32,1024]{1,0:T(8,128)(2,1)S(1)}, f32[3,32,2048]{2,1,0:T(8,128)S(1)}, f32[3,32,2048]{2,1,0:T(8,128)S(1)}) custom-call(s32[1,2]{1,0:T(1,128)S(1)} %fusion.15.slot_ref, bf16[256,2176]{1,0:T(8,128)(2,1)S(1)} %constant_dynamic-update-slice_fusion.9.held, ...), custom_call_target="tpu_custom_call" | custom-call | bytes 104857600 | tf_op jit(solution)/shard_map/experts/pallas_call | solution.py:97
  128.9 1.5 %collective-permute-start.30 = (bf16[32,1024]{1,0:T(8,128)(2,1)S(1)}, bf16[32,1024]{1,0:T(8,128)(2,1)S(1)}, u32[]{:S(2)}, u32[]{:S(2)}) collective-permute-start(bf16[32,1024]{1,0:T(8,128)(2,1)S(1)} %get-tuple-element.32), channel_id=1, source_target_pairs={{4,0},{8,4},{12,8},{14,12},{10,14},{6,10},{2,6},{0,2},{5,1},{9,5},... | collective-permute-start | bytes 196616 | tf_op jit(solution)/shard_map/ppermute | solution.py:48
  130.5 2.2 %collective-permute-done.26 = bf16[32,1024]{1,0:T(8,128)(2,1)S(1)} collective-permute-done((bf16[32,1024]{1,0:T(8,128)(2,1)S(1)}, bf16[32,1024]{1,0:T(8,128)(2,1)S(1)}, u32[]{:S(2)}, u32[]{:S(2)}) %collective-permute-start.26) | collective-permute-done | bytes 65568 | tf_op jit(solution)/shard_map/ppermute | solution.py:45
  133.3 1.6 %collective-permute-start.31 = (bf16[32,2048]{1,0:T(8,128)(2,1)S(1)}, bf16[32,2048]{1,0:T(8,128)(2,1)S(1)}, u32[]{:S(2)}, u32[]{:S(2)}) collective-permute-start(bf16[32,2048]{1,0:T(8,128)(2,1)S(1)} %pad_maximum_fusion.3), channel_id=1, source_target_pairs={{4,0},{8,4},{12,8},{14,12},{10,14},{6,10},{2,6},{0,2},{5,1},{9,5},... | collective-permute-start | bytes 393224 | tf_op jit(solution)/shard_map/ppermute | solution.py:48
  134.8 2.8 %collective-permute-done.27 = bf16[32,2048]{1,0:T(8,128)(2,1)S(1)} collective-permute-done((bf16[32,2048]{1,0:T(8,128)(2,1)S(1)}, bf16[32,2048]{1,0:T(8,128)(2,1)S(1)}, u32[]{:S(2)}, u32[]{:S(2)}) %collective-permute-start.27) | collective-permute-done | bytes 131104 | tf_op jit(solution)/shard_map/ppermute | solution.py:45
  138.3 1.6 %collective-permute-start.32 = (bf16[32,2048]{1,0:T(8,128)(2,1)S(1)}, bf16[32,2048]{1,0:T(8,128)(2,1)S(1)}, u32[]{:S(2)}, u32[]{:S(2)}) collective-permute-start(bf16[32,2048]{1,0:T(8,128)(2,1)S(1)} %fusion), channel_id=1, source_target_pairs={{4,0},{8,4},{12,8},{14,12},{10,14},{6,10},{2,6},{0,2},{5,1},{9,5},... | collective-permute-start | bytes 393224 | tf_op jit(solution)/shard_map/ppermute | solution.py:48
  139.9 2.9 %collective-permute-done.28 = bf16[32,2048]{1,0:T(8,128)(2,1)S(1)} collective-permute-done((bf16[32,2048]{1,0:T(8,128)(2,1)S(1)}, bf16[32,2048]{1,0:T(8,128)(2,1)S(1)}, u32[]{:S(2)}, u32[]{:S(2)}) %collective-permute-start.28) | collective-permute-done | bytes 131104 | tf_op jit(solution)/shard_map/ppermute | solution.py:45
  143.4 1.6 %collective-permute-start.33 = (bf16[32,2048]{1,0:T(8,128)(2,1)S(1)}, bf16[32,2048]{1,0:T(8,128)(2,1)S(1)}, u32[]{:S(2)}, u32[]{:S(2)}) collective-permute-start(bf16[32,2048]{1,0:T(8,128)(2,1)S(1)} %fusion.1), channel_id=1, source_target_pairs={{4,0},{8,4},{12,8},{14,12},{10,14},{6,10},{2,6},{0,2},{5,1},{9,5},... | collective-permute-start | bytes 393224 | tf_op jit(solution)/shard_map/ppermute | solution.py:48
  145.0 2.9 %collective-permute-done.29 = bf16[32,2048]{1,0:T(8,128)(2,1)S(1)} collective-permute-done((bf16[32,2048]{1,0:T(8,128)(2,1)S(1)}, bf16[32,2048]{1,0:T(8,128)(2,1)S(1)}, u32[]{:S(2)}, u32[]{:S(2)}) %collective-permute-start.29) | collective-permute-done | bytes 131104 | tf_op jit(solution)/shard_map/ppermute | solution.py:45
  147.8 0.6 collective-permute-done.33
  148.4 0.7 add_convert_fusion
  (117 shorter events, 6.0 us)
Async XLA Ops:
  0.0 42.0 %collective-permute-start.8 = (bf16[2048,1536]{1,0:T(8,128)(2,1)}, bf16[2048,1536]{1,0:T(8,128)(2,1)}, u32[]{:S(2)}, u32[]{:S(2)}) collective-permute-start(bf16[2048,1536]{1,0:T(8,128)(2,1)} %bitcast.58), channel_id=1, source_target_pairs={{0,1},{1,0},{2,3},{3,2},{4,5},{5,4},{6,7},{7,6},{8,9},{9,8},{10,11... | collective-permute-start | bytes 18874376 | tf_op jit(solution)/shard_map/ppermute | solution.py:418
  0.5 41.5 %collective-permute-start.9 = (bf16[768,2048]{1,0:T(8,128)(2,1)}, bf16[768,2048]{1,0:T(8,128)(2,1)S(1)}, u32[]{:S(2)}, u32[]{:S(2)}) collective-permute-start(bf16[768,2048]{1,0:T(8,128)(2,1)} %bitcast.51), channel_id=1, source_target_pairs={{0,1},{1,0},{2,3},{3,2},{4,5},{5,4},{6,7},{7,6},{8,9},{9,8},{10,11... | collective-permute-start | bytes 9437192 | tf_op jit(solution)/shard_map/ppermute | solution.py:419
  0.5 0.9 copy-start.9
  1.4 0.7 copy-start.14
  2.4 6.8 %collective-permute-start.1 = (bf16[32,2048]{1,0:T(8,128)(2,1)S(1)}, bf16[32,2048]{1,0:T(8,128)(2,1)}, u32[]{:S(2)}, u32[]{:S(2)}) collective-permute-start(bf16[32,2048]{1,0:T(8,128)(2,1)S(1)} %attention_norm.1), channel_id=1, source_target_pairs={{0,4},{4,8},{8,12},{12,14},{14,10},{10,6},{6,2},{2,0},{1,5},{5,9},... | collective-permute-start | bytes 393224 | tf_op jit(solution)/shard_map/ppermute | solution.py:45
  5.5 5.5 %collective-permute-start = (bf16[32,2048]{1,0:T(8,128)(2,1)S(1)}, bf16[32,2048]{1,0:T(8,128)(2,1)S(1)}, u32[]{:S(2)}, u32[]{:S(2)}) collective-permute-start(bf16[32,2048]{1,0:T(8,128)(2,1)S(1)} %attention_norm.1), channel_id=1, source_target_pairs={{4,0},{8,4},{12,8},{14,12},{10,14},{6,10},{2,6},{0,2},{5,1},{9,5},... | collective-permute-start | bytes 393224 | tf_op jit(solution)/shard_map/ppermute | solution.py:48
  6.2 6.8 %copy-start.8 = (bf16[256,2048]{1,0:T(8,128)(2,1)S(1)}, bf16[256,2048]{1,0:T(8,128)(2,1)}, u32[]{:S(2)}) copy-start(bf16[256,2048]{1,0:T(8,128)(2,1)} %constant_dynamic-update-slice_fusion.8) | copy-start | bytes 3145732
  9.2 5.2 %collective-permute-start.3 = (bf16[32,2048]{1,0:T(8,128)(2,1)}, bf16[32,2048]{1,0:T(8,128)(2,1)S(1)}, u32[]{:S(2)}, u32[]{:S(2)}) collective-permute-start(bf16[32,2048]{1,0:T(8,128)(2,1)} %collective-permute-done.1), channel_id=1, source_target_pairs={{0,4},{4,8},{8,12},{12,14},{14,10},{10,6},{6,2},{2,0},{1,5},{5,9},... | collective-permute-start | bytes 393224 | tf_op jit(solution)/shard_map/ppermute | solution.py:45
  11.0 5.2 %collective-permute-start.2 = (bf16[32,2048]{1,0:T(8,128)(2,1)S(1)}, bf16[32,2048]{1,0:T(8,128)(2,1)S(1)}, u32[]{:S(2)}, u32[]{:S(2)}) collective-permute-start(bf16[32,2048]{1,0:T(8,128)(2,1)S(1)} %collective-permute-done.refs_1_), channel_id=1, source_target_pairs={{4,0},{8,4},{12,8},{14,12},{10,14},{6,10},{2,6},{0,2},{5,1},{9,5},... | collective-permute-start | bytes 393224 | tf_op jit(solution)/shard_map/ppermute | solution.py:48
  14.4 5.0 %collective-permute-start.5 = (bf16[32,2048]{1,0:T(8,128)(2,1)S(1)}, bf16[32,2048]{1,0:T(8,128)(2,1)S(1)}, u32[]{:S(2)}, u32[]{:S(2)}) collective-permute-start(bf16[32,2048]{1,0:T(8,128)(2,1)S(1)} %collective-permute-done.3), channel_id=1, source_target_pairs={{0,4},{4,8},{8,12},{12,14},{14,10},{10,6},{6,2},{2,0},{1,5},{5,9},... | collective-permute-start | bytes 393224 | tf_op jit(solution)/shard_map/ppermute | solution.py:45
  16.2 5.3 %collective-permute-start.4 = (bf16[32,2048]{1,0:T(8,128)(2,1)S(1)}, bf16[32,2048]{1,0:T(8,128)(2,1)S(1)}, u32[]{:S(2)}, u32[]{:S(2)}) collective-permute-start(bf16[32,2048]{1,0:T(8,128)(2,1)S(1)} %collective-permute-done.2), channel_id=1, source_target_pairs={{4,0},{8,4},{12,8},{14,12},{10,14},{6,10},{2,6},{0,2},{5,1},{9,5},... | collective-permute-start | bytes 393224 | tf_op jit(solution)/shard_map/ppermute | solution.py:48
  19.4 4.3 %collective-permute-start.6 = (bf16[16,2048]{1,0:T(8,128)(2,1)S(1)}, bf16[16,2048]{1,0:T(8,128)(2,1)S(1)}, u32[]{:S(2)}, u32[]{:S(2)}) collective-permute-start(bf16[16,2048]{1,0:T(8,128)(2,1)S(1)} %slice.100), channel_id=1, source_target_pairs={{0,4},{4,8},{8,12},{12,14},{14,10},{10,6},{6,2},{2,0},{1,5},{5,9},... | collective-permute-start | bytes 196616 | tf_op jit(solution)/shard_map/ppermute | solution.py:45
  21.5 4.3 %collective-permute-start.7 = (bf16[16,2048]{1,0:T(8,128)(2,1)S(1)}, bf16[16,2048]{1,0:T(8,128)(2,1)S(1)}, u32[]{:S(2)}, u32[]{:S(2)}) collective-permute-start(bf16[16,2048]{1,0:T(8,128)(2,1)S(1)} %slice.101), channel_id=1, source_target_pairs={{4,0},{8,4},{12,8},{14,12},{10,14},{6,10},{2,6},{0,2},{5,1},{9,5},... | collective-permute-start | bytes 196616 | tf_op jit(solution)/shard_map/ppermute | solution.py:48
  25.8 7.3 %copy-start.19 = (s32[32,8]{0,1:T(8,128)S(1)}, s32[32,8]{0,1:T(8,128)}, u32[]{:S(2)}) copy-start(s32[32,8]{0,1:T(8,128)} %param.19) | copy-start | bytes 3076
  25.8 7.4 %copy-start.20 = (s32[32,8]{0,1:T(8,128)S(1)}, s32[32,8]{0,1:T(8,128)}, u32[]{:S(2)}) copy-start(s32[32,8]{0,1:T(8,128)} %param.20) | copy-start | bytes 3076
  25.8 7.5 %copy-start.18 = (s32[16]{0:T(128)S(1)}, s32[16]{0:T(128)}, u32[]{:S(2)}) copy-start(s32[16]{0:T(128)} %param.21) | copy-start | bytes 196
  25.9 8.2 %copy-start.15 = (s32[1,32]{1,0:T(1,128)S(1)}, s32[1,32]{1,0:T(1,128)}, u32[]{:S(2)}) copy-start(s32[1,32]{1,0:T(1,128)} %length_ref.1) | copy-start | bytes 388
  28.1 13.9 %all-to-all-start = ((bf16[8,32,640]{2,1,0:T(8,128)(2,1)}), bf16[8,32,640]{2,1,0:T(8,128)(2,1)S(1)}, u32[]{:S(2)}, u32[]{:S(2)}) async-start(bf16[8,32,640]{2,1,0:T(8,128)(2,1)} %project.1.refs_2_), calls=%async_computation | async-start | bytes 655360 | tf_op jit(solution)/shard_map/all_to_all | solution.py:455
  34.3 7.7 %copy-start.16 = (f32[128]{0:T(128)S(1)}, f32[128]{0:T(128)}, u32[]{:S(2)}) copy-start(f32[128]{0:T(128)} %param.24) | copy-start | bytes 1540
  34.3 7.7 %copy-start.17 = (f32[128]{0:T(128)S(1)}, f32[128]{0:T(128)}, u32[]{:S(2)}) copy-start(f32[128]{0:T(128)} %param.25) | copy-start | bytes 1540
  37.8 2.1 %copy-start.2 = (bf16[4096,512]{1,0:T(8,128)(2,1)}, bf16[4096,512]{1,0:T(8,128)(2,1)S(1)}, u32[]{:S(2)}) copy-start(bf16[4096,512]{1,0:T(8,128)(2,1)S(1)} %get-tuple-element.19.key_ref) | copy-start | bytes 12582916
  39.9 2.0 %copy-start.4 = (bf16[4096,512]{1,0:T(8,128)(2,1)}, bf16[4096,512]{1,0:T(8,128)(2,1)S(1)}, u32[]{:S(2)}) copy-start(bf16[4096,512]{1,0:T(8,128)(2,1)S(1)} %get-tuple-element.20.value_ref) | copy-start | bytes 12582916
  42.0 2.2 %copy-start.3 = (bf16[4096,512]{1,0:T(8,128)(2,1)S(1)}, bf16[4096,512]{1,0:T(8,128)(2,1)}, u32[]{:S(2)}) copy-start(bf16[4096,512]{1,0:T(8,128)(2,1)} %copy-done.2) | copy-start | bytes 12582916
  44.2 2.2 %copy-start.5 = (bf16[4096,512]{1,0:T(8,128)(2,1)S(1)}, bf16[4096,512]{1,0:T(8,128)(2,1)}, u32[]{:S(2)}) copy-start(bf16[4096,512]{1,0:T(8,128)(2,1)} %copy-done.4) | copy-start | bytes 12582916
  56.2 14.3 %all-to-all-start.1 = ((bf16[8,32,512]{2,1,0:T(8,128)(2,1)}), bf16[8,32,512]{2,1,0:T(8,128)(2,1)S(1)}, u32[]{:S(2)}, u32[]{:S(2)}) async-start(bf16[8,32,512]{2,1,0:T(8,128)(2,1)} %ragged_attention.1.refs_1_), calls=%async_computation.1 | async-start | bytes 524288 | tf_op jit(solution)/shard_map/all_to_all | solution.py:461
  62.2 1.6 %copy-start.7 = (bf16[512,2048]{1,0:T(8,128)(2,1)S(1)}, bf16[512,2048]{1,0:T(8,128)(2,1)}, u32[]{:S(2)}) copy-start(bf16[512,2048]{1,0:T(8,128)(2,1)} %refs_0_.3) | copy-start | bytes 6291460
  64.0 1.4 copy-start
  70.6 1.6 %copy-start.1 = (bf16[512,2048]{1,0:T(8,128)(2,1)S(1)}, bf16[512,2048]{1,0:T(8,128)(2,1)}, u32[]{:S(2)}) copy-start(bf16[512,2048]{1,0:T(8,128)(2,1)} %copy-done) | copy-start | bytes 6291460
  73.4 0.7 copy-start.11
  74.1 5.0 %collective-permute-start.10 = (bf16[32,1024]{1,0:T(8,128)(2,1)S(1)}, bf16[32,1024]{1,0:T(8,128)(2,1)S(1)}, u32[]{:S(2)}, u32[]{:S(2)}) collective-permute-start(bf16[32,1024]{1,0:T(8,128)(2,1)S(1)} %get-tuple-element.23), channel_id=1, source_target_pairs={{0,4},{4,8},{8,12},{12,14},{14,10},{10,6},{6,2},{2,0},{1,5},{5,9},... | collective-permute-start | bytes 196616 | tf_op jit(solution)/shard_map/ppermute | solution.py:45
  74.1 5.1 %collective-permute-start.14 = (bf16[32,1024]{1,0:T(8,128)(2,1)S(1)}, bf16[32,1024]{1,0:T(8,128)(2,1)S(1)}, u32[]{:S(2)}, u32[]{:S(2)}) collective-permute-start(bf16[32,1024]{1,0:T(8,128)(2,1)S(1)} %get-tuple-element.25), channel_id=1, source_target_pairs={{4,0},{8,4},{12,8},{14,12},{10,14},{6,10},{2,6},{0,2},{5,1},{9,5},... | collective-permute-start | bytes 196616 | tf_op jit(solution)/shard_map/ppermute | solution.py:48
  79.1 6.1 %collective-permute-start.11 = (bf16[32,2048]{1,0:T(8,128)(2,1)S(1)}, bf16[32,2048]{1,0:T(8,128)(2,1)S(1)}, u32[]{:S(2)}, u32[]{:S(2)}) collective-permute-start(bf16[32,2048]{1,0:T(8,128)(2,1)S(1)} %pad_maximum_fusion), channel_id=1, source_target_pairs={{0,4},{4,8},{8,12},{12,14},{14,10},{10,6},{6,2},{2,0},{1,5},{5,9},... | collective-permute-start | bytes 393224 | tf_op jit(solution)/shard_map/ppermute | solution.py:45
  79.2 18.3 %copy-start.10 = (bf16[32,2048]{1,0:T(8,128)(2,1)S(1)}, bf16[32,2048]{1,0:T(8,128)(2,1)}, u32[]{:S(2)}) copy-start(bf16[32,2048]{1,0:T(8,128)(2,1)} %hidden_ref.1) | copy-start | bytes 393220
  79.3 18.3 %copy-start.12 = (f32[32,2048]{1,0:T(8,128)S(1)}, f32[32,2048]{1,0:T(8,128)}, u32[]{:S(2)}) copy-start(f32[32,2048]{1,0:T(8,128)} %copy-done.11) | copy-start | bytes 786436
  79.3 18.3 %copy-start.13 = (f32[2048]{0:T(1024)S(1)}, f32[2048]{0:T(1024)}, u32[]{:S(2)}) copy-start(f32[2048]{0:T(1024)} %param.23) | copy-start | bytes 24580
  79.3 6.0 %collective-permute-start.15 = (bf16[32,2048]{1,0:T(8,128)(2,1)S(1)}, bf16[32,2048]{1,0:T(8,128)(2,1)S(1)}, u32[]{:S(2)}, u32[]{:S(2)}) collective-permute-start(bf16[32,2048]{1,0:T(8,128)(2,1)S(1)} %pad_maximum_fusion.1), channel_id=1, source_target_pairs={{4,0},{8,4},{12,8},{14,12},{10,14},{6,10},{2,6},{0,2},{5,1},{9,5},... | collective-permute-start | bytes 393224 | tf_op jit(solution)/shard_map/ppermute | solution.py:48
  85.3 5.6 %collective-permute-start.12 = (bf16[32,2048]{1,0:T(8,128)(2,1)S(1)}, bf16[32,2048]{1,0:T(8,128)(2,1)S(1)}, u32[]{:S(2)}, u32[]{:S(2)}) collective-permute-start(bf16[32,2048]{1,0:T(8,128)(2,1)S(1)} %fusion.6), channel_id=1, source_target_pairs={{0,4},{4,8},{8,12},{12,14},{14,10},{10,6},{6,2},{2,0},{1,5},{5,9},... | collective-permute-start | bytes 393224 | tf_op jit(solution)/shard_map/ppermute | solution.py:45
  85.4 6.2 %collective-permute-start.16 = (bf16[32,2048]{1,0:T(8,128)(2,1)S(1)}, bf16[32,2048]{1,0:T(8,128)(2,1)S(1)}, u32[]{:S(2)}, u32[]{:S(2)}) collective-permute-start(bf16[32,2048]{1,0:T(8,128)(2,1)S(1)} %fusion.4), channel_id=1, source_target_pairs={{4,0},{8,4},{12,8},{14,12},{10,14},{6,10},{2,6},{0,2},{5,1},{9,5},... | collective-permute-start | bytes 393224 | tf_op jit(solution)/shard_map/ppermute | solution.py:48
  91.6 5.6 %collective-permute-start.13 = (bf16[32,2048]{1,0:T(8,128)(2,1)}, bf16[32,2048]{1,0:T(8,128)(2,1)}, u32[]{:S(2)}, u32[]{:S(2)}) collective-permute-start(bf16[32,2048]{1,0:T(8,128)(2,1)} %fusion.7), channel_id=1, source_target_pairs={{0,4},{4,8},{8,12},{12,14},{14,10},{10,6},{6,2},{2,0},{1,5},{5,9},... | collective-permute-start | bytes 393224 | tf_op jit(solution)/shard_map/ppermute | solution.py:45
  92.2 5.3 %collective-permute-start.17 = (bf16[32,2048]{1,0:T(8,128)(2,1)}, bf16[32,2048]{1,0:T(8,128)(2,1)}, u32[]{:S(2)}, u32[]{:S(2)}) collective-permute-start(bf16[32,2048]{1,0:T(8,128)(2,1)} %fusion.5), channel_id=1, source_target_pairs={{4,0},{8,4},{12,8},{14,12},{10,14},{6,10},{2,6},{0,2},{5,1},{9,5},... | collective-permute-start | bytes 393224 | tf_op jit(solution)/shard_map/ppermute | solution.py:48
  98.7 5.5 %collective-permute-start.19 = (bf16[32,2176]{1,0:T(8,128)(2,1)S(1)}, bf16[32,2176]{1,0:T(8,128)(2,1)S(1)}, u32[]{:S(2)}, u32[]{:S(2)}) collective-permute-start(bf16[32,2176]{1,0:T(8,128)(2,1)S(1)} %get-tuple-element.27), channel_id=1, source_target_pairs={{0,4},{4,8},{8,12},{12,14},{14,10},{10,6},{6,2},{2,0},{1,5},{5,9},... | collective-permute-start | bytes 417800 | tf_op jit(solution)/shard_map/ppermute | solution.py:45
  99.4 5.8 %collective-permute-start.18 = (bf16[32,2176]{1,0:T(8,128)(2,1)S(1)}, bf16[32,2176]{1,0:T(8,128)(2,1)S(1)}, u32[]{:S(2)}, u32[]{:S(2)}) collective-permute-start(bf16[32,2176]{1,0:T(8,128)(2,1)S(1)} %get-tuple-element.27), channel_id=1, source_target_pairs={{4,0},{8,4},{12,8},{14,12},{10,14},{6,10},{2,6},{0,2},{5,1},{9,5},... | collective-permute-start | bytes 417800 | tf_op jit(solution)/shard_map/ppermute | solution.py:48
  104.2 5.4 %collective-permute-start.21 = (bf16[32,2176]{1,0:T(8,128)(2,1)S(1)}, bf16[32,2176]{1,0:T(8,128)(2,1)S(1)}, u32[]{:S(2)}, u32[]{:S(2)}) collective-permute-start(bf16[32,2176]{1,0:T(8,128)(2,1)S(1)} %collective-permute-done.19), channel_id=1, source_target_pairs={{0,4},{4,8},{8,12},{12,14},{14,10},{10,6},{6,2},{2,0},{1,5},{5,9},... | collective-permute-start | bytes 417800 | tf_op jit(solution)/shard_map/ppermute | solution.py:45
  105.2 5.1 %collective-permute-start.20 = (bf16[32,2176]{1,0:T(8,128)(2,1)S(1)}, bf16[32,2176]{1,0:T(8,128)(2,1)S(1)}, u32[]{:S(2)}, u32[]{:S(2)}) collective-permute-start(bf16[32,2176]{1,0:T(8,128)(2,1)S(1)} %collective-permute-done.18.refs_1_), channel_id=1, source_target_pairs={{4,0},{8,4},{12,8},{14,12},{10,14},{6,10},{2,6},{0,2},{5,1},{9,5},... | collective-permute-start | bytes 417800 | tf_op jit(solution)/shard_map/ppermute | solution.py:48
  106.6 5.1 %copy-start.6 = (bf16[1,768,2048]{2,1,0:T(8,128)(2,1)S(1)}, bf16[1,768,2048]{2,1,0:T(8,128)(2,1)}, u32[]{:S(2)}) copy-start(bf16[1,768,2048]{2,1,0:T(8,128)(2,1)} %param.29) | copy-start | bytes 9437188
  109.6 5.1 %collective-permute-start.23 = (bf16[32,2176]{1,0:T(8,128)(2,1)S(1)}, bf16[32,2176]{1,0:T(8,128)(2,1)S(1)}, u32[]{:S(2)}, u32[]{:S(2)}) collective-permute-start(bf16[32,2176]{1,0:T(8,128)(2,1)S(1)} %collective-permute-done.21), channel_id=1, source_target_pairs={{0,4},{4,8},{8,12},{12,14},{14,10},{10,6},{6,2},{2,0},{1,5},{5,9},... | collective-permute-start | bytes 417800 | tf_op jit(solution)/shard_map/ppermute | solution.py:45
  110.3 5.1 %collective-permute-start.22 = (bf16[32,2176]{1,0:T(8,128)(2,1)S(1)}, bf16[32,2176]{1,0:T(8,128)(2,1)S(1)}, u32[]{:S(2)}, u32[]{:S(2)}) collective-permute-start(bf16[32,2176]{1,0:T(8,128)(2,1)S(1)} %collective-permute-done.20.refs_1_), channel_id=1, source_target_pairs={{4,0},{8,4},{12,8},{14,12},{10,14},{6,10},{2,6},{0,2},{5,1},{9,5},... | collective-permute-start | bytes 417800 | tf_op jit(solution)/shard_map/ppermute | solution.py:48
  114.7 4.7 %collective-permute-start.24 = (bf16[16,2176]{1,0:T(8,128)(2,1)S(1)}, bf16[16,2176]{1,0:T(8,128)(2,1)S(1)}, u32[]{:S(2)}, u32[]{:S(2)}) collective-permute-start(bf16[16,2176]{1,0:T(8,128)(2,1)S(1)} %slice.106), channel_id=1, source_target_pairs={{0,4},{4,8},{8,12},{12,14},{14,10},{10,6},{6,2},{2,0},{1,5},{5,9},... | collective-permute-start | bytes 208904 | tf_op jit(solution)/shard_map/ppermute | solution.py:45
  115.3 5.1 %collective-permute-start.25 = (bf16[16,2176]{1,0:T(8,128)(2,1)S(1)}, bf16[16,2176]{1,0:T(8,128)(2,1)S(1)}, u32[]{:S(2)}, u32[]{:S(2)}) collective-permute-start(bf16[16,2176]{1,0:T(8,128)(2,1)S(1)} %slice.107), channel_id=1, source_target_pairs={{4,0},{8,4},{12,8},{14,12},{10,14},{6,10},{2,6},{0,2},{5,1},{9,5},... | collective-permute-start | bytes 208904 | tf_op jit(solution)/shard_map/ppermute | solution.py:48
  128.3 4.3 %collective-permute-start.26 = (bf16[32,1024]{1,0:T(8,128)(2,1)S(1)}, bf16[32,1024]{1,0:T(8,128)(2,1)S(1)}, u32[]{:S(2)}, u32[]{:S(2)}) collective-permute-start(bf16[32,1024]{1,0:T(8,128)(2,1)S(1)} %get-tuple-element.30), channel_id=1, source_target_pairs={{0,4},{4,8},{8,12},{12,14},{14,10},{10,6},{6,2},{2,0},{1,5},{5,9},... | collective-permute-start | bytes 196616 | tf_op jit(solution)/shard_map/ppermute | solution.py:45
  128.9 4.4 %collective-permute-start.30 = (bf16[32,1024]{1,0:T(8,128)(2,1)S(1)}, bf16[32,1024]{1,0:T(8,128)(2,1)S(1)}, u32[]{:S(2)}, u32[]{:S(2)}) collective-permute-start(bf16[32,1024]{1,0:T(8,128)(2,1)S(1)} %get-tuple-element.32), channel_id=1, source_target_pairs={{4,0},{8,4},{12,8},{14,12},{10,14},{6,10},{2,6},{0,2},{5,1},{9,5},... | collective-permute-start | bytes 196616 | tf_op jit(solution)/shard_map/ppermute | solution.py:48
  132.7 5.0 %collective-permute-start.27 = (bf16[32,2048]{1,0:T(8,128)(2,1)S(1)}, bf16[32,2048]{1,0:T(8,128)(2,1)S(1)}, u32[]{:S(2)}, u32[]{:S(2)}) collective-permute-start(bf16[32,2048]{1,0:T(8,128)(2,1)S(1)} %pad_maximum_fusion.2), channel_id=1, source_target_pairs={{0,4},{4,8},{8,12},{12,14},{14,10},{10,6},{6,2},{2,0},{1,5},{5,9},... | collective-permute-start | bytes 393224 | tf_op jit(solution)/shard_map/ppermute | solution.py:45
  133.3 5.0 %collective-permute-start.31 = (bf16[32,2048]{1,0:T(8,128)(2,1)S(1)}, bf16[32,2048]{1,0:T(8,128)(2,1)S(1)}, u32[]{:S(2)}, u32[]{:S(2)}) collective-permute-start(bf16[32,2048]{1,0:T(8,128)(2,1)S(1)} %pad_maximum_fusion.3), channel_id=1, source_target_pairs={{4,0},{8,4},{12,8},{14,12},{10,14},{6,10},{2,6},{0,2},{5,1},{9,5},... | collective-permute-start | bytes 393224 | tf_op jit(solution)/shard_map/ppermute | solution.py:48
  137.7 5.0 %collective-permute-start.28 = (bf16[32,2048]{1,0:T(8,128)(2,1)S(1)}, bf16[32,2048]{1,0:T(8,128)(2,1)S(1)}, u32[]{:S(2)}, u32[]{:S(2)}) collective-permute-start(bf16[32,2048]{1,0:T(8,128)(2,1)S(1)} %fusion.2), channel_id=1, source_target_pairs={{0,4},{4,8},{8,12},{12,14},{14,10},{10,6},{6,2},{2,0},{1,5},{5,9},... | collective-permute-start | bytes 393224 | tf_op jit(solution)/shard_map/ppermute | solution.py:45
  138.3 5.0 %collective-permute-start.32 = (bf16[32,2048]{1,0:T(8,128)(2,1)S(1)}, bf16[32,2048]{1,0:T(8,128)(2,1)S(1)}, u32[]{:S(2)}, u32[]{:S(2)}) collective-permute-start(bf16[32,2048]{1,0:T(8,128)(2,1)S(1)} %fusion), channel_id=1, source_target_pairs={{4,0},{8,4},{12,8},{14,12},{10,14},{6,10},{2,6},{0,2},{5,1},{9,5},... | collective-permute-start | bytes 393224 | tf_op jit(solution)/shard_map/ppermute | solution.py:48
  142.8 5.0 %collective-permute-start.29 = (bf16[32,2048]{1,0:T(8,128)(2,1)S(1)}, bf16[32,2048]{1,0:T(8,128)(2,1)S(1)}, u32[]{:S(2)}, u32[]{:S(2)}) collective-permute-start(bf16[32,2048]{1,0:T(8,128)(2,1)S(1)} %fusion.3), channel_id=1, source_target_pairs={{0,4},{4,8},{8,12},{12,14},{14,10},{10,6},{6,2},{2,0},{1,5},{5,9},... | collective-permute-start | bytes 393224 | tf_op jit(solution)/shard_map/ppermute | solution.py:45
  143.4 5.0 %collective-permute-start.33 = (bf16[32,2048]{1,0:T(8,128)(2,1)S(1)}, bf16[32,2048]{1,0:T(8,128)(2,1)S(1)}, u32[]{:S(2)}, u32[]{:S(2)}) collective-permute-start(bf16[32,2048]{1,0:T(8,128)(2,1)S(1)} %fusion.1), channel_id=1, source_target_pairs={{4,0},{8,4},{12,8},{14,12},{10,14},{6,10},{2,6},{0,2},{5,1},{9,5},... | collective-permute-start | bytes 393224 | tf_op jit(solution)/shard_map/ppermute | solution.py:48

commit v2 on v1

--- a/solution.py
+++ b/solution.py
@@ -121,14 +121,6 @@
     return copies
 
 
-def norm_kernel(hidden_hbm, gain_hbm, out_ref, hidden_ref, gain_ref, sems):
-    pairs = [(hidden_hbm, hidden_ref), (gain_hbm, gain_ref)]
-    for copy in start_copies(pairs, sems):
-        copy.wait()
-    values = hidden_ref[...].astype(jnp.float32)
-    out_ref[...] = norm_scale(values, gain_ref[...]).astype(jnp.bfloat16)
-
-
 def digit_kernel(holder_ref, ids_ref, codes_ref, out_ref):
     ids, codes = ids_ref[...], codes_ref[...]
     lane = lax.broadcasted_iota(jnp.int32, out_ref.shape, 1)
@@ -141,6 +133,10 @@
     out_ref[...] = high.astype(jnp.bfloat16)
 
 
+def tiled_gain(gain):
+    return jnp.broadcast_to(gain[None, :], (8, gain.shape[0]))
+
+
 def load_kernel(number, *refs):
     sources, targets, sems = refs[:number], refs[-1 - number : -1], refs[-1]
     for copy in start_copies(list(zip(sources, targets)), sems):
@@ -160,9 +156,14 @@
     )
 
 
-def project_kernel(count, owner_ref, normed_ref, weight_ref, out_ref):
-    rows = normed_ref.shape[0] // count
-    product = jnp.dot(normed_ref[...], weight_ref[...], preferred_element_type=jnp.float32)
+def project_kernel(count, owner_ref, hidden_ref, gain_ref, weight_ref, out_ref, held):
+    rows = hidden_ref.shape[0] // count
+    gain = gain_ref[:1, :]
+    for index in range(count):
+        at = slice(index * rows, (index + 1) * rows)
+        values = hidden_ref[at, :].astype(jnp.float32)
+        held[at, :] = norm_scale(values, gain).astype(jnp.bfloat16)
+    product = jnp.dot(held[...], weight_ref[...], preferred_element_type=jnp.float32)
     product = product.astype(jnp.bfloat16)
     for index in range(count):
         out_ref[owner_ref[0, index]] = product[index * rows : (index + 1) * rows]
@@ -203,7 +204,7 @@
     summed = own_ref[...] + up_ref[...].astype(jnp.float32) + down_ref[...].astype(jnp.float32)
     residual = hidden_ref[...].astype(jnp.float32) + summed
     residual_ref[...] = residual
-    sent_ref[:, :width] = norm_scale(residual, gain_ref[...]).astype(jnp.bfloat16)
+    sent_ref[:, :width] = norm_scale(residual, gain_ref[:1, :]).astype(jnp.bfloat16)
     sent_ref[:, width:] = digit_ref[...]
 
 
@@ -252,11 +253,16 @@
     sin_ref,
     query_gain_ref,
     key_gain_ref,
-    key_ref,
-    value_ref,
+    key_hbm,
+    value_hbm,
     *refs,
 ):
-    out_ref, queries, results, new_keys, new_values, start_ref = refs[-6:]
+    out_ref, queries, results, new_keys, new_values, key_ref, value_ref, start_ref, sems = refs[-9:]
+    fetches = [
+        pltpu.make_async_copy(key_hbm, key_ref, sems.at[0]),
+        pltpu.make_async_copy(value_hbm, value_ref, sems.at[1]),
+    ]
+    fetches[0].start()
     rows = merged_ref.shape[1]
     heads = queries.shape[0] // rows
     group = heads // kv_count
@@ -287,7 +293,11 @@
         new_keys[:, columns] = turned(head(heads + kv), key_gain)
         new_values[:, columns] = head(heads + kv_count + kv)
     for index in range(heads):
+        if index == heads // 2:
+            fetches[1].start()
         queries[pl.ds(index, rows, stride=heads), :] = turned(head(index), query_gain)
+
+    fetches[0].wait()
 
     place = lax.broadcasted_iota(jnp.int32, (WINDOW + ALIGN, heads), 0)
     kv_of_row = lax.broadcasted_iota(jnp.int32, (heads, HD), 0) // group
@@ -342,6 +352,11 @@
     def body(step, carry):
         at = [step * UNROLL + inner for inner in range(UNROLL)]
         weights = [weighed(scores) for scores in [scored(row) for row in at]]
+
+        @pl.when(step == 0)
+        def _():
+            fetches[1].wait()
+
         for row, weight in zip(at, weights):
             mix(row, weight)
         return carry
@@ -366,7 +381,7 @@
     return call(
         functools.partial(attention_kernel, kv_count),
         jax.ShapeDtypeStruct((count, rows, heads * HD // count), jnp.bfloat16),
-        [SMEM] + [VMEM] * 7 + [HBM] * len(swapped),
+        [SMEM] + [VMEM] * 5 + [HBM] * (2 + len(swapped)),
         (
             lengths,
             merged,
@@ -383,9 +398,12 @@
             pltpu.VMEM((heads * rows, HD), jnp.float32),
             pltpu.VMEM((rows, kv_count * HD), jnp.float32),
             pltpu.VMEM((rows, kv_count * HD), jnp.float32),
+            pltpu.VMEM(keys.shape, keys.dtype),
+            pltpu.VMEM(values.shape, values.dtype),
             pltpu.SMEM((rows + 1,), jnp.int32),
+            pltpu.SemaphoreType.DMA((2,)),
         ],
-        12,
+        57,
         "ragged_attention",
     )
 
@@ -430,33 +448,23 @@
         4,
         "gate_digits",
     )
-    normed = call(
-        norm_kernel,
-        jax.ShapeDtypeStruct((rows, width), bf16),
-        [ANY] * 2,
-        (hidden, attention_gain[None, :]),
-        [pltpu.VMEM((rows, width), bf16), pltpu.VMEM((1, width), jnp.float32), dma((2,))],
-        4,
-        "attention_norm",
-    )
     columns = project_weight.shape[1]
-    gathered, pieces = ring_gather(ring, normed)
+    gathered, pieces = ring_gather(ring, hidden)
     (project_weight,) = loaded([project_weight], pieces[1], 50, "load_project")
     blocks = call(
         functools.partial(project_kernel, count),
         jax.ShapeDtypeStruct((count, rows, columns), bf16),
-        [SMEM, VMEM, VMEM],
-        (owners, gathered, project_weight),
-        [],
+        [SMEM, VMEM, VMEM, VMEM],
+        (owners, gathered, tiled_gain(attention_gain), project_weight),
+        [pltpu.VMEM((count * rows, width), bf16)],
         8,
         "project",
     )
-    keys, values = loaded([key_cache[0], value_cache[0]], blocks, 44, "load_caches")
     blocks = lax.all_to_all(blocks, "dev", split_axis=0, concat_axis=0, tiled=True)
     if columns % HD:
         blocks = jnp.transpose(blocks, (1, 0, 2)).reshape(1, rows, -1)
     attention = attend(
-        blocks, lengths, query_gain, key_gain, keys, values, count, [digits, *gate_ups, *downs]
+        blocks, lengths, query_gain, key_gain, key_cache[0], value_cache[0], count, [digits, *gate_ups, *downs]
     )
     features = lax.all_to_all(attention, "dev", split_axis=0, concat_axis=0, tiled=True)
     (output_weight,) = loaded([output_weight], attention, 44, "load_output")
@@ -477,7 +485,7 @@
             jax.ShapeDtypeStruct((rows, width + HD), bf16),
         ],
         [VMEM] * 6,
-        (hidden, own, up, down, mixture_gain[None, :], digits),
+        (hidden, own, up, down, tiled_gain(mixture_gain), digits),
         [],
         4,
         "residual_norm",
@@ -485,13 +493,15 @@
     shifts = jnp.arange(subs, dtype=jnp.int32)[None, :]
     own_slots = lax.axis_index("dev") * subs + (lax.axis_index("sub") + shifts) % subs
     gathered, pieces = ring_gather(ring, sent)
-    (own_gate_up,) = loaded([expert_gate_up[0]], pieces[1], 42, "load_gate_up")
-    (own_down,) = loaded([expert_down[0]], pieces[3], 42, "load_down")
+    weights = []
+    for index, gate_up in enumerate([expert_gate_up[0]] + gate_ups):
+        weights += loaded([gate_up], pieces[2 * index + 1], 4, "load_gate_up")
+    weights += loaded([expert_down[0]] + downs, pieces[2 * subs + 1], 4, "load_downs")
     own, *partial = call(
         functools.partial(expert_kernel, count, slots),
         block_shapes(count, rows, width),
         [SMEM] + [VMEM] * (1 + 2 * subs),
-        (own_slots, gathered, own_gate_up, *gate_ups, own_down, *downs),
+        (own_slots, gathered, *weights),
         [
             pltpu.VMEM((count * rows, expert_down.shape[1]), bf16),
             pltpu.VMEM((count * rows, width), jnp.float32),

time: 150 us -> 139 us (0.927)
  local copies, waits for them, and re-layouts: 17.5 us -> 9.84 us
  waiting for transfers between devices: 50.1 us -> 54.9 us
  Pallas kernels: 32 us -> 27.6 us
  starting transfers between devices: 46.3 us -> 43.6 us
    unnamed x60 -> x50, local copies, waits for them, and re-layouts: 17.3 us -> 9.68 us
    all_to_all x1, waiting for transfers between devices: 0.01 us -> 6.39 us  [on_device(): lax.all_to_all(blocks, 'dev', split_axis=0, concat_axis=0, tiled=True)]
    ppermute x16, starting transfers between devices: 14 us -> 19.4 us  [ahead(): return lax.ppermute(values, 'dev', self.forward)]
    ppermute x16, starting transfers between devices: 20.9 us -> 15.4 us  [behind(): return lax.ppermute(values, 'dev', self.backward)]
    pallas_call x12 -> x11, Pallas kernels: 32 us -> 27.6 us  [call(): pl.pallas_call(body, out_shape=outs, in_specs=whole_blocks(ins), out_spec...]
    ppermute x16, waiting for transfers between devices: 40.9 us -> 37.7 us  [ahead(): return lax.ppermute(values, 'dev', self.forward)]
    all_to_all x1, starting transfers between devices: 6 us -> 3.42 us  [on_device(): lax.all_to_all(attention, 'dev', split_axis=0, concat_axis=0, tiled=True)]
  transfers between devices with their start and end apart: 36 -> 36, of which waited for: 20 -> 20; matrix products, arithmetic and copies ran while one was open for 3% -> 2% of each run, Pallas kernels for 8% -> 6%
where the time goes in v2:
time: 139 us; the launch traced here: 138 us
  waiting for transfers between devices  54.9 us (39%)
  starting transfers between devices  43.6 us (31%)
  Pallas kernels  27.6 us (20%)
  local copies, waits for them, and re-layouts  9.84 us (7%)
  other arithmetic  1.95 us (1%)
    ppermute x16, waiting for transfers between devices, ahead(): return lax.ppermute(values, 'dev', self.forward)  37.7 us
    pallas_call x11, Pallas kernels, call(): pl.pallas_call(body, out_shape=outs, in_specs=whole_blocks(ins), out_spec...  27.6 us
    ppermute x16, starting transfers between devices, ahead(): return lax.ppermute(values, 'dev', self.forward)  19.4 us
    ppermute x16, starting transfers between devices, behind(): return lax.ppermute(values, 'dev', self.backward)  15.4 us
    unnamed x50, local copies, waits for them, and re-layouts  9.68 us
    all_to_all x1, waiting for transfers between devices, on_device(): lax.all_to_all(blocks, 'dev', split_axis=0, concat_axis=0, tiled=True)  6.39 us
    all_to_all x1, waiting for transfers between devices, on_device(): lax.all_to_all(attention, 'dev', split_axis=0, concat_axis=0, tiled=True)  5.43 us
    ppermute x16, waiting for transfers between devices, behind(): return lax.ppermute(values, 'dev', self.backward)  5.38 us
  transfers between devices with their start and end apart: 36, of which 20 were waited for; matrix products, arithmetic and copies ran while one was open for 2% of the time, Pallas kernels for 6%

profile of v2, /device:TPU:0, one launch (start us, length us, event | category | flops | bytes accessed | tf_op | source)
XLA Modules:
  0.0 138.4 jit_solution(9134858268271489740)
XLA Ops:
  0.0 0.5 collective-permute-start.8
  0.5 3.0 %collective-permute-start.1 = (bf16[32,2048]{1,0:T(8,128)(2,1)}, bf16[32,2048]{1,0:T(8,128)(2,1)S(1)}, u32[]{:S(2)}, u32[]{:S(2)}) collective-permute-start(bf16[32,2048]{1,0:T(8,128)(2,1)} %hidden_ref.1), channel_id=1, source_target_pairs={{0,4},{4,8},{8,12},{12,14},{14,10},{10,6},{6,2},{2,0},{1,5},{5,9},... | collective-permute-start | bytes 393224 | tf_op jit(solution)/shard_map/ppermute | solution.py:45
  3.5 1.6 %constant_dynamic-update-slice_fusion.8 = bf16[256,2048]{1,0:T(8,128)(2,1)} fusion(bf16[32,2048]{1,0:T(8,128)(2,1)} %hidden_ref.1), kind=kLoop, calls=%fused_computation.45 | loop fusion | bytes 262144
  5.2 2.2 %collective-permute-done.1 = bf16[32,2048]{1,0:T(8,128)(2,1)S(1)} collective-permute-done((bf16[32,2048]{1,0:T(8,128)(2,1)}, bf16[32,2048]{1,0:T(8,128)(2,1)S(1)}, u32[]{:S(2)}, u32[]{:S(2)}) %collective-permute-start.1) | collective-permute-done | bytes 131104 | tf_op jit(solution)/shard_map/ppermute | solution.py:45
  7.4 1.8 %collective-permute-start.3 = (bf16[32,2048]{1,0:T(8,128)(2,1)S(1)}, bf16[32,2048]{1,0:T(8,128)(2,1)S(1)}, u32[]{:S(2)}, u32[]{:S(2)}) collective-permute-start(bf16[32,2048]{1,0:T(8,128)(2,1)S(1)} %collective-permute-done.1), channel_id=1, source_target_pairs={{0,4},{4,8},{8,12},{12,14},{14,10},{10,6},{6,2},{2,0},{1,5},{5,9},... | collective-permute-start | bytes 393224 | tf_op jit(solution)/shard_map/ppermute | solution.py:45
  9.4 1.7 %load_project.1.weight_ref = bf16[2048,640]{1,0:T(8,128)(2,1)S(1)} custom-call(bf16[2048,640]{1,0:T(8,128)(2,1)} %refs_0_.2, bf16[32,2048]{1,0:T(8,128)(2,1)S(1)} %collective-permute-done.refs_1_), custom_call_target="tpu_custom_call" | custom-call | bytes 104857600 | tf_op jit(solution)/shard_map/load_project/pallas_call | solution.py:97
  11.2 1.1 collective-permute-done.3
  12.3 1.8 %collective-permute-start.5 = (bf16[32,2048]{1,0:T(8,128)(2,1)S(1)}, bf16[32,2048]{1,0:T(8,128)(2,1)S(1)}, u32[]{:S(2)}, u32[]{:S(2)}) collective-permute-start(bf16[32,2048]{1,0:T(8,128)(2,1)S(1)} %collective-permute-done.3), channel_id=1, source_target_pairs={{0,4},{4,8},{8,12},{12,14},{14,10},{10,6},{6,2},{2,0},{1,5},{5,9},... | collective-permute-start | bytes 393224 | tf_op jit(solution)/shard_map/ppermute | solution.py:45
  14.4 3.1 %collective-permute-done.5 = bf16[32,2048]{1,0:T(8,128)(2,1)S(1)} collective-permute-done((bf16[32,2048]{1,0:T(8,128)(2,1)S(1)}, bf16[32,2048]{1,0:T(8,128)(2,1)S(1)}, u32[]{:S(2)}, u32[]{:S(2)}) %collective-permute-start.5) | collective-permute-done | bytes 131104 | tf_op jit(solution)/shard_map/ppermute | solution.py:45
  17.5 2.2 %collective-permute-start.6 = (bf16[16,2048]{1,0:T(8,128)(2,1)S(1)}, bf16[16,2048]{1,0:T(8,128)(2,1)S(1)}, u32[]{:S(2)}, u32[]{:S(2)}) collective-permute-start(bf16[16,2048]{1,0:T(8,128)(2,1)S(1)} %slice.100), channel_id=1, source_target_pairs={{0,4},{4,8},{8,12},{12,14},{14,10},{10,6},{6,2},{2,0},{1,5},{5,9},... | collective-permute-start | bytes 196616 | tf_op jit(solution)/shard_map/ppermute | solution.py:45
  19.8 2.1 %collective-permute-done.6 = bf16[16,2048]{1,0:T(8,128)(2,1)S(1)} collective-permute-done((bf16[16,2048]{1,0:T(8,128)(2,1)S(1)}, bf16[16,2048]{1,0:T(8,128)(2,1)S(1)}, u32[]{:S(2)}, u32[]{:S(2)}) %collective-permute-start.6) | collective-permute-done | bytes 65568 | tf_op jit(solution)/shard_map/ppermute | solution.py:45
  21.9 2.1 %collective-permute-done.7 = bf16[16,2048]{1,0:T(8,128)(2,1)S(1)} collective-permute-done((bf16[16,2048]{1,0:T(8,128)(2,1)S(1)}, bf16[16,2048]{1,0:T(8,128)(2,1)S(1)}, u32[]{:S(2)}, u32[]{:S(2)}) %collective-permute-start.7) | collective-permute-done | bytes 65568 | tf_op jit(solution)/shard_map/ppermute | solution.py:48
  24.1 2.5 %project.1 = bf16[8,32,640]{2,1,0:T(8,128)(2,1)} custom-call(s32[1,8]{1,0:T(1,128)S(1)} %compare_select_fusion.4.owner_ref, bf16[256,2048]{1,0:T(8,128)(2,1)S(1)} %constant_dynamic-update-slice_fusion.hidden_ref, f32[8,2048]{1,0:T(8,128)S(1)} %broadcast_in_dim.10.gain_ref, bf16[2048,640]{1,0:T(8,128)(2,1)S(1)} %load_project.1.weight_ref), custom_call_target="tpu_custom_call" | custom-call | bytes 104857600 | tf_op jit(solution)/shard_map/project/pallas_call | solution.py:97
  26.6 4.8 %all-to-all-start = ((bf16[8,32,640]{2,1,0:T(8,128)(2,1)}), bf16[8,32,640]{2,1,0:T(8,128)(2,1)}, u32[]{:S(2)}, u32[]{:S(2)}) async-start(bf16[8,32,640]{2,1,0:T(8,128)(2,1)} %project.1), calls=%async_computation | async-start | bytes 655360 | tf_op jit(solution)/shard_map/all_to_all | solution.py:463
  31.6 0.8 gate_digits.1.refs_0_.digit_ref
  32.3 0.6 copy-done.8
  33.1 0.7 pad_maximum_fusion.4
  33.8 6.4 %all-to-all-done.merged_ref = bf16[8,32,640]{2,1,0:T(8,128)(2,1)} async-done(((bf16[8,32,640]{2,1,0:T(8,128)(2,1)}), bf16[8,32,640]{2,1,0:T(8,128)(2,1)}, u32[]{:S(2)}, u32[]{:S(2)}) %all-to-all-start) | async-done | bytes 327712 | tf_op jit(solution)/shard_map/all_to_all | solution.py:463
  40.2 1.7 %copy-done = bf16[768,2048]{1,0:T(8,128)(2,1)} copy-done((bf16[768,2048]{1,0:T(8,128)(2,1)}, bf16[768,2048]{1,0:T(8,128)(2,1)S(1)}, u32[]{:S(2)}) %copy-start) | copy-done | bytes 3145752
  41.9 11.5 %ragged_attention.1.refs_1_ = bf16[8,32,512]{2,1,0:T(8,128)(2,1)} custom-call(s32[1,32]{1,0:T(1,128)} %length_ref.1, bf16[8,32,640]{2,1,0:T(8,128)(2,1)} %all-to-all-done.merged_ref, f32[32,128]{1,0:T(8,128)} %get-tuple-element.36.cos_ref, f32[32,128]{1,0:T(8,128)} %get-tuple-element.37.sin_ref, f32[1,128]{1,0:T(1,128)} %bitcast.56, f32[1,128]{1,0:T(1,128)} %bitcast.57, ...), custom_call_target="tpu_custom_call" | custom-call | bytes 104857600 | tf_op jit(solution)/shard_map/ragged_attention/pallas_call | solution.py:97
  53.4 3.4 %all-to-all-start.1 = ((bf16[8,32,512]{2,1,0:T(8,128)(2,1)}), bf16[8,32,512]{2,1,0:T(8,128)(2,1)S(1)}, u32[]{:S(2)}, u32[]{:S(2)}) async-start(bf16[8,32,512]{2,1,0:T(8,128)(2,1)} %ragged_attention.1.refs_1_), calls=%async_computation.1 | async-start | bytes 524288 | tf_op jit(solution)/shard_map/all_to_all | solution.py:469
  56.8 1.0 copy-done.4
  57.8 1.6 %copy-done.5 = bf16[512,2048]{1,0:T(8,128)(2,1)S(1)} copy-done((bf16[512,2048]{1,0:T(8,128)(2,1)S(1)}, bf16[512,2048]{1,0:T(8,128)(2,1)}, u32[]{:S(2)}) %copy-start.5) | copy-done | bytes 2097176
  59.5 5.4 %all-to-all-done.1.feature_ref = bf16[8,32,512]{2,1,0:T(8,128)(2,1)S(1)} async-done(((bf16[8,32,512]{2,1,0:T(8,128)(2,1)}), bf16[8,32,512]{2,1,0:T(8,128)(2,1)S(1)}, u32[]{:S(2)}, u32[]{:S(2)}) %all-to-all-start.1) | async-done | bytes 262176 | tf_op jit(solution)/shard_map/all_to_all | solution.py:469
  65.0 1.2 output_projection.1
  66.2 1.1 collective-permute-start.10
  67.3 1.0 collective-permute-start.14
  68.4 2.6 %collective-permute-done.10 = bf16[32,1024]{1,0:T(8,128)(2,1)S(1)} collective-permute-done((bf16[32,1024]{1,0:T(8,128)(2,1)S(1)}, bf16[32,1024]{1,0:T(8,128)(2,1)S(1)}, u32[]{:S(2)}, u32[]{:S(2)}) %collective-permute-start.10) | collective-permute-done | bytes 65568 | tf_op jit(solution)/shard_map/ppermute | solution.py:45
  71.0 1.3 collective-permute-start.11
  72.4 0.9 collective-permute-start.15
  73.3 4.0 %collective-permute-done.11 = bf16[32,2048]{1,0:T(8,128)(2,1)S(1)} collective-permute-done((bf16[32,2048]{1,0:T(8,128)(2,1)S(1)}, bf16[32,2048]{1,0:T(8,128)(2,1)S(1)}, u32[]{:S(2)}, u32[]{:S(2)}) %collective-permute-start.11) | collective-permute-done | bytes 131104 | tf_op jit(solution)/shard_map/ppermute | solution.py:45
  77.3 0.9 collective-permute-start.12
  78.2 1.3 collective-permute-start.16
  79.5 3.8 %collective-permute-done.12 = bf16[32,2048]{1,0:T(8,128)(2,1)S(1)} collective-permute-done((bf16[32,2048]{1,0:T(8,128)(2,1)S(1)}, bf16[32,2048]{1,0:T(8,128)(2,1)S(1)}, u32[]{:S(2)}, u32[]{:S(2)}) %collective-permute-start.12) | collective-permute-done | bytes 131104 | tf_op jit(solution)/shard_map/ppermute | solution.py:45
  83.3 1.3 collective-permute-start.13
  84.6 0.9 collective-permute-start.17
  85.5 3.0 %collective-permute-done.13.up_ref = bf16[32,2048]{1,0:T(8,128)(2,1)S(1)} collective-permute-done((bf16[32,2048]{1,0:T(8,128)(2,1)S(1)}, bf16[32,2048]{1,0:T(8,128)(2,1)S(1)}, u32[]{:S(2)}, u32[]{:S(2)}) %collective-permute-start.13) | collective-permute-done | bytes 131104 | tf_op jit(solution)/shard_map/ppermute | solution.py:45
  88.5 1.4 %collective-permute-done.17.down_ref = bf16[32,2048]{1,0:T(8,128)(2,1)S(1)} collective-permute-done((bf16[32,2048]{1,0:T(8,128)(2,1)S(1)}, bf16[32,2048]{1,0:T(8,128)(2,1)S(1)}, u32[]{:S(2)}, u32[]{:S(2)}) %collective-permute-start.17) | collective-permute-done | bytes 131104 | tf_op jit(solution)/shard_map/ppermute | solution.py:48
  90.6 1.7 %collective-permute-start.18 = (bf16[32,2176]{1,0:T(8,128)(2,1)S(1)}, bf16[32,2176]{1,0:T(8,128)(2,1)S(1)}, u32[]{:S(2)}, u32[]{:S(2)}) collective-permute-start(bf16[32,2176]{1,0:T(8,128)(2,1)S(1)} %get-tuple-element.25), channel_id=1, source_target_pairs={{4,0},{8,4},{12,8},{14,12},{10,14},{6,10},{2,6},{0,2},{5,1},{9,5},... | collective-permute-start | bytes 417800 | tf_op jit(solution)/shard_map/ppermute | solution.py:48
  92.3 3.0 %collective-permute-done.19 = bf16[32,2176]{1,0:T(8,128)(2,1)S(1)} collective-permute-done((bf16[32,2176]{1,0:T(8,128)(2,1)S(1)}, bf16[32,2176]{1,0:T(8,128)(2,1)S(1)}, u32[]{:S(2)}, u32[]{:S(2)}) %collective-permute-start.19) | collective-permute-done | bytes 139296 | tf_op jit(solution)/shard_map/ppermute | solution.py:45
  95.6 1.7 %collective-permute-start.20 = (bf16[32,2176]{1,0:T(8,128)(2,1)S(1)}, bf16[32,2176]{1,0:T(8,128)(2,1)S(1)}, u32[]{:S(2)}, u32[]{:S(2)}) collective-permute-start(bf16[32,2176]{1,0:T(8,128)(2,1)S(1)} %collective-permute-done.18.refs_1_), channel_id=1, source_target_pairs={{4,0},{8,4},{12,8},{14,12},{10,14},{6,10},{2,6},{0,2},{5,1},{9,5},... | collective-permute-start | bytes 417800 | tf_op jit(solution)/shard_map/ppermute | solution.py:48
  97.4 2.8 %copy-done.2 = bf16[1,2048,1536]{2,1,0:T(8,128)(2,1)S(1)} copy-done((bf16[1,2048,1536]{2,1,0:T(8,128)(2,1)S(1)}, bf16[1,2048,1536]{2,1,0:T(8,128)(2,1)}, u32[]{:S(2)}) %copy-start.2) | copy-done | bytes 6291480
  100.1 0.4 load_gate_up.2.refs_0_
  101.0 1.7 %collective-permute-start.22 = (bf16[32,2176]{1,0:T(8,128)(2,1)S(1)}, bf16[32,2176]{1,0:T(8,128)(2,1)S(1)}, u32[]{:S(2)}, u32[]{:S(2)}) collective-permute-start(bf16[32,2176]{1,0:T(8,128)(2,1)S(1)} %collective-permute-done.20.refs_1_), channel_id=1, source_target_pairs={{4,0},{8,4},{12,8},{14,12},{10,14},{6,10},{2,6},{0,2},{5,1},{9,5},... | collective-permute-start | bytes 417800 | tf_op jit(solution)/shard_map/ppermute | solution.py:48
  102.7 2.9 %load_gate_up.3.refs_1_ = bf16[2048,1536]{1,0:T(8,128)(2,1)S(1)} custom-call(bf16[2048,1536]{1,0:T(8,128)(2,1)} %collective-permute-done.8.refs_1_.refs_0_, bf16[32,2176]{1,0:T(8,128)(2,1)S(1)} %collective-permute-done.20.refs_1_), custom_call_target="tpu_custom_call" | custom-call | bytes 104857600 | tf_op jit(solution)/shard_map/load_gate_up/pallas_call | solution.py:97
  106.1 2.0 %collective-permute-start.25 = (bf16[16,2176]{1,0:T(8,128)(2,1)S(1)}, bf16[16,2176]{1,0:T(8,128)(2,1)S(1)}, u32[]{:S(2)}, u32[]{:S(2)}) collective-permute-start(bf16[16,2176]{1,0:T(8,128)(2,1)S(1)} %slice.107), channel_id=1, source_target_pairs={{4,0},{8,4},{12,8},{14,12},{10,14},{6,10},{2,6},{0,2},{5,1},{9,5},... | collective-permute-start | bytes 208904 | tf_op jit(solution)/shard_map/ppermute | solution.py:48
  108.2 0.4 load_downs.1
  108.6 2.1 %collective-permute-done.24 = bf16[16,2176]{1,0:T(8,128)(2,1)S(1)} collective-permute-done((bf16[16,2176]{1,0:T(8,128)(2,1)S(1)}, bf16[16,2176]{1,0:T(8,128)(2,1)S(1)}, u32[]{:S(2)}, u32[]{:S(2)}) %collective-permute-start.24) | collective-permute-done | bytes 69664 | tf_op jit(solution)/shard_map/ppermute | solution.py:45
  110.7 0.6 collective-permute-done.25
  111.3 5.7 %experts.1 = (f32[32,2048]{1,0:T(8,128)S(1)}, bf16[32,1024]{1,0:T(8,128)(2,1)S(1)}, bf16[32,1024]{1,0:T(8,128)(2,1)S(1)}, f32[3,32,2048]{2,1,0:T(8,128)S(1)}, f32[3,32,2048]{2,1,0:T(8,128)S(1)}) custom-call(s32[1,2]{1,0:T(1,128)S(1)} %fusion.15.slot_ref, bf16[256,2176]{1,0:T(8,128)(2,1)S(1)} %constant_dynamic-update-slice_fusion.9.held, ...), custom_call_target="tpu_custom_call" | custom-call | bytes 104857600 | tf_op jit(solution)/shard_map/experts/pallas_call | solution.py:97
  117.0 1.1 collective-permute-start.26
  118.2 1.0 collective-permute-start.30
  119.2 2.2 %collective-permute-done.26 = bf16[32,1024]{1,0:T(8,128)(2,1)S(1)} collective-permute-done((bf16[32,1024]{1,0:T(8,128)(2,1)S(1)}, bf16[32,1024]{1,0:T(8,128)(2,1)S(1)}, u32[]{:S(2)}, u32[]{:S(2)}) %collective-permute-start.26) | collective-permute-done | bytes 65568 | tf_op jit(solution)/shard_map/ppermute | solution.py:45
  121.4 1.1 collective-permute-start.27
  122.6 1.0 collective-permute-start.31
  123.6 2.8 %collective-permute-done.27 = bf16[32,2048]{1,0:T(8,128)(2,1)S(1)} collective-permute-done((bf16[32,2048]{1,0:T(8,128)(2,1)S(1)}, bf16[32,2048]{1,0:T(8,128)(2,1)S(1)}, u32[]{:S(2)}, u32[]{:S(2)}) %collective-permute-start.27) | collective-permute-done | bytes 131104 | tf_op jit(solution)/shard_map/ppermute | solution.py:45
  126.4 1.1 collective-permute-start.28
  127.6 1.0 collective-permute-start.32
  128.6 2.8 %collective-permute-done.28 = bf16[32,2048]{1,0:T(8,128)(2,1)S(1)} collective-permute-done((bf16[32,2048]{1,0:T(8,128)(2,1)S(1)}, bf16[32,2048]{1,0:T(8,128)(2,1)S(1)}, u32[]{:S(2)}, u32[]{:S(2)}) %collective-permute-start.28) | collective-permute-done | bytes 131104 | tf_op jit(solution)/shard_map/ppermute | solution.py:45
  131.5 1.1 collective-permute-start.29
  132.7 1.0 collective-permute-start.33
  133.7 2.8 %collective-permute-done.29 = bf16[32,2048]{1,0:T(8,128)(2,1)S(1)} collective-permute-done((bf16[32,2048]{1,0:T(8,128)(2,1)S(1)}, bf16[32,2048]{1,0:T(8,128)(2,1)S(1)}, u32[]{:S(2)}, u32[]{:S(2)}) %collective-permute-start.29) | collective-permute-done | bytes 131104 | tf_op jit(solution)/shard_map/ppermute | solution.py:45
  136.5 1.2 collective-permute-done.33
  137.7 0.7 add_convert_fusion
  (108 shorter events, 3.7 us)
Async XLA Ops:
  0.0 40.2 %collective-permute-start.8 = (bf16[2048,1536]{1,0:T(8,128)(2,1)}, bf16[2048,1536]{1,0:T(8,128)(2,1)}, u32[]{:S(2)}, u32[]{:S(2)}) collective-permute-start(bf16[2048,1536]{1,0:T(8,128)(2,1)} %bitcast.49), channel_id=1, source_target_pairs={{0,1},{1,0},{2,3},{3,2},{4,5},{5,4},{6,7},{7,6},{8,9},{9,8},{10,11... | collective-permute-start | bytes 18874376 | tf_op jit(solution)/shard_map/ppermute | solution.py:436
  0.5 39.7 %collective-permute-start.9 = (bf16[768,2048]{1,0:T(8,128)(2,1)}, bf16[768,2048]{1,0:T(8,128)(2,1)S(1)}, u32[]{:S(2)}, u32[]{:S(2)}) collective-permute-start(bf16[768,2048]{1,0:T(8,128)(2,1)} %bitcast.51), channel_id=1, source_target_pairs={{0,1},{1,0},{2,3},{3,2},{4,5},{5,4},{6,7},{7,6},{8,9},{9,8},{10,11... | collective-permute-start | bytes 9437192 | tf_op jit(solution)/shard_map/ppermute | solution.py:437
  0.5 6.8 %collective-permute-start.1 = (bf16[32,2048]{1,0:T(8,128)(2,1)}, bf16[32,2048]{1,0:T(8,128)(2,1)S(1)}, u32[]{:S(2)}, u32[]{:S(2)}) collective-permute-start(bf16[32,2048]{1,0:T(8,128)(2,1)} %hidden_ref.1), channel_id=1, source_target_pairs={{0,4},{4,8},{8,12},{12,14},{14,10},{10,6},{6,2},{2,0},{1,5},{5,9},... | collective-permute-start | bytes 393224 | tf_op jit(solution)/shard_map/ppermute | solution.py:45
  3.5 5.6 %collective-permute-start = (bf16[32,2048]{1,0:T(8,128)(2,1)}, bf16[32,2048]{1,0:T(8,128)(2,1)S(1)}, u32[]{:S(2)}, u32[]{:S(2)}) collective-permute-start(bf16[32,2048]{1,0:T(8,128)(2,1)} %hidden_ref.1), channel_id=1, source_target_pairs={{4,0},{8,4},{12,8},{14,12},{10,14},{6,10},{2,6},{0,2},{5,1},{9,5},... | collective-permute-start | bytes 393224 | tf_op jit(solution)/shard_map/ppermute | solution.py:48
  5.2 6.0 %copy-start.6 = (bf16[256,2048]{1,0:T(8,128)(2,1)S(1)}, bf16[256,2048]{1,0:T(8,128)(2,1)}, u32[]{:S(2)}) copy-start(bf16[256,2048]{1,0:T(8,128)(2,1)} %constant_dynamic-update-slice_fusion.8) | copy-start | bytes 3145732
  7.4 5.0 %collective-permute-start.3 = (bf16[32,2048]{1,0:T(8,128)(2,1)S(1)}, bf16[32,2048]{1,0:T(8,128)(2,1)S(1)}, u32[]{:S(2)}, u32[]{:S(2)}) collective-permute-start(bf16[32,2048]{1,0:T(8,128)(2,1)S(1)} %collective-permute-done.1), channel_id=1, source_target_pairs={{0,4},{4,8},{8,12},{12,14},{14,10},{10,6},{6,2},{2,0},{1,5},{5,9},... | collective-permute-start | bytes 393224 | tf_op jit(solution)/shard_map/ppermute | solution.py:45
  9.2 5.0 %collective-permute-start.2 = (bf16[32,2048]{1,0:T(8,128)(2,1)S(1)}, bf16[32,2048]{1,0:T(8,128)(2,1)S(1)}, u32[]{:S(2)}, u32[]{:S(2)}) collective-permute-start(bf16[32,2048]{1,0:T(8,128)(2,1)S(1)} %collective-permute-done.refs_1_), channel_id=1, source_target_pairs={{4,0},{8,4},{12,8},{14,12},{10,14},{6,10},{2,6},{0,2},{5,1},{9,5},... | collective-permute-start | bytes 393224 | tf_op jit(solution)/shard_map/ppermute | solution.py:48
  11.1 12.9 %copy-start.11 = (f32[2048]{0:T(1024)S(1)}, f32[2048]{0:T(1024)}, u32[]{:S(2)}) copy-start(f32[2048]{0:T(1024)} %param.22) | copy-start | bytes 24580
  12.3 5.2 %collective-permute-start.5 = (bf16[32,2048]{1,0:T(8,128)(2,1)S(1)}, bf16[32,2048]{1,0:T(8,128)(2,1)S(1)}, u32[]{:S(2)}, u32[]{:S(2)}) collective-permute-start(bf16[32,2048]{1,0:T(8,128)(2,1)S(1)} %collective-permute-done.3), channel_id=1, source_target_pairs={{0,4},{4,8},{8,12},{12,14},{14,10},{10,6},{6,2},{2,0},{1,5},{5,9},... | collective-permute-start | bytes 393224 | tf_op jit(solution)/shard_map/ppermute | solution.py:45
  14.1 5.5 %collective-permute-start.4 = (bf16[32,2048]{1,0:T(8,128)(2,1)S(1)}, bf16[32,2048]{1,0:T(8,128)(2,1)S(1)}, u32[]{:S(2)}, u32[]{:S(2)}) collective-permute-start(bf16[32,2048]{1,0:T(8,128)(2,1)S(1)} %collective-permute-done.2), channel_id=1, source_target_pairs={{4,0},{8,4},{12,8},{14,12},{10,14},{6,10},{2,6},{0,2},{5,1},{9,5},... | collective-permute-start | bytes 393224 | tf_op jit(solution)/shard_map/ppermute | solution.py:48
  17.5 4.3 %collective-permute-start.6 = (bf16[16,2048]{1,0:T(8,128)(2,1)S(1)}, bf16[16,2048]{1,0:T(8,128)(2,1)S(1)}, u32[]{:S(2)}, u32[]{:S(2)}) collective-permute-start(bf16[16,2048]{1,0:T(8,128)(2,1)S(1)} %slice.100), channel_id=1, source_target_pairs={{0,4},{4,8},{8,12},{12,14},{14,10},{10,6},{6,2},{2,0},{1,5},{5,9},... | collective-permute-start | bytes 196616 | tf_op jit(solution)/shard_map/ppermute | solution.py:45
  19.7 4.3 %collective-permute-start.7 = (bf16[16,2048]{1,0:T(8,128)(2,1)S(1)}, bf16[16,2048]{1,0:T(8,128)(2,1)S(1)}, u32[]{:S(2)}, u32[]{:S(2)}) collective-permute-start(bf16[16,2048]{1,0:T(8,128)(2,1)S(1)} %slice.101), channel_id=1, source_target_pairs={{4,0},{8,4},{12,8},{14,12},{10,14},{6,10},{2,6},{0,2},{5,1},{9,5},... | collective-permute-start | bytes 196616 | tf_op jit(solution)/shard_map/ppermute | solution.py:48
  24.0 7.4 %copy-start.13 = (s32[32,8]{0,1:T(8,128)S(1)}, s32[32,8]{0,1:T(8,128)}, u32[]{:S(2)}) copy-start(s32[32,8]{0,1:T(8,128)} %param.19) | copy-start | bytes 3076
  24.0 7.4 %copy-start.14 = (s32[32,8]{0,1:T(8,128)S(1)}, s32[32,8]{0,1:T(8,128)}, u32[]{:S(2)}) copy-start(s32[32,8]{0,1:T(8,128)} %param.20) | copy-start | bytes 3076
  24.0 7.5 %copy-start.10 = (s32[16]{0:T(128)S(1)}, s32[16]{0:T(128)}, u32[]{:S(2)}) copy-start(s32[16]{0:T(128)} %param.21) | copy-start | bytes 196
  24.1 8.9 %copy-start.15 = (s32[1,32]{1,0:T(1,128)S(1)}, s32[1,32]{1,0:T(1,128)}, u32[]{:S(2)}) copy-start(s32[1,32]{1,0:T(1,128)} %length_ref.1) | copy-start | bytes 388
  26.6 13.6 %all-to-all-start = ((bf16[8,32,640]{2,1,0:T(8,128)(2,1)}), bf16[8,32,640]{2,1,0:T(8,128)(2,1)}, u32[]{:S(2)}, u32[]{:S(2)}) async-start(bf16[8,32,640]{2,1,0:T(8,128)(2,1)} %project.1), calls=%async_computation | async-start | bytes 655360 | tf_op jit(solution)/shard_map/all_to_all | solution.py:463
  32.3 0.6 copy-start.8
  40.2 1.7 %copy-start = (bf16[768,2048]{1,0:T(8,128)(2,1)}, bf16[768,2048]{1,0:T(8,128)(2,1)S(1)}, u32[]{:S(2)}) copy-start(bf16[768,2048]{1,0:T(8,128)(2,1)S(1)} %collective-permute-done.9.refs_2_.refs_1_) | copy-start | bytes 9437188
  53.4 11.6 %all-to-all-start.1 = ((bf16[8,32,512]{2,1,0:T(8,128)(2,1)}), bf16[8,32,512]{2,1,0:T(8,128)(2,1)S(1)}, u32[]{:S(2)}, u32[]{:S(2)}) async-start(bf16[8,32,512]{2,1,0:T(8,128)(2,1)} %ragged_attention.1.refs_1_), calls=%async_computation.1 | async-start | bytes 524288 | tf_op jit(solution)/shard_map/all_to_all | solution.py:469
  56.8 1.0 copy-start.4
  57.8 1.6 %copy-start.5 = (bf16[512,2048]{1,0:T(8,128)(2,1)S(1)}, bf16[512,2048]{1,0:T(8,128)(2,1)}, u32[]{:S(2)}) copy-start(bf16[512,2048]{1,0:T(8,128)(2,1)} %refs_0_.3) | copy-start | bytes 6291460
  66.2 4.7 %collective-permute-start.10 = (bf16[32,1024]{1,0:T(8,128)(2,1)S(1)}, bf16[32,1024]{1,0:T(8,128)(2,1)S(1)}, u32[]{:S(2)}, u32[]{:S(2)}) collective-permute-start(bf16[32,1024]{1,0:T(8,128)(2,1)S(1)} %get-tuple-element.21), channel_id=1, source_target_pairs={{0,4},{4,8},{8,12},{12,14},{14,10},{10,6},{6,2},{2,0},{1,5},{5,9},... | collective-permute-start | bytes 196616 | tf_op jit(solution)/shard_map/ppermute | solution.py:45
  67.3 5.0 %collective-permute-start.14 = (bf16[32,1024]{1,0:T(8,128)(2,1)S(1)}, bf16[32,1024]{1,0:T(8,128)(2,1)S(1)}, u32[]{:S(2)}, u32[]{:S(2)}) collective-permute-start(bf16[32,1024]{1,0:T(8,128)(2,1)S(1)} %get-tuple-element.23), channel_id=1, source_target_pairs={{4,0},{8,4},{12,8},{14,12},{10,14},{6,10},{2,6},{0,2},{5,1},{9,5},... | collective-permute-start | bytes 196616 | tf_op jit(solution)/shard_map/ppermute | solution.py:48
  71.0 6.3 %collective-permute-start.11 = (bf16[32,2048]{1,0:T(8,128)(2,1)S(1)}, bf16[32,2048]{1,0:T(8,128)(2,1)S(1)}, u32[]{:S(2)}, u32[]{:S(2)}) collective-permute-start(bf16[32,2048]{1,0:T(8,128)(2,1)S(1)} %pad_maximum_fusion), channel_id=1, source_target_pairs={{0,4},{4,8},{8,12},{12,14},{14,10},{10,6},{6,2},{2,0},{1,5},{5,9},... | collective-permute-start | bytes 393224 | tf_op jit(solution)/shard_map/ppermute | solution.py:45
  72.4 17.6 %copy-start.12 = (f32[2048]{0:T(1024)S(1)}, f32[2048]{0:T(1024)}, u32[]{:S(2)}) copy-start(f32[2048]{0:T(1024)} %param.23) | copy-start | bytes 24580
  72.4 17.6 %copy-start.7 = (bf16[32,2048]{1,0:T(8,128)(2,1)S(1)}, bf16[32,2048]{1,0:T(8,128)(2,1)}, u32[]{:S(2)}) copy-start(bf16[32,2048]{1,0:T(8,128)(2,1)} %hidden_ref.1) | copy-start | bytes 393220
  72.4 17.6 %copy-start.9 = (bf16[32,128]{1,0:T(8,128)(2,1)S(1)}, bf16[32,128]{1,0:T(8,128)(2,1)}, u32[]{:S(2)}) copy-start(bf16[32,128]{1,0:T(8,128)(2,1)} %copy-done.8) | copy-start | bytes 24580
  72.4 5.8 %collective-permute-start.15 = (bf16[32,2048]{1,0:T(8,128)(2,1)S(1)}, bf16[32,2048]{1,0:T(8,128)(2,1)S(1)}, u32[]{:S(2)}, u32[]{:S(2)}) collective-permute-start(bf16[32,2048]{1,0:T(8,128)(2,1)S(1)} %pad_maximum_fusion.1), channel_id=1, source_target_pairs={{4,0},{8,4},{12,8},{14,12},{10,14},{6,10},{2,6},{0,2},{5,1},{9,5},... | collective-permute-start | bytes 393224 | tf_op jit(solution)/shard_map/ppermute | solution.py:48
  77.3 6.0 %collective-permute-start.12 = (bf16[32,2048]{1,0:T(8,128)(2,1)S(1)}, bf16[32,2048]{1,0:T(8,128)(2,1)S(1)}, u32[]{:S(2)}, u32[]{:S(2)}) collective-permute-start(bf16[32,2048]{1,0:T(8,128)(2,1)S(1)} %fusion.6), channel_id=1, source_target_pairs={{0,4},{4,8},{8,12},{12,14},{14,10},{10,6},{6,2},{2,0},{1,5},{5,9},... | collective-permute-start | bytes 393224 | tf_op jit(solution)/shard_map/ppermute | solution.py:45
  78.2 6.4 %collective-permute-start.16 = (bf16[32,2048]{1,0:T(8,128)(2,1)S(1)}, bf16[32,2048]{1,0:T(8,128)(2,1)S(1)}, u32[]{:S(2)}, u32[]{:S(2)}) collective-permute-start(bf16[32,2048]{1,0:T(8,128)(2,1)S(1)} %fusion.4), channel_id=1, source_target_pairs={{4,0},{8,4},{12,8},{14,12},{10,14},{6,10},{2,6},{0,2},{5,1},{9,5},... | collective-permute-start | bytes 393224 | tf_op jit(solution)/shard_map/ppermute | solution.py:48
  83.3 5.2 %collective-permute-start.13 = (bf16[32,2048]{1,0:T(8,128)(2,1)S(1)}, bf16[32,2048]{1,0:T(8,128)(2,1)S(1)}, u32[]{:S(2)}, u32[]{:S(2)}) collective-permute-start(bf16[32,2048]{1,0:T(8,128)(2,1)S(1)} %fusion.7), channel_id=1, source_target_pairs={{0,4},{4,8},{8,12},{12,14},{14,10},{10,6},{6,2},{2,0},{1,5},{5,9},... | collective-permute-start | bytes 393224 | tf_op jit(solution)/shard_map/ppermute | solution.py:45
  84.6 5.3 %collective-permute-start.17 = (bf16[32,2048]{1,0:T(8,128)(2,1)S(1)}, bf16[32,2048]{1,0:T(8,128)(2,1)S(1)}, u32[]{:S(2)}, u32[]{:S(2)}) collective-permute-start(bf16[32,2048]{1,0:T(8,128)(2,1)S(1)} %fusion.5), channel_id=1, source_target_pairs={{4,0},{8,4},{12,8},{14,12},{10,14},{6,10},{2,6},{0,2},{5,1},{9,5},... | collective-permute-start | bytes 393224 | tf_op jit(solution)/shard_map/ppermute | solution.py:48
  90.2 5.1 %collective-permute-start.19 = (bf16[32,2176]{1,0:T(8,128)(2,1)S(1)}, bf16[32,2176]{1,0:T(8,128)(2,1)S(1)}, u32[]{:S(2)}, u32[]{:S(2)}) collective-permute-start(bf16[32,2176]{1,0:T(8,128)(2,1)S(1)} %get-tuple-element.25), channel_id=1, source_target_pairs={{0,4},{4,8},{8,12},{12,14},{14,10},{10,6},{6,2},{2,0},{1,5},{5,9},... | collective-permute-start | bytes 417800 | tf_op jit(solution)/shard_map/ppermute | solution.py:45
  90.6 5.1 %collective-permute-start.18 = (bf16[32,2176]{1,0:T(8,128)(2,1)S(1)}, bf16[32,2176]{1,0:T(8,128)(2,1)S(1)}, u32[]{:S(2)}, u32[]{:S(2)}) collective-permute-start(bf16[32,2176]{1,0:T(8,128)(2,1)S(1)} %get-tuple-element.25), channel_id=1, source_target_pairs={{4,0},{8,4},{12,8},{14,12},{10,14},{6,10},{2,6},{0,2},{5,1},{9,5},... | collective-permute-start | bytes 417800 | tf_op jit(solution)/shard_map/ppermute | solution.py:48
  95.3 5.3 %collective-permute-start.21 = (bf16[32,2176]{1,0:T(8,128)(2,1)S(1)}, bf16[32,2176]{1,0:T(8,128)(2,1)S(1)}, u32[]{:S(2)}, u32[]{:S(2)}) collective-permute-start(bf16[32,2176]{1,0:T(8,128)(2,1)S(1)} %collective-permute-done.19), channel_id=1, source_target_pairs={{0,4},{4,8},{8,12},{12,14},{14,10},{10,6},{6,2},{2,0},{1,5},{5,9},... | collective-permute-start | bytes 417800 | tf_op jit(solution)/shard_map/ppermute | solution.py:45
  95.6 5.4 %collective-permute-start.20 = (bf16[32,2176]{1,0:T(8,128)(2,1)S(1)}, bf16[32,2176]{1,0:T(8,128)(2,1)S(1)}, u32[]{:S(2)}, u32[]{:S(2)}) collective-permute-start(bf16[32,2176]{1,0:T(8,128)(2,1)S(1)} %collective-permute-done.18.refs_1_), channel_id=1, source_target_pairs={{4,0},{8,4},{12,8},{14,12},{10,14},{6,10},{2,6},{0,2},{5,1},{9,5},... | collective-permute-start | bytes 417800 | tf_op jit(solution)/shard_map/ppermute | solution.py:48
  97.3 2.8 %copy-start.2 = (bf16[1,2048,1536]{2,1,0:T(8,128)(2,1)S(1)}, bf16[1,2048,1536]{2,1,0:T(8,128)(2,1)}, u32[]{:S(2)}) copy-start(bf16[1,2048,1536]{2,1,0:T(8,128)(2,1)} %param.28) | copy-start | bytes 18874372
  100.6 5.1 %collective-permute-start.23 = (bf16[32,2176]{1,0:T(8,128)(2,1)S(1)}, bf16[32,2176]{1,0:T(8,128)(2,1)S(1)}, u32[]{:S(2)}, u32[]{:S(2)}) collective-permute-start(bf16[32,2176]{1,0:T(8,128)(2,1)S(1)} %collective-permute-done.21), channel_id=1, source_target_pairs={{0,4},{4,8},{8,12},{12,14},{14,10},{10,6},{6,2},{2,0},{1,5},{5,9},... | collective-permute-start | bytes 417800 | tf_op jit(solution)/shard_map/ppermute | solution.py:45
  101.0 5.1 %collective-permute-start.22 = (bf16[32,2176]{1,0:T(8,128)(2,1)S(1)}, bf16[32,2176]{1,0:T(8,128)(2,1)S(1)}, u32[]{:S(2)}, u32[]{:S(2)}) collective-permute-start(bf16[32,2176]{1,0:T(8,128)(2,1)S(1)} %collective-permute-done.20.refs_1_), channel_id=1, source_target_pairs={{4,0},{8,4},{12,8},{14,12},{10,14},{6,10},{2,6},{0,2},{5,1},{9,5},... | collective-permute-start | bytes 417800 | tf_op jit(solution)/shard_map/ppermute | solution.py:48
  102.7 5.4 %copy-start.1 = (bf16[768,2048]{1,0:T(8,128)(2,1)S(1)}, bf16[768,2048]{1,0:T(8,128)(2,1)}, u32[]{:S(2)}) copy-start(bf16[768,2048]{1,0:T(8,128)(2,1)} %copy-done) | copy-start | bytes 9437188
  102.7 5.4 %copy-start.3 = (bf16[1,768,2048]{2,1,0:T(8,128)(2,1)S(1)}, bf16[1,768,2048]{2,1,0:T(8,128)(2,1)}, u32[]{:S(2)}) copy-start(bf16[1,768,2048]{2,1,0:T(8,128)(2,1)} %param.29) | copy-start | bytes 9437188
  105.7 5.0 %collective-permute-start.24 = (bf16[16,2176]{1,0:T(8,128)(2,1)S(1)}, bf16[16,2176]{1,0:T(8,128)(2,1)S(1)}, u32[]{:S(2)}, u32[]{:S(2)}) collective-permute-start(bf16[16,2176]{1,0:T(8,128)(2,1)S(1)} %slice.106), channel_id=1, source_target_pairs={{0,4},{4,8},{8,12},{12,14},{14,10},{10,6},{6,2},{2,0},{1,5},{5,9},... | collective-permute-start | bytes 208904 | tf_op jit(solution)/shard_map/ppermute | solution.py:45
  106.1 5.2 %collective-permute-start.25 = (bf16[16,2176]{1,0:T(8,128)(2,1)S(1)}, bf16[16,2176]{1,0:T(8,128)(2,1)S(1)}, u32[]{:S(2)}, u32[]{:S(2)}) collective-permute-start(bf16[16,2176]{1,0:T(8,128)(2,1)S(1)} %slice.107), channel_id=1, source_target_pairs={{4,0},{8,4},{12,8},{14,12},{10,14},{6,10},{2,6},{0,2},{5,1},{9,5},... | collective-permute-start | bytes 208904 | tf_op jit(solution)/shard_map/ppermute | solution.py:48
  117.0 4.3 %collective-permute-start.26 = (bf16[32,1024]{1,0:T(8,128)(2,1)S(1)}, bf16[32,1024]{1,0:T(8,128)(2,1)S(1)}, u32[]{:S(2)}, u32[]{:S(2)}) collective-permute-start(bf16[32,1024]{1,0:T(8,128)(2,1)S(1)} %get-tuple-element.30), channel_id=1, source_target_pairs={{0,4},{4,8},{8,12},{12,14},{14,10},{10,6},{6,2},{2,0},{1,5},{5,9},... | collective-permute-start | bytes 196616 | tf_op jit(solution)/shard_map/ppermute | solution.py:45
  118.2 4.4 %collective-permute-start.30 = (bf16[32,1024]{1,0:T(8,128)(2,1)S(1)}, bf16[32,1024]{1,0:T(8,128)(2,1)S(1)}, u32[]{:S(2)}, u32[]{:S(2)}) collective-permute-start(bf16[32,1024]{1,0:T(8,128)(2,1)S(1)} %get-tuple-element.32), channel_id=1, source_target_pairs={{4,0},{8,4},{12,8},{14,12},{10,14},{6,10},{2,6},{0,2},{5,1},{9,5},... | collective-permute-start | bytes 196616 | tf_op jit(solution)/shard_map/ppermute | solution.py:48
  121.4 5.0 %collective-permute-start.27 = (bf16[32,2048]{1,0:T(8,128)(2,1)S(1)}, bf16[32,2048]{1,0:T(8,128)(2,1)S(1)}, u32[]{:S(2)}, u32[]{:S(2)}) collective-permute-start(bf16[32,2048]{1,0:T(8,128)(2,1)S(1)} %pad_maximum_fusion.2), channel_id=1, source_target_pairs={{0,4},{4,8},{8,12},{12,14},{14,10},{10,6},{6,2},{2,0},{1,5},{5,9},... | collective-permute-start | bytes 393224 | tf_op jit(solution)/shard_map/ppermute | solution.py:45
  122.6 5.0 %collective-permute-start.31 = (bf16[32,2048]{1,0:T(8,128)(2,1)S(1)}, bf16[32,2048]{1,0:T(8,128)(2,1)S(1)}, u32[]{:S(2)}, u32[]{:S(2)}) collective-permute-start(bf16[32,2048]{1,0:T(8,128)(2,1)S(1)} %pad_maximum_fusion.3), channel_id=1, source_target_pairs={{4,0},{8,4},{12,8},{14,12},{10,14},{6,10},{2,6},{0,2},{5,1},{9,5},... | collective-permute-start | bytes 393224 | tf_op jit(solution)/shard_map/ppermute | solution.py:48
  126.4 5.0 %collective-permute-start.28 = (bf16[32,2048]{1,0:T(8,128)(2,1)S(1)}, bf16[32,2048]{1,0:T(8,128)(2,1)S(1)}, u32[]{:S(2)}, u32[]{:S(2)}) collective-permute-start(bf16[32,2048]{1,0:T(8,128)(2,1)S(1)} %fusion.2), channel_id=1, source_target_pairs={{0,4},{4,8},{8,12},{12,14},{14,10},{10,6},{6,2},{2,0},{1,5},{5,9},... | collective-permute-start | bytes 393224 | tf_op jit(solution)/shard_map/ppermute | solution.py:45
  127.6 5.0 %collective-permute-start.32 = (bf16[32,2048]{1,0:T(8,128)(2,1)S(1)}, bf16[32,2048]{1,0:T(8,128)(2,1)S(1)}, u32[]{:S(2)}, u32[]{:S(2)}) collective-permute-start(bf16[32,2048]{1,0:T(8,128)(2,1)S(1)} %fusion), channel_id=1, source_target_pairs={{4,0},{8,4},{12,8},{14,12},{10,14},{6,10},{2,6},{0,2},{5,1},{9,5},... | collective-permute-start | bytes 393224 | tf_op jit(solution)/shard_map/ppermute | solution.py:48
  131.5 5.0 %collective-permute-start.29 = (bf16[32,2048]{1,0:T(8,128)(2,1)S(1)}, bf16[32,2048]{1,0:T(8,128)(2,1)S(1)}, u32[]{:S(2)}, u32[]{:S(2)}) collective-permute-start(bf16[32,2048]{1,0:T(8,128)(2,1)S(1)} %fusion.3), channel_id=1, source_target_pairs={{0,4},{4,8},{8,12},{12,14},{14,10},{10,6},{6,2},{2,0},{1,5},{5,9},... | collective-permute-start | bytes 393224 | tf_op jit(solution)/shard_map/ppermute | solution.py:45
  132.7 5.0 %collective-permute-start.33 = (bf16[32,2048]{1,0:T(8,128)(2,1)S(1)}, bf16[32,2048]{1,0:T(8,128)(2,1)S(1)}, u32[]{:S(2)}, u32[]{:S(2)}) collective-permute-start(bf16[32,2048]{1,0:T(8,128)(2,1)S(1)} %fusion.1), channel_id=1, source_target_pairs={{4,0},{8,4},{12,8},{14,12},{10,14},{6,10},{2,6},{0,2},{5,1},{9,5},... | collective-permute-start | bytes 393224 | tf_op jit(solution)/shard_map/ppermute | solution.py:48

commit v3 on v2

--- a/solution.py
+++ b/solution.py
@@ -86,7 +86,9 @@
         else:
             up, down = mine_up + up, mine_down + down
         up, down = ring.ahead(up.astype(sent)), ring.behind(down.astype(sent))
-    return up, down
+        if distance == 2:
+            early = up
+    return up, down, early
 
 
 def whole_blocks(kinds):
@@ -156,17 +158,30 @@
     )
 
 
-def project_kernel(count, owner_ref, hidden_ref, gain_ref, weight_ref, out_ref, held):
-    rows = hidden_ref.shape[0] // count
+def project(hidden_ref, gain_ref, weight_ref, held, rows):
     gain = gain_ref[:1, :]
-    for index in range(count):
-        at = slice(index * rows, (index + 1) * rows)
+    for start in range(0, hidden_ref.shape[0], rows):
+        at = slice(start, start + rows)
         values = hidden_ref[at, :].astype(jnp.float32)
         held[at, :] = norm_scale(values, gain).astype(jnp.bfloat16)
     product = jnp.dot(held[...], weight_ref[...], preferred_element_type=jnp.float32)
-    product = product.astype(jnp.bfloat16)
-    for index in range(count):
-        out_ref[owner_ref[0, index]] = product[index * rows : (index + 1) * rows]
+    return product.astype(jnp.bfloat16)
+
+
+def project_near_kernel(rows, hidden_ref, gain_ref, weight_ref, out_ref, held):
+    out_ref[...] = project(hidden_ref, gain_ref, weight_ref, held, rows)
+
+
+def project_kernel(count, owner_ref, near_ref, hidden_ref, gain_ref, weight_ref, *refs):
+    out_ref, held = refs[-2:]
+    rows = (near_ref.shape[0] + hidden_ref.shape[0]) // count
+    nearby = near_ref.shape[0] // rows
+    product = project(hidden_ref, gain_ref, weight_ref, held, rows)
+    for index in range(nearby):
+        out_ref[owner_ref[0, index]] = near_ref[index * rows : (index + 1) * rows, :]
+    for index in range(nearby, count):
+        at = (index - nearby) * rows
+        out_ref[owner_ref[0, index]] = product[at : at + rows]
 
 
 def output_kernel(count, owner_ref, feature_ref, weight_ref, *refs):
@@ -430,11 +445,13 @@
     rows, width = hidden.shape
     slots = expert_device.shape[0]
 
-    gate_ups, downs = [], []
-    for shift in range(1, subs):
-        swap = [(i, (i - shift) % subs) for i in range(subs)]
-        gate_ups.append(lax.ppermute(expert_gate_up[0], "sub", swap))
-        downs.append(lax.ppermute(expert_down[0], "sub", swap))
+    def swapped(values):
+        return [
+            lax.ppermute(values, "sub", [(i, (i - shift) % subs) for i in range(subs)])
+            for shift in range(1, subs)
+        ]
+
+    gate_ups = swapped(expert_gate_up[0])
 
     bf16 = jnp.bfloat16
     owners = ring.owners()
@@ -449,14 +466,26 @@
         "gate_digits",
     )
     columns = project_weight.shape[1]
-    gathered, pieces = ring_gather(ring, hidden)
+    _, pieces = ring_gather(ring, hidden)
     (project_weight,) = loaded([project_weight], pieces[1], 50, "load_project")
+    gain = tiled_gain(attention_gain)
+    nearby = max(1, count - 3)
+    near = call(
+        functools.partial(project_near_kernel, rows),
+        jax.ShapeDtypeStruct((nearby * rows, columns), bf16),
+        [VMEM] * 3,
+        (jnp.concatenate(pieces[:nearby], axis=0), gain, project_weight),
+        [pltpu.VMEM((nearby * rows, width), bf16)],
+        8,
+        "project_near",
+    )
+    late = jnp.concatenate(pieces[nearby:], axis=0)
     blocks = call(
         functools.partial(project_kernel, count),
         jax.ShapeDtypeStruct((count, rows, columns), bf16),
-        [SMEM, VMEM, VMEM, VMEM],
-        (owners, gathered, tiled_gain(attention_gain), project_weight),
-        [pltpu.VMEM((count * rows, width), bf16)],
+        [SMEM] + [VMEM] * 4,
+        (owners, near, late, gain, project_weight),
+        [pltpu.VMEM(late.shape, bf16)],
         8,
         "project",
     )
@@ -464,8 +493,10 @@
     if columns % HD:
         blocks = jnp.transpose(blocks, (1, 0, 2)).reshape(1, rows, -1)
     attention = attend(
-        blocks, lengths, query_gain, key_gain, key_cache[0], value_cache[0], count, [digits, *gate_ups, *downs]
-    )
+        blocks, lengths, query_gain, key_gain, key_cache[0], value_cache[0], count, [digits, *gate_ups]
+    )
+    down, attention = lax.optimization_barrier((expert_down[0], attention))
+    downs = swapped(down)
     features = lax.all_to_all(attention, "dev", split_axis=0, concat_axis=0, tiled=True)
     (output_weight,) = loaded([output_weight], attention, 44, "load_output")
     own, *partial = call(
@@ -477,7 +508,8 @@
         8,
         "output_projection",
     )
-    up, down = ring_scatter_sum(ring, *partial)
+    up, down, early = ring_scatter_sum(ring, *partial)
+    own_gate_up = loaded([expert_gate_up[0]], early, 4, "load_gate_up")
     residual, sent = call(
         residual_kernel,
         [
@@ -493,10 +525,11 @@
     shifts = jnp.arange(subs, dtype=jnp.int32)[None, :]
     own_slots = lax.axis_index("dev") * subs + (lax.axis_index("sub") + shifts) % subs
     gathered, pieces = ring_gather(ring, sent)
-    weights = []
-    for index, gate_up in enumerate([expert_gate_up[0]] + gate_ups):
+    weights = list(own_gate_up)
+    for index, gate_up in enumerate(gate_ups):
         weights += loaded([gate_up], pieces[2 * index + 1], 4, "load_gate_up")
-    weights += loaded([expert_down[0]] + downs, pieces[2 * subs + 1], 4, "load_downs")
+    weights += loaded([expert_down[0]], pieces[2 * subs - 1], 4, "load_down")
+    weights = [*weights, *downs]
     own, *partial = call(
         functools.partial(expert_kernel, count, slots),
         block_shapes(count, rows, width),
@@ -509,7 +542,7 @@
         18,
         "experts",
     )
-    up, down = ring_scatter_sum(ring, *partial)
+    up, down, _ = ring_scatter_sum(ring, *partial)
     return (residual + own + up + down).astype(bf16)
 
 

time: 139 us -> 137 us (0.986)
  local copies, waits for them, and re-layouts: 9.84 us -> 8.16 us
    ppermute x16, starting transfers between devices: 19.4 us -> 16.8 us  [ahead(): return lax.ppermute(values, 'dev', self.forward)]
    ppermute x16, starting transfers between devices: 15.4 us -> 17.2 us  [behind(): return lax.ppermute(values, 'dev', self.backward)]
    unnamed x50 -> x42, local copies, waits for them, and re-layouts: 9.68 us -> 7.99 us
    pallas_call x11 -> x12, Pallas kernels: 27.6 us -> 28.4 us  [call(): pl.pallas_call(body, out_shape=outs, in_specs=whole_blocks(ins), out_spec...]
  transfers between devices with their start and end apart: 36 -> 36, of which waited for: 20 -> 21; matrix products, arithmetic and copies ran while one was open for 2% -> 3% of each run, Pallas kernels for 6% -> 7%
where the time goes in v3:
time: 137 us
  waiting for transfers between devices  53.7 us (39%)
  starting transfers between devices  42.7 us (31%)
  Pallas kernels  28.4 us (21%)
  local copies, waits for them, and re-layouts  8.16 us (6%)
  other arithmetic  3.24 us (2%)
    ppermute x16, waiting for transfers between devices, ahead(): return lax.ppermute(values, 'dev', self.forward)  37.2 us
    pallas_call x12, Pallas kernels, call(): pl.pallas_call(body, out_shape=outs, in_specs=whole_blocks(ins), out_spec...  28.4 us
    ppermute x16, starting transfers between devices, behind(): return lax.ppermute(values, 'dev', self.backward)  17.2 us
    ppermute x16, starting transfers between devices, ahead(): return lax.ppermute(values, 'dev', self.forward)  16.8 us
    unnamed x42, local copies, waits for them, and re-layouts  7.99 us
    all_to_all x1, waiting for transfers between devices, on_device(): lax.all_to_all(blocks, 'dev', split_axis=0, concat_axis=0, tiled=True)  6.28 us
    all_to_all x1, waiting for transfers between devices, on_device(): lax.all_to_all(attention, 'dev', split_axis=0, concat_axis=0, tiled=True)  5.55 us
    all_to_all x1, starting transfers between devices, on_device(): lax.all_to_all(blocks, 'dev', split_axis=0, concat_axis=0, tiled=True)  4.82 us
  transfers between devices with their start and end apart: 36, of which 21 were waited for; matrix products, arithmetic and copies ran while one was open for 3% of the time, Pallas kernels for 7%

profile of v3, /device:TPU:0, one launch (start us, length us, event | category | flops | bytes accessed | tf_op | source)
XLA Modules:
  0.0 136.7 jit_solution(7913580338423730367)
XLA Ops:
  0.5 2.6 %collective-permute-start.1 = (bf16[32,2048]{1,0:T(8,128)(2,1)}, bf16[32,2048]{1,0:T(8,128)(2,1)S(1)}, u32[]{:S(2)}, u32[]{:S(2)}) collective-permute-start(bf16[32,2048]{1,0:T(8,128)(2,1)} %hidden_ref.1), channel_id=1, source_target_pairs={{0,4},{4,8},{8,12},{12,14},{14,10},{10,6},{6,2},{2,0},{1,5},{5,9},... | collective-permute-start | bytes 393224 | tf_op jit(solution)/shard_map/ppermute | solution.py:45
  3.0 1.0 constant_dynamic-update-slice_fusion.4
  4.1 3.3 %collective-permute-done.1 = bf16[32,2048]{1,0:T(8,128)(2,1)S(1)} collective-permute-done((bf16[32,2048]{1,0:T(8,128)(2,1)}, bf16[32,2048]{1,0:T(8,128)(2,1)S(1)}, u32[]{:S(2)}, u32[]{:S(2)}) %collective-permute-start.1) | collective-permute-done | bytes 131104 | tf_op jit(solution)/shard_map/ppermute | solution.py:45
  7.3 1.8 %collective-permute-start.3 = (bf16[32,2048]{1,0:T(8,128)(2,1)S(1)}, bf16[32,2048]{1,0:T(8,128)(2,1)S(1)}, u32[]{:S(2)}, u32[]{:S(2)}) collective-permute-start(bf16[32,2048]{1,0:T(8,128)(2,1)S(1)} %collective-permute-done.1), channel_id=1, source_target_pairs={{0,4},{4,8},{8,12},{12,14},{14,10},{10,6},{6,2},{2,0},{1,5},{5,9},... | collective-permute-start | bytes 393224 | tf_op jit(solution)/shard_map/ppermute | solution.py:45
  9.4 1.7 %load_project.1.weight_ref = bf16[2048,640]{1,0:T(8,128)(2,1)S(1)} custom-call(bf16[2048,640]{1,0:T(8,128)(2,1)} %refs_0_.2, bf16[32,2048]{1,0:T(8,128)(2,1)S(1)} %collective-permute-done.refs_1_), custom_call_target="tpu_custom_call" | custom-call | bytes 104857600 | tf_op jit(solution)/shard_map/load_project/pallas_call | solution.py:99
  11.2 1.5 %collective-permute-done.3 = bf16[32,2048]{1,0:T(8,128)(2,1)S(1)} collective-permute-done((bf16[32,2048]{1,0:T(8,128)(2,1)S(1)}, bf16[32,2048]{1,0:T(8,128)(2,1)S(1)}, u32[]{:S(2)}, u32[]{:S(2)}) %collective-permute-start.3) | collective-permute-done | bytes 131104 | tf_op jit(solution)/shard_map/ppermute | solution.py:45
  12.7 1.6 %collective-permute-start.5 = (bf16[32,2048]{1,0:T(8,128)(2,1)S(1)}, bf16[32,2048]{1,0:T(8,128)(2,1)S(1)}, u32[]{:S(2)}, u32[]{:S(2)}) collective-permute-start(bf16[32,2048]{1,0:T(8,128)(2,1)S(1)} %collective-permute-done.3), channel_id=1, source_target_pairs={{0,4},{4,8},{8,12},{12,14},{14,10},{10,6},{6,2},{2,0},{1,5},{5,9},... | collective-permute-start | bytes 393224 | tf_op jit(solution)/shard_map/ppermute | solution.py:45
  14.7 2.9 %collective-permute-done.5 = bf16[32,2048]{1,0:T(8,128)(2,1)S(1)} collective-permute-done((bf16[32,2048]{1,0:T(8,128)(2,1)S(1)}, bf16[32,2048]{1,0:T(8,128)(2,1)S(1)}, u32[]{:S(2)}, u32[]{:S(2)}) %collective-permute-start.5) | collective-permute-done | bytes 131104 | tf_op jit(solution)/shard_map/ppermute | solution.py:45
  17.7 1.6 %collective-permute-start.6 = (bf16[16,2048]{1,0:T(8,128)(2,1)S(1)}, bf16[16,2048]{1,0:T(8,128)(2,1)S(1)}, u32[]{:S(2)}, u32[]{:S(2)}) collective-permute-start(bf16[16,2048]{1,0:T(8,128)(2,1)S(1)} %slice.100), channel_id=1, source_target_pairs={{0,4},{4,8},{8,12},{12,14},{14,10},{10,6},{6,2},{2,0},{1,5},{5,9},... | collective-permute-start | bytes 196616 | tf_op jit(solution)/shard_map/ppermute | solution.py:45
  19.8 0.8 project_near.1.near_ref
  20.6 1.3 collective-permute-done.6
  21.9 1.7 %collective-permute-done.7 = bf16[16,2048]{1,0:T(8,128)(2,1)S(1)} collective-permute-done((bf16[16,2048]{1,0:T(8,128)(2,1)S(1)}, bf16[16,2048]{1,0:T(8,128)(2,1)S(1)}, u32[]{:S(2)}, u32[]{:S(2)}) %collective-permute-start.7) | collective-permute-done | bytes 65568 | tf_op jit(solution)/shard_map/ppermute | solution.py:48
  23.7 2.0 %project.1 = bf16[8,32,640]{2,1,0:T(8,128)(2,1)} custom-call(s32[1,8]{1,0:T(1,128)S(1)} %compare_select_fusion.4.owner_ref, bf16[160,640]{1,0:T(8,128)(2,1)S(1)} %project_near.1.near_ref, bf16[96,2048]{1,0:T(8,128)(2,1)S(1)} %pad_maximum_fusion.hidden_ref, f32[8,2048]{1,0:T(8,128)S(1)} %broadcast_in_dim.10.gain_ref, bf16[2048,640]{1,0:T(8,128)(2,1)S(1)} %load_project.1.weight_ref), custom_call_target="tpu_custom_call" | custom-call | bytes 104857600 | tf_op jit(solution)/shard_map/project/pallas_call | solution.py:99
  25.6 4.8 %all-to-all-start = ((bf16[8,32,640]{2,1,0:T(8,128)(2,1)}), bf16[8,32,640]{2,1,0:T(8,128)(2,1)S(1)}, u32[]{:S(2)}, u32[]{:S(2)}) async-start(bf16[8,32,640]{2,1,0:T(8,128)(2,1)} %project.1), calls=%async_computation | async-start | bytes 655360 | tf_op jit(solution)/shard_map/all_to_all | solution.py:492
  30.6 0.8 gate_digits.1.refs_0_.digit_ref
  31.4 0.6 copy-done.5
  32.1 0.7 pad_maximum_fusion.5
  32.8 6.3 %all-to-all-done.merged_ref = bf16[8,32,640]{2,1,0:T(8,128)(2,1)S(1)} async-done(((bf16[8,32,640]{2,1,0:T(8,128)(2,1)}), bf16[8,32,640]{2,1,0:T(8,128)(2,1)S(1)}, u32[]{:S(2)}, u32[]{:S(2)}) %all-to-all-start) | async-done | bytes 327712 | tf_op jit(solution)/shard_map/all_to_all | solution.py:492
  39.1 0.7 copy-done.8
  39.8 11.5 %ragged_attention.1.refs_1_ = bf16[8,32,512]{2,1,0:T(8,128)(2,1)} custom-call(s32[1,32]{1,0:T(1,128)} %length_ref.1, bf16[8,32,640]{2,1,0:T(8,128)(2,1)} %copy-done.8, f32[32,128]{1,0:T(8,128)} %get-tuple-element.36.cos_ref, f32[32,128]{1,0:T(8,128)} %get-tuple-element.37.sin_ref, f32[1,128]{1,0:T(1,128)} %bitcast.56, f32[1,128]{1,0:T(1,128)} %bitcast.57, ...), custom_call_target="tpu_custom_call" | custom-call | bytes 104857600 | tf_op jit(solution)/shard_map/ragged_attention/pallas_call | solution.py:99
  51.3 3.4 %all-to-all-start.1 = ((bf16[8,32,512]{2,1,0:T(8,128)(2,1)}), bf16[8,32,512]{2,1,0:T(8,128)(2,1)S(1)}, u32[]{:S(2)}, u32[]{:S(2)}) async-start(bf16[8,32,512]{2,1,0:T(8,128)(2,1)} %ragged_attention.1.refs_1_), calls=%async_computation.1 | async-start | bytes 524288 | tf_op jit(solution)/shard_map/all_to_all | solution.py:500
  54.8 1.0 copy-done.2
  55.7 1.6 %copy-done.3 = bf16[512,2048]{1,0:T(8,128)(2,1)S(1)} copy-done((bf16[512,2048]{1,0:T(8,128)(2,1)S(1)}, bf16[512,2048]{1,0:T(8,128)(2,1)}, u32[]{:S(2)}) %copy-start.3) | copy-done | bytes 2097176
  57.5 5.5 %all-to-all-done.1.feature_ref = bf16[8,32,512]{2,1,0:T(8,128)(2,1)S(1)} async-done(((bf16[8,32,512]{2,1,0:T(8,128)(2,1)}), bf16[8,32,512]{2,1,0:T(8,128)(2,1)S(1)}, u32[]{:S(2)}, u32[]{:S(2)}) %all-to-all-start.1) | async-done | bytes 262176 | tf_op jit(solution)/shard_map/all_to_all | solution.py:500
  63.0 1.2 output_projection.1
  64.3 0.6 collective-permute-start.9
  64.9 1.4 %collective-permute-start.13 = (bf16[32,1024]{1,0:T(8,128)(2,1)S(1)}, bf16[32,1024]{1,0:T(8,128)(2,1)S(1)}, u32[]{:S(2)}, u32[]{:S(2)}) collective-permute-start(bf16[32,1024]{1,0:T(8,128)(2,1)S(1)} %get-tuple-element.24), channel_id=1, source_target_pairs={{4,0},{8,4},{12,8},{14,12},{10,14},{6,10},{2,6},{0,2},{5,1},{9,5},... | collective-permute-start | bytes 196616 | tf_op jit(solution)/shard_map/ppermute | solution.py:48
  66.4 2.6 %collective-permute-done.9 = bf16[32,1024]{1,0:T(8,128)(2,1)S(1)} collective-permute-done((bf16[32,1024]{1,0:T(8,128)(2,1)S(1)}, bf16[32,1024]{1,0:T(8,128)(2,1)S(1)}, u32[]{:S(2)}, u32[]{:S(2)}) %collective-permute-start.9) | collective-permute-done | bytes 65568 | tf_op jit(solution)/shard_map/ppermute | solution.py:45
  69.1 0.9 collective-permute-start.10
  70.0 1.3 collective-permute-start.14
  71.4 3.6 %collective-permute-done.10 = bf16[32,2048]{1,0:T(8,128)(2,1)S(1)} collective-permute-done((bf16[32,2048]{1,0:T(8,128)(2,1)S(1)}, bf16[32,2048]{1,0:T(8,128)(2,1)S(1)}, u32[]{:S(2)}, u32[]{:S(2)}) %collective-permute-start.10) | collective-permute-done | bytes 131104 | tf_op jit(solution)/shard_map/ppermute | solution.py:45
  75.0 1.1 collective-permute-start.11
  76.2 1.0 collective-permute-start.15
  77.2 2.9 %collective-permute-done.11.refs_1_ = bf16[32,2048]{1,0:T(8,128)(2,1)S(1)} collective-permute-done((bf16[32,2048]{1,0:T(8,128)(2,1)S(1)}, bf16[32,2048]{1,0:T(8,128)(2,1)S(1)}, u32[]{:S(2)}, u32[]{:S(2)}) %collective-permute-start.11) | collective-permute-done | bytes 131104 | tf_op jit(solution)/shard_map/ppermute | solution.py:45
  80.0 0.7 fusion.7
  80.7 1.1 collective-permute-start.12
  81.8 0.7 fusion.5
  82.5 0.9 collective-permute-start.16
  83.4 2.8 %copy-done = bf16[1,2048,1536]{2,1,0:T(8,128)(2,1)S(1)} copy-done((bf16[1,2048,1536]{2,1,0:T(8,128)(2,1)S(1)}, bf16[1,2048,1536]{2,1,0:T(8,128)(2,1)}, u32[]{:S(2)}) %copy-start) | copy-done | bytes 6291480
  86.7 1.1 collective-permute-done.16.down_ref
  87.8 1.1 residual_norm.1
  88.9 0.5 collective-permute-start.18
  89.4 1.6 %collective-permute-start.17 = (bf16[32,2176]{1,0:T(8,128)(2,1)S(1)}, bf16[32,2176]{1,0:T(8,128)(2,1)S(1)}, u32[]{:S(2)}, u32[]{:S(2)}) collective-permute-start(bf16[32,2176]{1,0:T(8,128)(2,1)S(1)} %get-tuple-element.26), channel_id=1, source_target_pairs={{4,0},{8,4},{12,8},{14,12},{10,14},{6,10},{2,6},{0,2},{5,1},{9,5},... | collective-permute-start | bytes 417800 | tf_op jit(solution)/shard_map/ppermute | solution.py:48
  91.0 3.4 %collective-permute-done.18 = bf16[32,2176]{1,0:T(8,128)(2,1)S(1)} collective-permute-done((bf16[32,2176]{1,0:T(8,128)(2,1)S(1)}, bf16[32,2176]{1,0:T(8,128)(2,1)S(1)}, u32[]{:S(2)}, u32[]{:S(2)}) %collective-permute-start.18) | collective-permute-done | bytes 139296 | tf_op jit(solution)/shard_map/ppermute | solution.py:45
  94.4 1.1 collective-permute-start.20
  95.5 0.9 collective-permute-start.19
  96.5 2.8 %load_gate_up.3.refs_1_ = bf16[2048,1536]{1,0:T(8,128)(2,1)S(1)} custom-call(bf16[2048,1536]{1,0:T(8,128)(2,1)} %collective-permute-done.8.refs_1_.refs_0_, bf16[32,2176]{1,0:T(8,128)(2,1)S(1)} %collective-permute-done.17.refs_1_), custom_call_target="tpu_custom_call" | custom-call | bytes 104857600 | tf_op jit(solution)/shard_map/load_gate_up/pallas_call | solution.py:99
  99.5 1.3 collective-permute-start.22
  100.8 0.7 collective-permute-start.21
  101.8 2.9 %collective-permute-done.22 = bf16[32,2176]{1,0:T(8,128)(2,1)S(1)} collective-permute-done((bf16[32,2176]{1,0:T(8,128)(2,1)S(1)}, bf16[32,2176]{1,0:T(8,128)(2,1)S(1)}, u32[]{:S(2)}, u32[]{:S(2)}) %collective-permute-start.22) | collective-permute-done | bytes 139296 | tf_op jit(solution)/shard_map/ppermute | solution.py:45
  104.6 1.2 collective-permute-start.23
  105.9 1.0 collective-permute-start.24
  106.9 2.0 %collective-permute-done.23 = bf16[16,2176]{1,0:T(8,128)(2,1)S(1)} collective-permute-done((bf16[16,2176]{1,0:T(8,128)(2,1)S(1)}, bf16[16,2176]{1,0:T(8,128)(2,1)S(1)}, u32[]{:S(2)}, u32[]{:S(2)}) %collective-permute-start.23) | collective-permute-done | bytes 69664 | tf_op jit(solution)/shard_map/ppermute | solution.py:45
  109.0 1.5 %collective-permute-done.24 = bf16[16,2176]{1,0:T(8,128)(2,1)S(1)} collective-permute-done((bf16[16,2176]{1,0:T(8,128)(2,1)S(1)}, bf16[16,2176]{1,0:T(8,128)(2,1)S(1)}, u32[]{:S(2)}, u32[]{:S(2)}) %collective-permute-start.24) | collective-permute-done | bytes 69664 | tf_op jit(solution)/shard_map/ppermute | solution.py:48
  110.4 5.7 %experts.1 = (f32[32,2048]{1,0:T(8,128)S(1)}, bf16[32,1024]{1,0:T(8,128)(2,1)S(1)}, bf16[32,1024]{1,0:T(8,128)(2,1)S(1)}, f32[3,32,2048]{2,1,0:T(8,128)S(1)}, f32[3,32,2048]{2,1,0:T(8,128)S(1)}) custom-call(s32[1,2]{1,0:T(1,128)S(1)} %fusion.15.slot_ref, bf16[256,2176]{1,0:T(8,128)(2,1)S(1)} %constant_dynamic-update-slice_fusion.5.held, ...), custom_call_target="tpu_custom_call" | custom-call | bytes 104857600 | tf_op jit(solution)/shard_map/experts/pallas_call | solution.py:99
  116.5 1.7 %collective-permute-start.30 = (bf16[32,1024]{1,0:T(8,128)(2,1)S(1)}, bf16[32,1024]{1,0:T(8,128)(2,1)S(1)}, u32[]{:S(2)}, u32[]{:S(2)}) collective-permute-start(bf16[32,1024]{1,0:T(8,128)(2,1)S(1)} %get-tuple-element.32), channel_id=1, source_target_pairs={{4,0},{8,4},{12,8},{14,12},{10,14},{6,10},{2,6},{0,2},{5,1},{9,5},... | collective-permute-start | bytes 196616 | tf_op jit(solution)/shard_map/ppermute | solution.py:48
  118.3 2.2 %collective-permute-done.26 = bf16[32,1024]{1,0:T(8,128)(2,1)S(1)} collective-permute-done((bf16[32,1024]{1,0:T(8,128)(2,1)S(1)}, bf16[32,1024]{1,0:T(8,128)(2,1)S(1)}, u32[]{:S(2)}, u32[]{:S(2)}) %collective-permute-start.26) | collective-permute-done | bytes 65568 | tf_op jit(solution)/shard_map/ppermute | solution.py:45
  120.9 1.8 %collective-permute-start.31 = (bf16[32,2048]{1,0:T(8,128)(2,1)S(1)}, bf16[32,2048]{1,0:T(8,128)(2,1)S(1)}, u32[]{:S(2)}, u32[]{:S(2)}) collective-permute-start(bf16[32,2048]{1,0:T(8,128)(2,1)S(1)} %pad_maximum_fusion.4), channel_id=1, source_target_pairs={{4,0},{8,4},{12,8},{14,12},{10,14},{6,10},{2,6},{0,2},{5,1},{9,5},... | collective-permute-start | bytes 393224 | tf_op jit(solution)/shard_map/ppermute | solution.py:48
  122.7 2.8 %collective-permute-done.27 = bf16[32,2048]{1,0:T(8,128)(2,1)S(1)} collective-permute-done((bf16[32,2048]{1,0:T(8,128)(2,1)S(1)}, bf16[32,2048]{1,0:T(8,128)(2,1)S(1)}, u32[]{:S(2)}, u32[]{:S(2)}) %collective-permute-start.27) | collective-permute-done | bytes 131104 | tf_op jit(solution)/shard_map/ppermute | solution.py:45
  125.9 1.8 %collective-permute-start.32 = (bf16[32,2048]{1,0:T(8,128)(2,1)S(1)}, bf16[32,2048]{1,0:T(8,128)(2,1)S(1)}, u32[]{:S(2)}, u32[]{:S(2)}) collective-permute-start(bf16[32,2048]{1,0:T(8,128)(2,1)S(1)} %fusion), channel_id=1, source_target_pairs={{4,0},{8,4},{12,8},{14,12},{10,14},{6,10},{2,6},{0,2},{5,1},{9,5},... | collective-permute-start | bytes 393224 | tf_op jit(solution)/shard_map/ppermute | solution.py:48
  127.7 2.8 %collective-permute-done.28 = bf16[32,2048]{1,0:T(8,128)(2,1)S(1)} collective-permute-done((bf16[32,2048]{1,0:T(8,128)(2,1)S(1)}, bf16[32,2048]{1,0:T(8,128)(2,1)S(1)}, u32[]{:S(2)}, u32[]{:S(2)}) %collective-permute-start.28) | collective-permute-done | bytes 131104 | tf_op jit(solution)/shard_map/ppermute | solution.py:45
  131.0 1.8 %collective-permute-start.33 = (bf16[32,2048]{1,0:T(8,128)(2,1)S(1)}, bf16[32,2048]{1,0:T(8,128)(2,1)S(1)}, u32[]{:S(2)}, u32[]{:S(2)}) collective-permute-start(bf16[32,2048]{1,0:T(8,128)(2,1)S(1)} %fusion.1), channel_id=1, source_target_pairs={{4,0},{8,4},{12,8},{14,12},{10,14},{6,10},{2,6},{0,2},{5,1},{9,5},... | collective-permute-start | bytes 393224 | tf_op jit(solution)/shard_map/ppermute | solution.py:48
  132.8 2.8 %collective-permute-done.29 = bf16[32,2048]{1,0:T(8,128)(2,1)S(1)} collective-permute-done((bf16[32,2048]{1,0:T(8,128)(2,1)S(1)}, bf16[32,2048]{1,0:T(8,128)(2,1)S(1)}, u32[]{:S(2)}, u32[]{:S(2)}) %collective-permute-start.29) | collective-permute-done | bytes 131104 | tf_op jit(solution)/shard_map/ppermute | solution.py:45
  136.0 0.7 add_convert_fusion
  (102 shorter events, 5.4 us)
Async XLA Ops:
  0.0 39.1 %collective-permute-start.8 = (bf16[2048,1536]{1,0:T(8,128)(2,1)}, bf16[2048,1536]{1,0:T(8,128)(2,1)}, u32[]{:S(2)}, u32[]{:S(2)}) collective-permute-start(bf16[2048,1536]{1,0:T(8,128)(2,1)} %bitcast.49), channel_id=1, source_target_pairs={{0,1},{1,0},{2,3},{3,2},{4,5},{5,4},{6,7},{7,6},{8,9},{9,8},{10,11... | collective-permute-start | bytes 18874376 | tf_op jit(solution)/shard_map/ppermute | solution.py:450
  0.5 6.9 %collective-permute-start.1 = (bf16[32,2048]{1,0:T(8,128)(2,1)}, bf16[32,2048]{1,0:T(8,128)(2,1)S(1)}, u32[]{:S(2)}, u32[]{:S(2)}) collective-permute-start(bf16[32,2048]{1,0:T(8,128)(2,1)} %hidden_ref.1), channel_id=1, source_target_pairs={{0,4},{4,8},{8,12},{12,14},{14,10},{10,6},{6,2},{2,0},{1,5},{5,9},... | collective-permute-start | bytes 393224 | tf_op jit(solution)/shard_map/ppermute | solution.py:45
  3.0 6.1 %collective-permute-start = (bf16[32,2048]{1,0:T(8,128)(2,1)}, bf16[32,2048]{1,0:T(8,128)(2,1)S(1)}, u32[]{:S(2)}, u32[]{:S(2)}) collective-permute-start(bf16[32,2048]{1,0:T(8,128)(2,1)} %hidden_ref.1), channel_id=1, source_target_pairs={{4,0},{8,4},{12,8},{14,12},{10,14},{6,10},{2,6},{0,2},{5,1},{9,5},... | collective-permute-start | bytes 393224 | tf_op jit(solution)/shard_map/ppermute | solution.py:48
  7.3 5.3 %collective-permute-start.3 = (bf16[32,2048]{1,0:T(8,128)(2,1)S(1)}, bf16[32,2048]{1,0:T(8,128)(2,1)S(1)}, u32[]{:S(2)}, u32[]{:S(2)}) collective-permute-start(bf16[32,2048]{1,0:T(8,128)(2,1)S(1)} %collective-permute-done.1), channel_id=1, source_target_pairs={{0,4},{4,8},{8,12},{12,14},{14,10},{10,6},{6,2},{2,0},{1,5},{5,9},... | collective-permute-start | bytes 393224 | tf_op jit(solution)/shard_map/ppermute | solution.py:45
  9.2 5.1 %collective-permute-start.2 = (bf16[32,2048]{1,0:T(8,128)(2,1)S(1)}, bf16[32,2048]{1,0:T(8,128)(2,1)S(1)}, u32[]{:S(2)}, u32[]{:S(2)}) collective-permute-start(bf16[32,2048]{1,0:T(8,128)(2,1)S(1)} %collective-permute-done.refs_1_), channel_id=1, source_target_pairs={{4,0},{8,4},{12,8},{14,12},{10,14},{6,10},{2,6},{0,2},{5,1},{9,5},... | collective-permute-start | bytes 393224 | tf_op jit(solution)/shard_map/ppermute | solution.py:48
  11.1 8.6 %copy-start.9 = (f32[2048]{0:T(1024)S(1)}, f32[2048]{0:T(1024)}, u32[]{:S(2)}) copy-start(f32[2048]{0:T(1024)} %param.22) | copy-start | bytes 24580
  12.7 5.0 %collective-permute-start.5 = (bf16[32,2048]{1,0:T(8,128)(2,1)S(1)}, bf16[32,2048]{1,0:T(8,128)(2,1)S(1)}, u32[]{:S(2)}, u32[]{:S(2)}) collective-permute-start(bf16[32,2048]{1,0:T(8,128)(2,1)S(1)} %collective-permute-done.3), channel_id=1, source_target_pairs={{0,4},{4,8},{8,12},{12,14},{14,10},{10,6},{6,2},{2,0},{1,5},{5,9},... | collective-permute-start | bytes 393224 | tf_op jit(solution)/shard_map/ppermute | solution.py:45
  14.3 5.0 %collective-permute-start.4 = (bf16[32,2048]{1,0:T(8,128)(2,1)S(1)}, bf16[32,2048]{1,0:T(8,128)(2,1)S(1)}, u32[]{:S(2)}, u32[]{:S(2)}) collective-permute-start(bf16[32,2048]{1,0:T(8,128)(2,1)S(1)} %collective-permute-done.2), channel_id=1, source_target_pairs={{4,0},{8,4},{12,8},{14,12},{10,14},{6,10},{2,6},{0,2},{5,1},{9,5},... | collective-permute-start | bytes 393224 | tf_op jit(solution)/shard_map/ppermute | solution.py:48
  17.7 4.3 %collective-permute-start.6 = (bf16[16,2048]{1,0:T(8,128)(2,1)S(1)}, bf16[16,2048]{1,0:T(8,128)(2,1)S(1)}, u32[]{:S(2)}, u32[]{:S(2)}) collective-permute-start(bf16[16,2048]{1,0:T(8,128)(2,1)S(1)} %slice.100), channel_id=1, source_target_pairs={{0,4},{4,8},{8,12},{12,14},{14,10},{10,6},{6,2},{2,0},{1,5},{5,9},... | collective-permute-start | bytes 196616 | tf_op jit(solution)/shard_map/ppermute | solution.py:45
  19.3 4.3 %collective-permute-start.7 = (bf16[16,2048]{1,0:T(8,128)(2,1)S(1)}, bf16[16,2048]{1,0:T(8,128)(2,1)S(1)}, u32[]{:S(2)}, u32[]{:S(2)}) collective-permute-start(bf16[16,2048]{1,0:T(8,128)(2,1)S(1)} %slice.101), channel_id=1, source_target_pairs={{4,0},{8,4},{12,8},{14,12},{10,14},{6,10},{2,6},{0,2},{5,1},{9,5},... | collective-permute-start | bytes 196616 | tf_op jit(solution)/shard_map/ppermute | solution.py:48
  23.6 6.8 %copy-start.11 = (s32[32,8]{0,1:T(8,128)S(1)}, s32[32,8]{0,1:T(8,128)}, u32[]{:S(2)}) copy-start(s32[32,8]{0,1:T(8,128)} %param.19) | copy-start | bytes 3076
  23.6 6.9 %copy-start.12 = (s32[32,8]{0,1:T(8,128)S(1)}, s32[32,8]{0,1:T(8,128)}, u32[]{:S(2)}) copy-start(s32[32,8]{0,1:T(8,128)} %param.20) | copy-start | bytes 3076
  23.6 7.0 %copy-start.7 = (s32[16]{0:T(128)S(1)}, s32[16]{0:T(128)}, u32[]{:S(2)}) copy-start(s32[16]{0:T(128)} %param.21) | copy-start | bytes 196
  23.6 8.3 %copy-start.13 = (s32[1,32]{1,0:T(1,128)S(1)}, s32[1,32]{1,0:T(1,128)}, u32[]{:S(2)}) copy-start(s32[1,32]{1,0:T(1,128)} %length_ref.1) | copy-start | bytes 388
  25.6 13.5 %all-to-all-start = ((bf16[8,32,640]{2,1,0:T(8,128)(2,1)}), bf16[8,32,640]{2,1,0:T(8,128)(2,1)S(1)}, u32[]{:S(2)}, u32[]{:S(2)}) async-start(bf16[8,32,640]{2,1,0:T(8,128)(2,1)} %project.1), calls=%async_computation | async-start | bytes 655360 | tf_op jit(solution)/shard_map/all_to_all | solution.py:492
  31.4 0.6 copy-start.5
  39.1 0.7 copy-start.8
  51.3 11.7 %all-to-all-start.1 = ((bf16[8,32,512]{2,1,0:T(8,128)(2,1)}), bf16[8,32,512]{2,1,0:T(8,128)(2,1)S(1)}, u32[]{:S(2)}, u32[]{:S(2)}) async-start(bf16[8,32,512]{2,1,0:T(8,128)(2,1)} %ragged_attention.1.refs_1_), calls=%async_computation.1 | async-start | bytes 524288 | tf_op jit(solution)/shard_map/all_to_all | solution.py:500
  54.7 1.0 copy-start.2
  55.7 1.6 %copy-start.3 = (bf16[512,2048]{1,0:T(8,128)(2,1)S(1)}, bf16[512,2048]{1,0:T(8,128)(2,1)}, u32[]{:S(2)}) copy-start(bf16[512,2048]{1,0:T(8,128)(2,1)} %refs_0_.3) | copy-start | bytes 6291460
  64.3 4.8 %collective-permute-start.9 = (bf16[32,1024]{1,0:T(8,128)(2,1)S(1)}, bf16[32,1024]{1,0:T(8,128)(2,1)S(1)}, u32[]{:S(2)}, u32[]{:S(2)}) collective-permute-start(bf16[32,1024]{1,0:T(8,128)(2,1)S(1)} %get-tuple-element.22), channel_id=1, source_target_pairs={{0,4},{4,8},{8,12},{12,14},{14,10},{10,6},{6,2},{2,0},{1,5},{5,9},... | collective-permute-start | bytes 196616 | tf_op jit(solution)/shard_map/ppermute | solution.py:45
  64.9 5.1 %collective-permute-start.13 = (bf16[32,1024]{1,0:T(8,128)(2,1)S(1)}, bf16[32,1024]{1,0:T(8,128)(2,1)S(1)}, u32[]{:S(2)}, u32[]{:S(2)}) collective-permute-start(bf16[32,1024]{1,0:T(8,128)(2,1)S(1)} %get-tuple-element.24), channel_id=1, source_target_pairs={{4,0},{8,4},{12,8},{14,12},{10,14},{6,10},{2,6},{0,2},{5,1},{9,5},... | collective-permute-start | bytes 196616 | tf_op jit(solution)/shard_map/ppermute | solution.py:48
  69.1 14.3 %copy-start.1 = (bf16[1,768,2048]{2,1,0:T(8,128)(2,1)S(1)}, bf16[1,768,2048]{2,1,0:T(8,128)(2,1)}, u32[]{:S(2)}) copy-start(bf16[1,768,2048]{2,1,0:T(8,128)(2,1)} %param.29) | copy-start | bytes 9437188
  69.1 5.9 %collective-permute-start.10 = (bf16[32,2048]{1,0:T(8,128)(2,1)S(1)}, bf16[32,2048]{1,0:T(8,128)(2,1)S(1)}, u32[]{:S(2)}, u32[]{:S(2)}) collective-permute-start(bf16[32,2048]{1,0:T(8,128)(2,1)S(1)} %pad_maximum_fusion.1), channel_id=1, source_target_pairs={{0,4},{4,8},{8,12},{12,14},{14,10},{10,6},{6,2},{2,0},{1,5},{5,9},... | collective-permute-start | bytes 393224 | tf_op jit(solution)/shard_map/ppermute | solution.py:45
  70.0 6.1 %collective-permute-start.14 = (bf16[32,2048]{1,0:T(8,128)(2,1)S(1)}, bf16[32,2048]{1,0:T(8,128)(2,1)S(1)}, u32[]{:S(2)}, u32[]{:S(2)}) collective-permute-start(bf16[32,2048]{1,0:T(8,128)(2,1)S(1)} %pad_maximum_fusion.2), channel_id=1, source_target_pairs={{4,0},{8,4},{12,8},{14,12},{10,14},{6,10},{2,6},{0,2},{5,1},{9,5},... | collective-permute-start | bytes 393224 | tf_op jit(solution)/shard_map/ppermute | solution.py:48
  75.0 5.0 %collective-permute-start.11 = (bf16[32,2048]{1,0:T(8,128)(2,1)S(1)}, bf16[32,2048]{1,0:T(8,128)(2,1)S(1)}, u32[]{:S(2)}, u32[]{:S(2)}) collective-permute-start(bf16[32,2048]{1,0:T(8,128)(2,1)S(1)} %fusion.6), channel_id=1, source_target_pairs={{0,4},{4,8},{8,12},{12,14},{14,10},{10,6},{6,2},{2,0},{1,5},{5,9},... | collective-permute-start | bytes 393224 | tf_op jit(solution)/shard_map/ppermute | solution.py:45
  76.2 5.6 %collective-permute-start.15 = (bf16[32,2048]{1,0:T(8,128)(2,1)S(1)}, bf16[32,2048]{1,0:T(8,128)(2,1)S(1)}, u32[]{:S(2)}, u32[]{:S(2)}) collective-permute-start(bf16[32,2048]{1,0:T(8,128)(2,1)S(1)} %fusion.4), channel_id=1, source_target_pairs={{4,0},{8,4},{12,8},{14,12},{10,14},{6,10},{2,6},{0,2},{5,1},{9,5},... | collective-permute-start | bytes 393224 | tf_op jit(solution)/shard_map/ppermute | solution.py:48
  80.7 6.0 %collective-permute-start.12 = (bf16[32,2048]{1,0:T(8,128)(2,1)}, bf16[32,2048]{1,0:T(8,128)(2,1)}, u32[]{:S(2)}, u32[]{:S(2)}) collective-permute-start(bf16[32,2048]{1,0:T(8,128)(2,1)} %fusion.7), channel_id=1, source_target_pairs={{0,4},{4,8},{8,12},{12,14},{14,10},{10,6},{6,2},{2,0},{1,5},{5,9},... | collective-permute-start | bytes 393224 | tf_op jit(solution)/shard_map/ppermute | solution.py:45
  82.5 5.3 %collective-permute-start.16 = (bf16[32,2048]{1,0:T(8,128)(2,1)}, bf16[32,2048]{1,0:T(8,128)(2,1)}, u32[]{:S(2)}, u32[]{:S(2)}) collective-permute-start(bf16[32,2048]{1,0:T(8,128)(2,1)} %fusion.5), channel_id=1, source_target_pairs={{4,0},{8,4},{12,8},{14,12},{10,14},{6,10},{2,6},{0,2},{5,1},{9,5},... | collective-permute-start | bytes 393224 | tf_op jit(solution)/shard_map/ppermute | solution.py:48
  83.4 27.0 %collective-permute-start.25 = (bf16[768,2048]{1,0:T(8,128)(2,1)S(1)}, bf16[768,2048]{1,0:T(8,128)(2,1)S(1)}, u32[]{:S(2)}, u32[]{:S(2)}) collective-permute-start(bf16[768,2048]{1,0:T(8,128)(2,1)S(1)} %bitcast.51), channel_id=1, source_target_pairs={{0,1},{1,0},{2,3},{3,2},{4,5},{5,4},{6,7},{7,6},{8,9},{9,8},{10,11... | collective-permute-start | bytes 9437192 | tf_op jit(solution)/shard_map/ppermute | solution.py:450
  83.4 2.8 %copy-start = (bf16[1,2048,1536]{2,1,0:T(8,128)(2,1)S(1)}, bf16[1,2048,1536]{2,1,0:T(8,128)(2,1)}, u32[]{:S(2)}) copy-start(bf16[1,2048,1536]{2,1,0:T(8,128)(2,1)} %param.28) | copy-start | bytes 18874372
  86.2 1.5 %copy-start.10 = (f32[2048]{0:T(1024)S(1)}, f32[2048]{0:T(1024)}, u32[]{:S(2)}) copy-start(f32[2048]{0:T(1024)} %param.23) | copy-start | bytes 24580
  86.2 1.6 %copy-start.4 = (bf16[32,2048]{1,0:T(8,128)(2,1)S(1)}, bf16[32,2048]{1,0:T(8,128)(2,1)}, u32[]{:S(2)}) copy-start(bf16[32,2048]{1,0:T(8,128)(2,1)} %hidden_ref.1) | copy-start | bytes 393220
  86.2 1.6 %copy-start.6 = (bf16[32,128]{1,0:T(8,128)(2,1)S(1)}, bf16[32,128]{1,0:T(8,128)(2,1)}, u32[]{:S(2)}) copy-start(bf16[32,128]{1,0:T(8,128)(2,1)} %copy-done.5) | copy-start | bytes 24580
  88.9 5.5 %collective-permute-start.18 = (bf16[32,2176]{1,0:T(8,128)(2,1)S(1)}, bf16[32,2176]{1,0:T(8,128)(2,1)S(1)}, u32[]{:S(2)}, u32[]{:S(2)}) collective-permute-start(bf16[32,2176]{1,0:T(8,128)(2,1)S(1)} %get-tuple-element.26), channel_id=1, source_target_pairs={{0,4},{4,8},{8,12},{12,14},{14,10},{10,6},{6,2},{2,0},{1,5},{5,9},... | collective-permute-start | bytes 417800 | tf_op jit(solution)/shard_map/ppermute | solution.py:45
  89.4 6.1 %collective-permute-start.17 = (bf16[32,2176]{1,0:T(8,128)(2,1)S(1)}, bf16[32,2176]{1,0:T(8,128)(2,1)S(1)}, u32[]{:S(2)}, u32[]{:S(2)}) collective-permute-start(bf16[32,2176]{1,0:T(8,128)(2,1)S(1)} %get-tuple-element.26), channel_id=1, source_target_pairs={{4,0},{8,4},{12,8},{14,12},{10,14},{6,10},{2,6},{0,2},{5,1},{9,5},... | collective-permute-start | bytes 417800 | tf_op jit(solution)/shard_map/ppermute | solution.py:48
  94.4 5.1 %collective-permute-start.20 = (bf16[32,2176]{1,0:T(8,128)(2,1)S(1)}, bf16[32,2176]{1,0:T(8,128)(2,1)S(1)}, u32[]{:S(2)}, u32[]{:S(2)}) collective-permute-start(bf16[32,2176]{1,0:T(8,128)(2,1)S(1)} %collective-permute-done.18), channel_id=1, source_target_pairs={{0,4},{4,8},{8,12},{12,14},{14,10},{10,6},{6,2},{2,0},{1,5},{5,9},... | collective-permute-start | bytes 417800 | tf_op jit(solution)/shard_map/ppermute | solution.py:45
  95.5 5.3 %collective-permute-start.19 = (bf16[32,2176]{1,0:T(8,128)(2,1)S(1)}, bf16[32,2176]{1,0:T(8,128)(2,1)S(1)}, u32[]{:S(2)}, u32[]{:S(2)}) collective-permute-start(bf16[32,2176]{1,0:T(8,128)(2,1)S(1)} %collective-permute-done.17.refs_1_), channel_id=1, source_target_pairs={{4,0},{8,4},{12,8},{14,12},{10,14},{6,10},{2,6},{0,2},{5,1},{9,5},... | collective-permute-start | bytes 417800 | tf_op jit(solution)/shard_map/ppermute | solution.py:48
  99.5 5.2 %collective-permute-start.22 = (bf16[32,2176]{1,0:T(8,128)(2,1)S(1)}, bf16[32,2176]{1,0:T(8,128)(2,1)S(1)}, u32[]{:S(2)}, u32[]{:S(2)}) collective-permute-start(bf16[32,2176]{1,0:T(8,128)(2,1)S(1)} %collective-permute-done.20), channel_id=1, source_target_pairs={{0,4},{4,8},{8,12},{12,14},{14,10},{10,6},{6,2},{2,0},{1,5},{5,9},... | collective-permute-start | bytes 417800 | tf_op jit(solution)/shard_map/ppermute | solution.py:45
  100.8 5.1 %collective-permute-start.21 = (bf16[32,2176]{1,0:T(8,128)(2,1)S(1)}, bf16[32,2176]{1,0:T(8,128)(2,1)S(1)}, u32[]{:S(2)}, u32[]{:S(2)}) collective-permute-start(bf16[32,2176]{1,0:T(8,128)(2,1)S(1)} %collective-permute-done.19.refs_1_), channel_id=1, source_target_pairs={{4,0},{8,4},{12,8},{14,12},{10,14},{6,10},{2,6},{0,2},{5,1},{9,5},... | collective-permute-start | bytes 417800 | tf_op jit(solution)/shard_map/ppermute | solution.py:48
  104.6 4.3 %collective-permute-start.23 = (bf16[16,2176]{1,0:T(8,128)(2,1)S(1)}, bf16[16,2176]{1,0:T(8,128)(2,1)S(1)}, u32[]{:S(2)}, u32[]{:S(2)}) collective-permute-start(bf16[16,2176]{1,0:T(8,128)(2,1)S(1)} %slice.106), channel_id=1, source_target_pairs={{0,4},{4,8},{8,12},{12,14},{14,10},{10,6},{6,2},{2,0},{1,5},{5,9},... | collective-permute-start | bytes 208904 | tf_op jit(solution)/shard_map/ppermute | solution.py:45
  105.9 4.5 %collective-permute-start.24 = (bf16[16,2176]{1,0:T(8,128)(2,1)S(1)}, bf16[16,2176]{1,0:T(8,128)(2,1)S(1)}, u32[]{:S(2)}, u32[]{:S(2)}) collective-permute-start(bf16[16,2176]{1,0:T(8,128)(2,1)S(1)} %slice.107), channel_id=1, source_target_pairs={{4,0},{8,4},{12,8},{14,12},{10,14},{6,10},{2,6},{0,2},{5,1},{9,5},... | collective-permute-start | bytes 208904 | tf_op jit(solution)/shard_map/ppermute | solution.py:48
  116.1 4.3 %collective-permute-start.26 = (bf16[32,1024]{1,0:T(8,128)(2,1)S(1)}, bf16[32,1024]{1,0:T(8,128)(2,1)S(1)}, u32[]{:S(2)}, u32[]{:S(2)}) collective-permute-start(bf16[32,1024]{1,0:T(8,128)(2,1)S(1)} %get-tuple-element.30), channel_id=1, source_target_pairs={{0,4},{4,8},{8,12},{12,14},{14,10},{10,6},{6,2},{2,0},{1,5},{5,9},... | collective-permute-start | bytes 196616 | tf_op jit(solution)/shard_map/ppermute | solution.py:45
  116.5 4.4 %collective-permute-start.30 = (bf16[32,1024]{1,0:T(8,128)(2,1)S(1)}, bf16[32,1024]{1,0:T(8,128)(2,1)S(1)}, u32[]{:S(2)}, u32[]{:S(2)}) collective-permute-start(bf16[32,1024]{1,0:T(8,128)(2,1)S(1)} %get-tuple-element.32), channel_id=1, source_target_pairs={{4,0},{8,4},{12,8},{14,12},{10,14},{6,10},{2,6},{0,2},{5,1},{9,5},... | collective-permute-start | bytes 196616 | tf_op jit(solution)/shard_map/ppermute | solution.py:48
  120.5 5.0 %collective-permute-start.27 = (bf16[32,2048]{1,0:T(8,128)(2,1)S(1)}, bf16[32,2048]{1,0:T(8,128)(2,1)S(1)}, u32[]{:S(2)}, u32[]{:S(2)}) collective-permute-start(bf16[32,2048]{1,0:T(8,128)(2,1)S(1)} %pad_maximum_fusion.3), channel_id=1, source_target_pairs={{0,4},{4,8},{8,12},{12,14},{14,10},{10,6},{6,2},{2,0},{1,5},{5,9},... | collective-permute-start | bytes 393224 | tf_op jit(solution)/shard_map/ppermute | solution.py:45
  120.9 5.0 %collective-permute-start.31 = (bf16[32,2048]{1,0:T(8,128)(2,1)S(1)}, bf16[32,2048]{1,0:T(8,128)(2,1)S(1)}, u32[]{:S(2)}, u32[]{:S(2)}) collective-permute-start(bf16[32,2048]{1,0:T(8,128)(2,1)S(1)} %pad_maximum_fusion.4), channel_id=1, source_target_pairs={{4,0},{8,4},{12,8},{14,12},{10,14},{6,10},{2,6},{0,2},{5,1},{9,5},... | collective-permute-start | bytes 393224 | tf_op jit(solution)/shard_map/ppermute | solution.py:48
  125.6 5.0 %collective-permute-start.28 = (bf16[32,2048]{1,0:T(8,128)(2,1)S(1)}, bf16[32,2048]{1,0:T(8,128)(2,1)S(1)}, u32[]{:S(2)}, u32[]{:S(2)}) collective-permute-start(bf16[32,2048]{1,0:T(8,128)(2,1)S(1)} %fusion.2), channel_id=1, source_target_pairs={{0,4},{4,8},{8,12},{12,14},{14,10},{10,6},{6,2},{2,0},{1,5},{5,9},... | collective-permute-start | bytes 393224 | tf_op jit(solution)/shard_map/ppermute | solution.py:45
  125.9 5.0 %collective-permute-start.32 = (bf16[32,2048]{1,0:T(8,128)(2,1)S(1)}, bf16[32,2048]{1,0:T(8,128)(2,1)S(1)}, u32[]{:S(2)}, u32[]{:S(2)}) collective-permute-start(bf16[32,2048]{1,0:T(8,128)(2,1)S(1)} %fusion), channel_id=1, source_target_pairs={{4,0},{8,4},{12,8},{14,12},{10,14},{6,10},{2,6},{0,2},{5,1},{9,5},... | collective-permute-start | bytes 393224 | tf_op jit(solution)/shard_map/ppermute | solution.py:48
  130.6 5.0 %collective-permute-start.29 = (bf16[32,2048]{1,0:T(8,128)(2,1)S(1)}, bf16[32,2048]{1,0:T(8,128)(2,1)S(1)}, u32[]{:S(2)}, u32[]{:S(2)}) collective-permute-start(bf16[32,2048]{1,0:T(8,128)(2,1)S(1)} %fusion.3), channel_id=1, source_target_pairs={{0,4},{4,8},{8,12},{12,14},{14,10},{10,6},{6,2},{2,0},{1,5},{5,9},... | collective-permute-start | bytes 393224 | tf_op jit(solution)/shard_map/ppermute | solution.py:45
  131.0 5.0 %collective-permute-start.33 = (bf16[32,2048]{1,0:T(8,128)(2,1)S(1)}, bf16[32,2048]{1,0:T(8,128)(2,1)S(1)}, u32[]{:S(2)}, u32[]{:S(2)}) collective-permute-start(bf16[32,2048]{1,0:T(8,128)(2,1)S(1)} %fusion.1), channel_id=1, source_target_pairs={{4,0},{8,4},{12,8},{14,12},{10,14},{6,10},{2,6},{0,2},{5,1},{9,5},... | collective-permute-start | bytes 393224 | tf_op jit(solution)/shard_map/ppermute | solution.py:48

commit v4 on v3

--- a/solution.py
+++ b/solution.py
@@ -16,7 +16,7 @@
 LONGEST = 256
 ALIGN = 16
 WINDOW = LONGEST + ALIGN
-UNROLL = 8
+UNROLL = 16
 TILE = 256
 
 

time: 137 us -> 137 us (level)
  no operation moved by 1% of the time
where the time goes in v4:
time: 137 us; the launch traced here: 136 us
  waiting for transfers between devices  53.7 us (39%)
  starting transfers between devices  42.7 us (31%)
  Pallas kernels  27.7 us (20%)
  local copies, waits for them, and re-layouts  8.16 us (6%)
  other arithmetic  3.24 us (2%)
    ppermute x16, waiting for transfers between devices, ahead(): return lax.ppermute(values, 'dev', self.forward)  37.2 us
    pallas_call x12, Pallas kernels, call(): pl.pallas_call(body, out_shape=outs, in_specs=whole_blocks(ins), out_spec...  27.7 us
    ppermute x16, starting transfers between devices, behind(): return lax.ppermute(values, 'dev', self.backward)  17.2 us
    ppermute x16, starting transfers between devices, ahead(): return lax.ppermute(values, 'dev', self.forward)  16.8 us
    unnamed x42, local copies, waits for them, and re-layouts  7.99 us
    all_to_all x1, waiting for transfers between devices, on_device(): lax.all_to_all(blocks, 'dev', split_axis=0, concat_axis=0, tiled=True)  6.28 us
    all_to_all x1, waiting for transfers between devices, on_device(): lax.all_to_all(attention, 'dev', split_axis=0, concat_axis=0, tiled=True)  5.55 us
    all_to_all x1, starting transfers between devices, on_device(): lax.all_to_all(blocks, 'dev', split_axis=0, concat_axis=0, tiled=True)  4.82 us
  transfers between devices with their start and end apart: 36, of which 21 were waited for; matrix products, arithmetic and copies ran while one was open for 3% of the time, Pallas kernels for 7%

profile of v4, /device:TPU:0, one launch (start us, length us, event | category | flops | bytes accessed | tf_op | source)
XLA Modules:
  0.0 136.0 jit_solution(14209315464027687848)
XLA Ops:
  0.5 2.6 %collective-permute-start.1 = (bf16[32,2048]{1,0:T(8,128)(2,1)}, bf16[32,2048]{1,0:T(8,128)(2,1)S(1)}, u32[]{:S(2)}, u32[]{:S(2)}) collective-permute-start(bf16[32,2048]{1,0:T(8,128)(2,1)} %hidden_ref.1), channel_id=1, source_target_pairs={{0,4},{4,8},{8,12},{12,14},{14,10},{10,6},{6,2},{2,0},{1,5},{5,9},... | collective-permute-start | bytes 393224 | tf_op jit(solution)/shard_map/ppermute | solution.py:45
  3.0 1.0 constant_dynamic-update-slice_fusion.4
  4.1 3.3 %collective-permute-done.1 = bf16[32,2048]{1,0:T(8,128)(2,1)S(1)} collective-permute-done((bf16[32,2048]{1,0:T(8,128)(2,1)}, bf16[32,2048]{1,0:T(8,128)(2,1)S(1)}, u32[]{:S(2)}, u32[]{:S(2)}) %collective-permute-start.1) | collective-permute-done | bytes 131104 | tf_op jit(solution)/shard_map/ppermute | solution.py:45
  7.3 1.8 %collective-permute-start.3 = (bf16[32,2048]{1,0:T(8,128)(2,1)S(1)}, bf16[32,2048]{1,0:T(8,128)(2,1)S(1)}, u32[]{:S(2)}, u32[]{:S(2)}) collective-permute-start(bf16[32,2048]{1,0:T(8,128)(2,1)S(1)} %collective-permute-done.1), channel_id=1, source_target_pairs={{0,4},{4,8},{8,12},{12,14},{14,10},{10,6},{6,2},{2,0},{1,5},{5,9},... | collective-permute-start | bytes 393224 | tf_op jit(solution)/shard_map/ppermute | solution.py:45
  9.4 1.7 %load_project.1.weight_ref = bf16[2048,640]{1,0:T(8,128)(2,1)S(1)} custom-call(bf16[2048,640]{1,0:T(8,128)(2,1)} %refs_0_.2, bf16[32,2048]{1,0:T(8,128)(2,1)S(1)} %collective-permute-done.refs_1_), custom_call_target="tpu_custom_call" | custom-call | bytes 104857600 | tf_op jit(solution)/shard_map/load_project/pallas_call | solution.py:99
  11.2 1.5 %collective-permute-done.3 = bf16[32,2048]{1,0:T(8,128)(2,1)S(1)} collective-permute-done((bf16[32,2048]{1,0:T(8,128)(2,1)S(1)}, bf16[32,2048]{1,0:T(8,128)(2,1)S(1)}, u32[]{:S(2)}, u32[]{:S(2)}) %collective-permute-start.3) | collective-permute-done | bytes 131104 | tf_op jit(solution)/shard_map/ppermute | solution.py:45
  12.7 1.6 %collective-permute-start.5 = (bf16[32,2048]{1,0:T(8,128)(2,1)S(1)}, bf16[32,2048]{1,0:T(8,128)(2,1)S(1)}, u32[]{:S(2)}, u32[]{:S(2)}) collective-permute-start(bf16[32,2048]{1,0:T(8,128)(2,1)S(1)} %collective-permute-done.3), channel_id=1, source_target_pairs={{0,4},{4,8},{8,12},{12,14},{14,10},{10,6},{6,2},{2,0},{1,5},{5,9},... | collective-permute-start | bytes 393224 | tf_op jit(solution)/shard_map/ppermute | solution.py:45
  14.7 2.9 %collective-permute-done.5 = bf16[32,2048]{1,0:T(8,128)(2,1)S(1)} collective-permute-done((bf16[32,2048]{1,0:T(8,128)(2,1)S(1)}, bf16[32,2048]{1,0:T(8,128)(2,1)S(1)}, u32[]{:S(2)}, u32[]{:S(2)}) %collective-permute-start.5) | collective-permute-done | bytes 131104 | tf_op jit(solution)/shard_map/ppermute | solution.py:45
  17.7 1.6 %collective-permute-start.6 = (bf16[16,2048]{1,0:T(8,128)(2,1)S(1)}, bf16[16,2048]{1,0:T(8,128)(2,1)S(1)}, u32[]{:S(2)}, u32[]{:S(2)}) collective-permute-start(bf16[16,2048]{1,0:T(8,128)(2,1)S(1)} %slice.100), channel_id=1, source_target_pairs={{0,4},{4,8},{8,12},{12,14},{14,10},{10,6},{6,2},{2,0},{1,5},{5,9},... | collective-permute-start | bytes 196616 | tf_op jit(solution)/shard_map/ppermute | solution.py:45
  19.8 0.8 project_near.1.near_ref
  20.6 1.3 collective-permute-done.6
  21.9 1.7 %collective-permute-done.7 = bf16[16,2048]{1,0:T(8,128)(2,1)S(1)} collective-permute-done((bf16[16,2048]{1,0:T(8,128)(2,1)S(1)}, bf16[16,2048]{1,0:T(8,128)(2,1)S(1)}, u32[]{:S(2)}, u32[]{:S(2)}) %collective-permute-start.7) | collective-permute-done | bytes 65568 | tf_op jit(solution)/shard_map/ppermute | solution.py:48
  23.7 2.0 %project.1 = bf16[8,32,640]{2,1,0:T(8,128)(2,1)} custom-call(s32[1,8]{1,0:T(1,128)S(1)} %compare_select_fusion.4.owner_ref, bf16[160,640]{1,0:T(8,128)(2,1)S(1)} %project_near.1.near_ref, bf16[96,2048]{1,0:T(8,128)(2,1)S(1)} %pad_maximum_fusion.hidden_ref, f32[8,2048]{1,0:T(8,128)S(1)} %broadcast_in_dim.10.gain_ref, bf16[2048,640]{1,0:T(8,128)(2,1)S(1)} %load_project.1.weight_ref), custom_call_target="tpu_custom_call" | custom-call | bytes 104857600 | tf_op jit(solution)/shard_map/project/pallas_call | solution.py:99
  25.6 4.8 %all-to-all-start = ((bf16[8,32,640]{2,1,0:T(8,128)(2,1)}), bf16[8,32,640]{2,1,0:T(8,128)(2,1)S(1)}, u32[]{:S(2)}, u32[]{:S(2)}) async-start(bf16[8,32,640]{2,1,0:T(8,128)(2,1)} %project.1), calls=%async_computation | async-start | bytes 655360 | tf_op jit(solution)/shard_map/all_to_all | solution.py:492
  30.6 0.8 gate_digits.1.refs_0_.digit_ref
  31.4 0.6 copy-done.5
  32.1 0.7 pad_maximum_fusion.5
  32.8 6.3 %all-to-all-done.merged_ref = bf16[8,32,640]{2,1,0:T(8,128)(2,1)S(1)} async-done(((bf16[8,32,640]{2,1,0:T(8,128)(2,1)}), bf16[8,32,640]{2,1,0:T(8,128)(2,1)S(1)}, u32[]{:S(2)}, u32[]{:S(2)}) %all-to-all-start) | async-done | bytes 327712 | tf_op jit(solution)/shard_map/all_to_all | solution.py:492
  39.1 0.7 copy-done.8
  39.8 10.7 %ragged_attention.1.refs_1_ = bf16[8,32,512]{2,1,0:T(8,128)(2,1)} custom-call(s32[1,32]{1,0:T(1,128)} %length_ref.1, bf16[8,32,640]{2,1,0:T(8,128)(2,1)} %copy-done.8, f32[32,128]{1,0:T(8,128)} %get-tuple-element.36.cos_ref, f32[32,128]{1,0:T(8,128)} %get-tuple-element.37.sin_ref, f32[1,128]{1,0:T(1,128)} %bitcast.56, f32[1,128]{1,0:T(1,128)} %bitcast.57, ...), custom_call_target="tpu_custom_call" | custom-call | bytes 104857600 | tf_op jit(solution)/shard_map/ragged_attention/pallas_call | solution.py:99
  50.6 3.4 %all-to-all-start.1 = ((bf16[8,32,512]{2,1,0:T(8,128)(2,1)}), bf16[8,32,512]{2,1,0:T(8,128)(2,1)S(1)}, u32[]{:S(2)}, u32[]{:S(2)}) async-start(bf16[8,32,512]{2,1,0:T(8,128)(2,1)} %ragged_attention.1.refs_1_), calls=%async_computation.1 | async-start | bytes 524288 | tf_op jit(solution)/shard_map/all_to_all | solution.py:500
  54.0 1.0 copy-done.2
  55.0 1.6 %copy-done.3 = bf16[512,2048]{1,0:T(8,128)(2,1)S(1)} copy-done((bf16[512,2048]{1,0:T(8,128)(2,1)S(1)}, bf16[512,2048]{1,0:T(8,128)(2,1)}, u32[]{:S(2)}) %copy-start.3) | copy-done | bytes 2097176
  56.7 5.5 %all-to-all-done.1.feature_ref = bf16[8,32,512]{2,1,0:T(8,128)(2,1)S(1)} async-done(((bf16[8,32,512]{2,1,0:T(8,128)(2,1)}), bf16[8,32,512]{2,1,0:T(8,128)(2,1)S(1)}, u32[]{:S(2)}, u32[]{:S(2)}) %all-to-all-start.1) | async-done | bytes 262176 | tf_op jit(solution)/shard_map/all_to_all | solution.py:500
  62.3 1.2 output_projection.1
  63.5 0.6 collective-permute-start.9
  64.2 1.4 %collective-permute-start.13 = (bf16[32,1024]{1,0:T(8,128)(2,1)S(1)}, bf16[32,1024]{1,0:T(8,128)(2,1)S(1)}, u32[]{:S(2)}, u32[]{:S(2)}) collective-permute-start(bf16[32,1024]{1,0:T(8,128)(2,1)S(1)} %get-tuple-element.24), channel_id=1, source_target_pairs={{4,0},{8,4},{12,8},{14,12},{10,14},{6,10},{2,6},{0,2},{5,1},{9,5},... | collective-permute-start | bytes 196616 | tf_op jit(solution)/shard_map/ppermute | solution.py:48
  65.7 2.6 %collective-permute-done.9 = bf16[32,1024]{1,0:T(8,128)(2,1)S(1)} collective-permute-done((bf16[32,1024]{1,0:T(8,128)(2,1)S(1)}, bf16[32,1024]{1,0:T(8,128)(2,1)S(1)}, u32[]{:S(2)}, u32[]{:S(2)}) %collective-permute-start.9) | collective-permute-done | bytes 65568 | tf_op jit(solution)/shard_map/ppermute | solution.py:45
  68.4 0.9 collective-permute-start.10
  69.3 1.3 collective-permute-start.14
  70.6 3.6 %collective-permute-done.10 = bf16[32,2048]{1,0:T(8,128)(2,1)S(1)} collective-permute-done((bf16[32,2048]{1,0:T(8,128)(2,1)S(1)}, bf16[32,2048]{1,0:T(8,128)(2,1)S(1)}, u32[]{:S(2)}, u32[]{:S(2)}) %collective-permute-start.10) | collective-permute-done | bytes 131104 | tf_op jit(solution)/shard_map/ppermute | solution.py:45
  74.2 1.1 collective-permute-start.11
  75.4 1.0 collective-permute-start.15
  76.4 2.9 %collective-permute-done.11.refs_1_ = bf16[32,2048]{1,0:T(8,128)(2,1)S(1)} collective-permute-done((bf16[32,2048]{1,0:T(8,128)(2,1)S(1)}, bf16[32,2048]{1,0:T(8,128)(2,1)S(1)}, u32[]{:S(2)}, u32[]{:S(2)}) %collective-permute-start.11) | collective-permute-done | bytes 131104 | tf_op jit(solution)/shard_map/ppermute | solution.py:45
  79.3 0.7 fusion.7
  80.0 1.1 collective-permute-start.12
  81.0 0.7 fusion.5
  81.7 0.9 collective-permute-start.16
  82.7 2.8 %copy-done = bf16[1,2048,1536]{2,1,0:T(8,128)(2,1)S(1)} copy-done((bf16[1,2048,1536]{2,1,0:T(8,128)(2,1)S(1)}, bf16[1,2048,1536]{2,1,0:T(8,128)(2,1)}, u32[]{:S(2)}) %copy-start) | copy-done | bytes 6291480
  85.9 1.1 collective-permute-done.16.down_ref
  87.0 1.1 residual_norm.1
  88.2 0.5 collective-permute-start.18
  88.7 1.6 %collective-permute-start.17 = (bf16[32,2176]{1,0:T(8,128)(2,1)S(1)}, bf16[32,2176]{1,0:T(8,128)(2,1)S(1)}, u32[]{:S(2)}, u32[]{:S(2)}) collective-permute-start(bf16[32,2176]{1,0:T(8,128)(2,1)S(1)} %get-tuple-element.26), channel_id=1, source_target_pairs={{4,0},{8,4},{12,8},{14,12},{10,14},{6,10},{2,6},{0,2},{5,1},{9,5},... | collective-permute-start | bytes 417800 | tf_op jit(solution)/shard_map/ppermute | solution.py:48
  90.3 3.4 %collective-permute-done.18 = bf16[32,2176]{1,0:T(8,128)(2,1)S(1)} collective-permute-done((bf16[32,2176]{1,0:T(8,128)(2,1)S(1)}, bf16[32,2176]{1,0:T(8,128)(2,1)S(1)}, u32[]{:S(2)}, u32[]{:S(2)}) %collective-permute-start.18) | collective-permute-done | bytes 139296 | tf_op jit(solution)/shard_map/ppermute | solution.py:45
  93.7 1.1 collective-permute-start.20
  94.8 0.9 collective-permute-start.19
  95.7 2.8 %load_gate_up.3.refs_1_ = bf16[2048,1536]{1,0:T(8,128)(2,1)S(1)} custom-call(bf16[2048,1536]{1,0:T(8,128)(2,1)} %collective-permute-done.8.refs_1_.refs_0_, bf16[32,2176]{1,0:T(8,128)(2,1)S(1)} %collective-permute-done.17.refs_1_), custom_call_target="tpu_custom_call" | custom-call | bytes 104857600 | tf_op jit(solution)/shard_map/load_gate_up/pallas_call | solution.py:99
  98.7 1.3 collective-permute-start.22
  100.1 0.7 collective-permute-start.21
  101.0 2.9 %collective-permute-done.22 = bf16[32,2176]{1,0:T(8,128)(2,1)S(1)} collective-permute-done((bf16[32,2176]{1,0:T(8,128)(2,1)S(1)}, bf16[32,2176]{1,0:T(8,128)(2,1)S(1)}, u32[]{:S(2)}, u32[]{:S(2)}) %collective-permute-start.22) | collective-permute-done | bytes 139296 | tf_op jit(solution)/shard_map/ppermute | solution.py:45
  103.9 1.2 collective-permute-start.23
  105.1 1.0 collective-permute-start.24
  106.2 2.0 %collective-permute-done.23 = bf16[16,2176]{1,0:T(8,128)(2,1)S(1)} collective-permute-done((bf16[16,2176]{1,0:T(8,128)(2,1)S(1)}, bf16[16,2176]{1,0:T(8,128)(2,1)S(1)}, u32[]{:S(2)}, u32[]{:S(2)}) %collective-permute-start.23) | collective-permute-done | bytes 69664 | tf_op jit(solution)/shard_map/ppermute | solution.py:45
  108.2 1.5 %collective-permute-done.24 = bf16[16,2176]{1,0:T(8,128)(2,1)S(1)} collective-permute-done((bf16[16,2176]{1,0:T(8,128)(2,1)S(1)}, bf16[16,2176]{1,0:T(8,128)(2,1)S(1)}, u32[]{:S(2)}, u32[]{:S(2)}) %collective-permute-start.24) | collective-permute-done | bytes 69664 | tf_op jit(solution)/shard_map/ppermute | solution.py:48
  109.7 5.7 %experts.1 = (f32[32,2048]{1,0:T(8,128)S(1)}, bf16[32,1024]{1,0:T(8,128)(2,1)S(1)}, bf16[32,1024]{1,0:T(8,128)(2,1)S(1)}, f32[3,32,2048]{2,1,0:T(8,128)S(1)}, f32[3,32,2048]{2,1,0:T(8,128)S(1)}) custom-call(s32[1,2]{1,0:T(1,128)S(1)} %fusion.15.slot_ref, bf16[256,2176]{1,0:T(8,128)(2,1)S(1)} %constant_dynamic-update-slice_fusion.5.held, ...), custom_call_target="tpu_custom_call" | custom-call | bytes 104857600 | tf_op jit(solution)/shard_map/experts/pallas_call | solution.py:99
  115.7 1.7 %collective-permute-start.30 = (bf16[32,1024]{1,0:T(8,128)(2,1)S(1)}, bf16[32,1024]{1,0:T(8,128)(2,1)S(1)}, u32[]{:S(2)}, u32[]{:S(2)}) collective-permute-start(bf16[32,1024]{1,0:T(8,128)(2,1)S(1)} %get-tuple-element.32), channel_id=1, source_target_pairs={{4,0},{8,4},{12,8},{14,12},{10,14},{6,10},{2,6},{0,2},{5,1},{9,5},... | collective-permute-start | bytes 196616 | tf_op jit(solution)/shard_map/ppermute | solution.py:48
  117.5 2.2 %collective-permute-done.26 = bf16[32,1024]{1,0:T(8,128)(2,1)S(1)} collective-permute-done((bf16[32,1024]{1,0:T(8,128)(2,1)S(1)}, bf16[32,1024]{1,0:T(8,128)(2,1)S(1)}, u32[]{:S(2)}, u32[]{:S(2)}) %collective-permute-start.26) | collective-permute-done | bytes 65568 | tf_op jit(solution)/shard_map/ppermute | solution.py:45
  120.1 1.8 %collective-permute-start.31 = (bf16[32,2048]{1,0:T(8,128)(2,1)S(1)}, bf16[32,2048]{1,0:T(8,128)(2,1)S(1)}, u32[]{:S(2)}, u32[]{:S(2)}) collective-permute-start(bf16[32,2048]{1,0:T(8,128)(2,1)S(1)} %pad_maximum_fusion.4), channel_id=1, source_target_pairs={{4,0},{8,4},{12,8},{14,12},{10,14},{6,10},{2,6},{0,2},{5,1},{9,5},... | collective-permute-start | bytes 393224 | tf_op jit(solution)/shard_map/ppermute | solution.py:48
  121.9 2.8 %collective-permute-done.27 = bf16[32,2048]{1,0:T(8,128)(2,1)S(1)} collective-permute-done((bf16[32,2048]{1,0:T(8,128)(2,1)S(1)}, bf16[32,2048]{1,0:T(8,128)(2,1)S(1)}, u32[]{:S(2)}, u32[]{:S(2)}) %collective-permute-start.27) | collective-permute-done | bytes 131104 | tf_op jit(solution)/shard_map/ppermute | solution.py:45
  125.2 1.8 %collective-permute-start.32 = (bf16[32,2048]{1,0:T(8,128)(2,1)S(1)}, bf16[32,2048]{1,0:T(8,128)(2,1)S(1)}, u32[]{:S(2)}, u32[]{:S(2)}) collective-permute-start(bf16[32,2048]{1,0:T(8,128)(2,1)S(1)} %fusion), channel_id=1, source_target_pairs={{4,0},{8,4},{12,8},{14,12},{10,14},{6,10},{2,6},{0,2},{5,1},{9,5},... | collective-permute-start | bytes 393224 | tf_op jit(solution)/shard_map/ppermute | solution.py:48
  127.0 2.8 %collective-permute-done.28 = bf16[32,2048]{1,0:T(8,128)(2,1)S(1)} collective-permute-done((bf16[32,2048]{1,0:T(8,128)(2,1)S(1)}, bf16[32,2048]{1,0:T(8,128)(2,1)S(1)}, u32[]{:S(2)}, u32[]{:S(2)}) %collective-permute-start.28) | collective-permute-done | bytes 131104 | tf_op jit(solution)/shard_map/ppermute | solution.py:45
  130.2 1.8 %collective-permute-start.33 = (bf16[32,2048]{1,0:T(8,128)(2,1)S(1)}, bf16[32,2048]{1,0:T(8,128)(2,1)S(1)}, u32[]{:S(2)}, u32[]{:S(2)}) collective-permute-start(bf16[32,2048]{1,0:T(8,128)(2,1)S(1)} %fusion.1), channel_id=1, source_target_pairs={{4,0},{8,4},{12,8},{14,12},{10,14},{6,10},{2,6},{0,2},{5,1},{9,5},... | collective-permute-start | bytes 393224 | tf_op jit(solution)/shard_map/ppermute | solution.py:48
  132.0 2.8 %collective-permute-done.29 = bf16[32,2048]{1,0:T(8,128)(2,1)S(1)} collective-permute-done((bf16[32,2048]{1,0:T(8,128)(2,1)S(1)}, bf16[32,2048]{1,0:T(8,128)(2,1)S(1)}, u32[]{:S(2)}, u32[]{:S(2)}) %collective-permute-start.29) | collective-permute-done | bytes 131104 | tf_op jit(solution)/shard_map/ppermute | solution.py:45
  135.3 0.7 add_convert_fusion
  (102 shorter events, 5.4 us)
Async XLA Ops:
  0.0 39.1 %collective-permute-start.8 = (bf16[2048,1536]{1,0:T(8,128)(2,1)}, bf16[2048,1536]{1,0:T(8,128)(2,1)}, u32[]{:S(2)}, u32[]{:S(2)}) collective-permute-start(bf16[2048,1536]{1,0:T(8,128)(2,1)} %bitcast.49), channel_id=1, source_target_pairs={{0,1},{1,0},{2,3},{3,2},{4,5},{5,4},{6,7},{7,6},{8,9},{9,8},{10,11... | collective-permute-start | bytes 18874376 | tf_op jit(solution)/shard_map/ppermute | solution.py:450
  0.5 6.9 %collective-permute-start.1 = (bf16[32,2048]{1,0:T(8,128)(2,1)}, bf16[32,2048]{1,0:T(8,128)(2,1)S(1)}, u32[]{:S(2)}, u32[]{:S(2)}) collective-permute-start(bf16[32,2048]{1,0:T(8,128)(2,1)} %hidden_ref.1), channel_id=1, source_target_pairs={{0,4},{4,8},{8,12},{12,14},{14,10},{10,6},{6,2},{2,0},{1,5},{5,9},... | collective-permute-start | bytes 393224 | tf_op jit(solution)/shard_map/ppermute | solution.py:45
  3.0 6.1 %collective-permute-start = (bf16[32,2048]{1,0:T(8,128)(2,1)}, bf16[32,2048]{1,0:T(8,128)(2,1)S(1)}, u32[]{:S(2)}, u32[]{:S(2)}) collective-permute-start(bf16[32,2048]{1,0:T(8,128)(2,1)} %hidden_ref.1), channel_id=1, source_target_pairs={{4,0},{8,4},{12,8},{14,12},{10,14},{6,10},{2,6},{0,2},{5,1},{9,5},... | collective-permute-start | bytes 393224 | tf_op jit(solution)/shard_map/ppermute | solution.py:48
  7.3 5.3 %collective-permute-start.3 = (bf16[32,2048]{1,0:T(8,128)(2,1)S(1)}, bf16[32,2048]{1,0:T(8,128)(2,1)S(1)}, u32[]{:S(2)}, u32[]{:S(2)}) collective-permute-start(bf16[32,2048]{1,0:T(8,128)(2,1)S(1)} %collective-permute-done.1), channel_id=1, source_target_pairs={{0,4},{4,8},{8,12},{12,14},{14,10},{10,6},{6,2},{2,0},{1,5},{5,9},... | collective-permute-start | bytes 393224 | tf_op jit(solution)/shard_map/ppermute | solution.py:45
  9.2 5.1 %collective-permute-start.2 = (bf16[32,2048]{1,0:T(8,128)(2,1)S(1)}, bf16[32,2048]{1,0:T(8,128)(2,1)S(1)}, u32[]{:S(2)}, u32[]{:S(2)}) collective-permute-start(bf16[32,2048]{1,0:T(8,128)(2,1)S(1)} %collective-permute-done.refs_1_), channel_id=1, source_target_pairs={{4,0},{8,4},{12,8},{14,12},{10,14},{6,10},{2,6},{0,2},{5,1},{9,5},... | collective-permute-start | bytes 393224 | tf_op jit(solution)/shard_map/ppermute | solution.py:48
  11.1 8.6 %copy-start.9 = (f32[2048]{0:T(1024)S(1)}, f32[2048]{0:T(1024)}, u32[]{:S(2)}) copy-start(f32[2048]{0:T(1024)} %param.22) | copy-start | bytes 24580
  12.7 5.0 %collective-permute-start.5 = (bf16[32,2048]{1,0:T(8,128)(2,1)S(1)}, bf16[32,2048]{1,0:T(8,128)(2,1)S(1)}, u32[]{:S(2)}, u32[]{:S(2)}) collective-permute-start(bf16[32,2048]{1,0:T(8,128)(2,1)S(1)} %collective-permute-done.3), channel_id=1, source_target_pairs={{0,4},{4,8},{8,12},{12,14},{14,10},{10,6},{6,2},{2,0},{1,5},{5,9},... | collective-permute-start | bytes 393224 | tf_op jit(solution)/shard_map/ppermute | solution.py:45
  14.3 5.0 %collective-permute-start.4 = (bf16[32,2048]{1,0:T(8,128)(2,1)S(1)}, bf16[32,2048]{1,0:T(8,128)(2,1)S(1)}, u32[]{:S(2)}, u32[]{:S(2)}) collective-permute-start(bf16[32,2048]{1,0:T(8,128)(2,1)S(1)} %collective-permute-done.2), channel_id=1, source_target_pairs={{4,0},{8,4},{12,8},{14,12},{10,14},{6,10},{2,6},{0,2},{5,1},{9,5},... | collective-permute-start | bytes 393224 | tf_op jit(solution)/shard_map/ppermute | solution.py:48
  17.7 4.3 %collective-permute-start.6 = (bf16[16,2048]{1,0:T(8,128)(2,1)S(1)}, bf16[16,2048]{1,0:T(8,128)(2,1)S(1)}, u32[]{:S(2)}, u32[]{:S(2)}) collective-permute-start(bf16[16,2048]{1,0:T(8,128)(2,1)S(1)} %slice.100), channel_id=1, source_target_pairs={{0,4},{4,8},{8,12},{12,14},{14,10},{10,6},{6,2},{2,0},{1,5},{5,9},... | collective-permute-start | bytes 196616 | tf_op jit(solution)/shard_map/ppermute | solution.py:45
  19.3 4.3 %collective-permute-start.7 = (bf16[16,2048]{1,0:T(8,128)(2,1)S(1)}, bf16[16,2048]{1,0:T(8,128)(2,1)S(1)}, u32[]{:S(2)}, u32[]{:S(2)}) collective-permute-start(bf16[16,2048]{1,0:T(8,128)(2,1)S(1)} %slice.101), channel_id=1, source_target_pairs={{4,0},{8,4},{12,8},{14,12},{10,14},{6,10},{2,6},{0,2},{5,1},{9,5},... | collective-permute-start | bytes 196616 | tf_op jit(solution)/shard_map/ppermute | solution.py:48
  23.6 6.8 %copy-start.11 = (s32[32,8]{0,1:T(8,128)S(1)}, s32[32,8]{0,1:T(8,128)}, u32[]{:S(2)}) copy-start(s32[32,8]{0,1:T(8,128)} %param.19) | copy-start | bytes 3076
  23.6 6.9 %copy-start.12 = (s32[32,8]{0,1:T(8,128)S(1)}, s32[32,8]{0,1:T(8,128)}, u32[]{:S(2)}) copy-start(s32[32,8]{0,1:T(8,128)} %param.20) | copy-start | bytes 3076
  23.6 7.0 %copy-start.7 = (s32[16]{0:T(128)S(1)}, s32[16]{0:T(128)}, u32[]{:S(2)}) copy-start(s32[16]{0:T(128)} %param.21) | copy-start | bytes 196
  23.6 8.3 %copy-start.13 = (s32[1,32]{1,0:T(1,128)S(1)}, s32[1,32]{1,0:T(1,128)}, u32[]{:S(2)}) copy-start(s32[1,32]{1,0:T(1,128)} %length_ref.1) | copy-start | bytes 388
  25.6 13.5 %all-to-all-start = ((bf16[8,32,640]{2,1,0:T(8,128)(2,1)}), bf16[8,32,640]{2,1,0:T(8,128)(2,1)S(1)}, u32[]{:S(2)}, u32[]{:S(2)}) async-start(bf16[8,32,640]{2,1,0:T(8,128)(2,1)} %project.1), calls=%async_computation | async-start | bytes 655360 | tf_op jit(solution)/shard_map/all_to_all | solution.py:492
  31.4 0.6 copy-start.5
  39.1 0.7 copy-start.8
  50.6 11.7 %all-to-all-start.1 = ((bf16[8,32,512]{2,1,0:T(8,128)(2,1)}), bf16[8,32,512]{2,1,0:T(8,128)(2,1)S(1)}, u32[]{:S(2)}, u32[]{:S(2)}) async-start(bf16[8,32,512]{2,1,0:T(8,128)(2,1)} %ragged_attention.1.refs_1_), calls=%async_computation.1 | async-start | bytes 524288 | tf_op jit(solution)/shard_map/all_to_all | solution.py:500
  54.0 1.0 copy-start.2
  55.0 1.6 %copy-start.3 = (bf16[512,2048]{1,0:T(8,128)(2,1)S(1)}, bf16[512,2048]{1,0:T(8,128)(2,1)}, u32[]{:S(2)}) copy-start(bf16[512,2048]{1,0:T(8,128)(2,1)} %refs_0_.3) | copy-start | bytes 6291460
  63.5 4.8 %collective-permute-start.9 = (bf16[32,1024]{1,0:T(8,128)(2,1)S(1)}, bf16[32,1024]{1,0:T(8,128)(2,1)S(1)}, u32[]{:S(2)}, u32[]{:S(2)}) collective-permute-start(bf16[32,1024]{1,0:T(8,128)(2,1)S(1)} %get-tuple-element.22), channel_id=1, source_target_pairs={{0,4},{4,8},{8,12},{12,14},{14,10},{10,6},{6,2},{2,0},{1,5},{5,9},... | collective-permute-start | bytes 196616 | tf_op jit(solution)/shard_map/ppermute | solution.py:45
  64.2 5.1 %collective-permute-start.13 = (bf16[32,1024]{1,0:T(8,128)(2,1)S(1)}, bf16[32,1024]{1,0:T(8,128)(2,1)S(1)}, u32[]{:S(2)}, u32[]{:S(2)}) collective-permute-start(bf16[32,1024]{1,0:T(8,128)(2,1)S(1)} %get-tuple-element.24), channel_id=1, source_target_pairs={{4,0},{8,4},{12,8},{14,12},{10,14},{6,10},{2,6},{0,2},{5,1},{9,5},... | collective-permute-start | bytes 196616 | tf_op jit(solution)/shard_map/ppermute | solution.py:48
  68.3 14.3 %copy-start.1 = (bf16[1,768,2048]{2,1,0:T(8,128)(2,1)S(1)}, bf16[1,768,2048]{2,1,0:T(8,128)(2,1)}, u32[]{:S(2)}) copy-start(bf16[1,768,2048]{2,1,0:T(8,128)(2,1)} %param.29) | copy-start | bytes 9437188
  68.4 5.9 %collective-permute-start.10 = (bf16[32,2048]{1,0:T(8,128)(2,1)S(1)}, bf16[32,2048]{1,0:T(8,128)(2,1)S(1)}, u32[]{:S(2)}, u32[]{:S(2)}) collective-permute-start(bf16[32,2048]{1,0:T(8,128)(2,1)S(1)} %pad_maximum_fusion.1), channel_id=1, source_target_pairs={{0,4},{4,8},{8,12},{12,14},{14,10},{10,6},{6,2},{2,0},{1,5},{5,9},... | collective-permute-start | bytes 393224 | tf_op jit(solution)/shard_map/ppermute | solution.py:45
  69.3 6.1 %collective-permute-start.14 = (bf16[32,2048]{1,0:T(8,128)(2,1)S(1)}, bf16[32,2048]{1,0:T(8,128)(2,1)S(1)}, u32[]{:S(2)}, u32[]{:S(2)}) collective-permute-start(bf16[32,2048]{1,0:T(8,128)(2,1)S(1)} %pad_maximum_fusion.2), channel_id=1, source_target_pairs={{4,0},{8,4},{12,8},{14,12},{10,14},{6,10},{2,6},{0,2},{5,1},{9,5},... | collective-permute-start | bytes 393224 | tf_op jit(solution)/shard_map/ppermute | solution.py:48
  74.2 5.0 %collective-permute-start.11 = (bf16[32,2048]{1,0:T(8,128)(2,1)S(1)}, bf16[32,2048]{1,0:T(8,128)(2,1)S(1)}, u32[]{:S(2)}, u32[]{:S(2)}) collective-permute-start(bf16[32,2048]{1,0:T(8,128)(2,1)S(1)} %fusion.6), channel_id=1, source_target_pairs={{0,4},{4,8},{8,12},{12,14},{14,10},{10,6},{6,2},{2,0},{1,5},{5,9},... | collective-permute-start | bytes 393224 | tf_op jit(solution)/shard_map/ppermute | solution.py:45
  75.4 5.6 %collective-permute-start.15 = (bf16[32,2048]{1,0:T(8,128)(2,1)S(1)}, bf16[32,2048]{1,0:T(8,128)(2,1)S(1)}, u32[]{:S(2)}, u32[]{:S(2)}) collective-permute-start(bf16[32,2048]{1,0:T(8,128)(2,1)S(1)} %fusion.4), channel_id=1, source_target_pairs={{4,0},{8,4},{12,8},{14,12},{10,14},{6,10},{2,6},{0,2},{5,1},{9,5},... | collective-permute-start | bytes 393224 | tf_op jit(solution)/shard_map/ppermute | solution.py:48
  80.0 6.0 %collective-permute-start.12 = (bf16[32,2048]{1,0:T(8,128)(2,1)}, bf16[32,2048]{1,0:T(8,128)(2,1)}, u32[]{:S(2)}, u32[]{:S(2)}) collective-permute-start(bf16[32,2048]{1,0:T(8,128)(2,1)} %fusion.7), channel_id=1, source_target_pairs={{0,4},{4,8},{8,12},{12,14},{14,10},{10,6},{6,2},{2,0},{1,5},{5,9},... | collective-permute-start | bytes 393224 | tf_op jit(solution)/shard_map/ppermute | solution.py:45
  81.7 5.3 %collective-permute-start.16 = (bf16[32,2048]{1,0:T(8,128)(2,1)}, bf16[32,2048]{1,0:T(8,128)(2,1)}, u32[]{:S(2)}, u32[]{:S(2)}) collective-permute-start(bf16[32,2048]{1,0:T(8,128)(2,1)} %fusion.5), channel_id=1, source_target_pairs={{4,0},{8,4},{12,8},{14,12},{10,14},{6,10},{2,6},{0,2},{5,1},{9,5},... | collective-permute-start | bytes 393224 | tf_op jit(solution)/shard_map/ppermute | solution.py:48
  82.7 27.0 %collective-permute-start.25 = (bf16[768,2048]{1,0:T(8,128)(2,1)S(1)}, bf16[768,2048]{1,0:T(8,128)(2,1)S(1)}, u32[]{:S(2)}, u32[]{:S(2)}) collective-permute-start(bf16[768,2048]{1,0:T(8,128)(2,1)S(1)} %bitcast.51), channel_id=1, source_target_pairs={{0,1},{1,0},{2,3},{3,2},{4,5},{5,4},{6,7},{7,6},{8,9},{9,8},{10,11... | collective-permute-start | bytes 9437192 | tf_op jit(solution)/shard_map/ppermute | solution.py:450
  82.7 2.8 %copy-start = (bf16[1,2048,1536]{2,1,0:T(8,128)(2,1)S(1)}, bf16[1,2048,1536]{2,1,0:T(8,128)(2,1)}, u32[]{:S(2)}) copy-start(bf16[1,2048,1536]{2,1,0:T(8,128)(2,1)} %param.28) | copy-start | bytes 18874372
  85.5 1.5 %copy-start.10 = (f32[2048]{0:T(1024)S(1)}, f32[2048]{0:T(1024)}, u32[]{:S(2)}) copy-start(f32[2048]{0:T(1024)} %param.23) | copy-start | bytes 24580
  85.5 1.6 %copy-start.4 = (bf16[32,2048]{1,0:T(8,128)(2,1)S(1)}, bf16[32,2048]{1,0:T(8,128)(2,1)}, u32[]{:S(2)}) copy-start(bf16[32,2048]{1,0:T(8,128)(2,1)} %hidden_ref.1) | copy-start | bytes 393220
  85.5 1.6 %copy-start.6 = (bf16[32,128]{1,0:T(8,128)(2,1)S(1)}, bf16[32,128]{1,0:T(8,128)(2,1)}, u32[]{:S(2)}) copy-start(bf16[32,128]{1,0:T(8,128)(2,1)} %copy-done.5) | copy-start | bytes 24580
  88.2 5.5 %collective-permute-start.18 = (bf16[32,2176]{1,0:T(8,128)(2,1)S(1)}, bf16[32,2176]{1,0:T(8,128)(2,1)S(1)}, u32[]{:S(2)}, u32[]{:S(2)}) collective-permute-start(bf16[32,2176]{1,0:T(8,128)(2,1)S(1)} %get-tuple-element.26), channel_id=1, source_target_pairs={{0,4},{4,8},{8,12},{12,14},{14,10},{10,6},{6,2},{2,0},{1,5},{5,9},... | collective-permute-start | bytes 417800 | tf_op jit(solution)/shard_map/ppermute | solution.py:45
  88.7 6.1 %collective-permute-start.17 = (bf16[32,2176]{1,0:T(8,128)(2,1)S(1)}, bf16[32,2176]{1,0:T(8,128)(2,1)S(1)}, u32[]{:S(2)}, u32[]{:S(2)}) collective-permute-start(bf16[32,2176]{1,0:T(8,128)(2,1)S(1)} %get-tuple-element.26), channel_id=1, source_target_pairs={{4,0},{8,4},{12,8},{14,12},{10,14},{6,10},{2,6},{0,2},{5,1},{9,5},... | collective-permute-start | bytes 417800 | tf_op jit(solution)/shard_map/ppermute | solution.py:48
  93.7 5.1 %collective-permute-start.20 = (bf16[32,2176]{1,0:T(8,128)(2,1)S(1)}, bf16[32,2176]{1,0:T(8,128)(2,1)S(1)}, u32[]{:S(2)}, u32[]{:S(2)}) collective-permute-start(bf16[32,2176]{1,0:T(8,128)(2,1)S(1)} %collective-permute-done.18), channel_id=1, source_target_pairs={{0,4},{4,8},{8,12},{12,14},{14,10},{10,6},{6,2},{2,0},{1,5},{5,9},... | collective-permute-start | bytes 417800 | tf_op jit(solution)/shard_map/ppermute | solution.py:45
  94.8 5.3 %collective-permute-start.19 = (bf16[32,2176]{1,0:T(8,128)(2,1)S(1)}, bf16[32,2176]{1,0:T(8,128)(2,1)S(1)}, u32[]{:S(2)}, u32[]{:S(2)}) collective-permute-start(bf16[32,2176]{1,0:T(8,128)(2,1)S(1)} %collective-permute-done.17.refs_1_), channel_id=1, source_target_pairs={{4,0},{8,4},{12,8},{14,12},{10,14},{6,10},{2,6},{0,2},{5,1},{9,5},... | collective-permute-start | bytes 417800 | tf_op jit(solution)/shard_map/ppermute | solution.py:48
  98.7 5.2 %collective-permute-start.22 = (bf16[32,2176]{1,0:T(8,128)(2,1)S(1)}, bf16[32,2176]{1,0:T(8,128)(2,1)S(1)}, u32[]{:S(2)}, u32[]{:S(2)}) collective-permute-start(bf16[32,2176]{1,0:T(8,128)(2,1)S(1)} %collective-permute-done.20), channel_id=1, source_target_pairs={{0,4},{4,8},{8,12},{12,14},{14,10},{10,6},{6,2},{2,0},{1,5},{5,9},... | collective-permute-start | bytes 417800 | tf_op jit(solution)/shard_map/ppermute | solution.py:45
  100.1 5.1 %collective-permute-start.21 = (bf16[32,2176]{1,0:T(8,128)(2,1)S(1)}, bf16[32,2176]{1,0:T(8,128)(2,1)S(1)}, u32[]{:S(2)}, u32[]{:S(2)}) collective-permute-start(bf16[32,2176]{1,0:T(8,128)(2,1)S(1)} %collective-permute-done.19.refs_1_), channel_id=1, source_target_pairs={{4,0},{8,4},{12,8},{14,12},{10,14},{6,10},{2,6},{0,2},{5,1},{9,5},... | collective-permute-start | bytes 417800 | tf_op jit(solution)/shard_map/ppermute | solution.py:48
  103.9 4.3 %collective-permute-start.23 = (bf16[16,2176]{1,0:T(8,128)(2,1)S(1)}, bf16[16,2176]{1,0:T(8,128)(2,1)S(1)}, u32[]{:S(2)}, u32[]{:S(2)}) collective-permute-start(bf16[16,2176]{1,0:T(8,128)(2,1)S(1)} %slice.106), channel_id=1, source_target_pairs={{0,4},{4,8},{8,12},{12,14},{14,10},{10,6},{6,2},{2,0},{1,5},{5,9},... | collective-permute-start | bytes 208904 | tf_op jit(solution)/shard_map/ppermute | solution.py:45
  105.1 4.5 %collective-permute-start.24 = (bf16[16,2176]{1,0:T(8,128)(2,1)S(1)}, bf16[16,2176]{1,0:T(8,128)(2,1)S(1)}, u32[]{:S(2)}, u32[]{:S(2)}) collective-permute-start(bf16[16,2176]{1,0:T(8,128)(2,1)S(1)} %slice.107), channel_id=1, source_target_pairs={{4,0},{8,4},{12,8},{14,12},{10,14},{6,10},{2,6},{0,2},{5,1},{9,5},... | collective-permute-start | bytes 208904 | tf_op jit(solution)/shard_map/ppermute | solution.py:48
  115.4 4.3 %collective-permute-start.26 = (bf16[32,1024]{1,0:T(8,128)(2,1)S(1)}, bf16[32,1024]{1,0:T(8,128)(2,1)S(1)}, u32[]{:S(2)}, u32[]{:S(2)}) collective-permute-start(bf16[32,1024]{1,0:T(8,128)(2,1)S(1)} %get-tuple-element.30), channel_id=1, source_target_pairs={{0,4},{4,8},{8,12},{12,14},{14,10},{10,6},{6,2},{2,0},{1,5},{5,9},... | collective-permute-start | bytes 196616 | tf_op jit(solution)/shard_map/ppermute | solution.py:45
  115.7 4.4 %collective-permute-start.30 = (bf16[32,1024]{1,0:T(8,128)(2,1)S(1)}, bf16[32,1024]{1,0:T(8,128)(2,1)S(1)}, u32[]{:S(2)}, u32[]{:S(2)}) collective-permute-start(bf16[32,1024]{1,0:T(8,128)(2,1)S(1)} %get-tuple-element.32), channel_id=1, source_target_pairs={{4,0},{8,4},{12,8},{14,12},{10,14},{6,10},{2,6},{0,2},{5,1},{9,5},... | collective-permute-start | bytes 196616 | tf_op jit(solution)/shard_map/ppermute | solution.py:48
  119.8 5.0 %collective-permute-start.27 = (bf16[32,2048]{1,0:T(8,128)(2,1)S(1)}, bf16[32,2048]{1,0:T(8,128)(2,1)S(1)}, u32[]{:S(2)}, u32[]{:S(2)}) collective-permute-start(bf16[32,2048]{1,0:T(8,128)(2,1)S(1)} %pad_maximum_fusion.3), channel_id=1, source_target_pairs={{0,4},{4,8},{8,12},{12,14},{14,10},{10,6},{6,2},{2,0},{1,5},{5,9},... | collective-permute-start | bytes 393224 | tf_op jit(solution)/shard_map/ppermute | solution.py:45
  120.1 5.0 %collective-permute-start.31 = (bf16[32,2048]{1,0:T(8,128)(2,1)S(1)}, bf16[32,2048]{1,0:T(8,128)(2,1)S(1)}, u32[]{:S(2)}, u32[]{:S(2)}) collective-permute-start(bf16[32,2048]{1,0:T(8,128)(2,1)S(1)} %pad_maximum_fusion.4), channel_id=1, source_target_pairs={{4,0},{8,4},{12,8},{14,12},{10,14},{6,10},{2,6},{0,2},{5,1},{9,5},... | collective-permute-start | bytes 393224 | tf_op jit(solution)/shard_map/ppermute | solution.py:48
  124.8 5.0 %collective-permute-start.28 = (bf16[32,2048]{1,0:T(8,128)(2,1)S(1)}, bf16[32,2048]{1,0:T(8,128)(2,1)S(1)}, u32[]{:S(2)}, u32[]{:S(2)}) collective-permute-start(bf16[32,2048]{1,0:T(8,128)(2,1)S(1)} %fusion.2), channel_id=1, source_target_pairs={{0,4},{4,8},{8,12},{12,14},{14,10},{10,6},{6,2},{2,0},{1,5},{5,9},... | collective-permute-start | bytes 393224 | tf_op jit(solution)/shard_map/ppermute | solution.py:45
  125.2 5.0 %collective-permute-start.32 = (bf16[32,2048]{1,0:T(8,128)(2,1)S(1)}, bf16[32,2048]{1,0:T(8,128)(2,1)S(1)}, u32[]{:S(2)}, u32[]{:S(2)}) collective-permute-start(bf16[32,2048]{1,0:T(8,128)(2,1)S(1)} %fusion), channel_id=1, source_target_pairs={{4,0},{8,4},{12,8},{14,12},{10,14},{6,10},{2,6},{0,2},{5,1},{9,5},... | collective-permute-start | bytes 393224 | tf_op jit(solution)/shard_map/ppermute | solution.py:48
  129.9 5.0 %collective-permute-start.29 = (bf16[32,2048]{1,0:T(8,128)(2,1)S(1)}, bf16[32,2048]{1,0:T(8,128)(2,1)S(1)}, u32[]{:S(2)}, u32[]{:S(2)}) collective-permute-start(bf16[32,2048]{1,0:T(8,128)(2,1)S(1)} %fusion.3), channel_id=1, source_target_pairs={{0,4},{4,8},{8,12},{12,14},{14,10},{10,6},{6,2},{2,0},{1,5},{5,9},... | collective-permute-start | bytes 393224 | tf_op jit(solution)/shard_map/ppermute | solution.py:45
  130.2 5.0 %collective-permute-start.33 = (bf16[32,2048]{1,0:T(8,128)(2,1)S(1)}, bf16[32,2048]{1,0:T(8,128)(2,1)S(1)}, u32[]{:S(2)}, u32[]{:S(2)}) collective-permute-start(bf16[32,2048]{1,0:T(8,128)(2,1)S(1)} %fusion.1), channel_id=1, source_target_pairs={{4,0},{8,4},{12,8},{14,12},{10,14},{6,10},{2,6},{0,2},{5,1},{9,5},... | collective-permute-start | bytes 393224 | tf_op jit(solution)/shard_map/ppermute | solution.py:48

commit v5 on v4

--- a/solution.py
+++ b/solution.py
@@ -248,8 +248,8 @@
                 for column in (start, inner + start)
             ]
             units[:, start : start + TILE] = (jax.nn.silu(gate) * up).astype(jnp.bfloat16)
-        for start in range(0, width, 2 * TILE):
-            columns = slice(start, start + 2 * TILE)
+        for start in range(0, width, 4 * TILE):
+            columns = slice(start, start + 4 * TILE)
             result = jnp.dot(
                 units[...], downs[shift][:, columns], preferred_element_type=jnp.float32
             )

time: 137 us -> 137 us (level)
  no operation moved by 1% of the time
where the time goes in v5:
time: 137 us; the launch traced here: 136 us
  waiting for transfers between devices  53.7 us (39%)
  starting transfers between devices  42.7 us (31%)
  Pallas kernels  27.7 us (20%)
  local copies, waits for them, and re-layouts  8.16 us (6%)
  other arithmetic  3.24 us (2%)
    ppermute x16, waiting for transfers between devices, ahead(): return lax.ppermute(values, 'dev', self.forward)  37.2 us
    pallas_call x12, Pallas kernels, call(): pl.pallas_call(body, out_shape=outs, in_specs=whole_blocks(ins), out_spec...  27.7 us
    ppermute x16, starting transfers between devices, behind(): return lax.ppermute(values, 'dev', self.backward)  17.2 us
    ppermute x16, starting transfers between devices, ahead(): return lax.ppermute(values, 'dev', self.forward)  16.8 us
    unnamed x42, local copies, waits for them, and re-layouts  7.99 us
    all_to_all x1, waiting for transfers between devices, on_device(): lax.all_to_all(blocks, 'dev', split_axis=0, concat_axis=0, tiled=True)  6.28 us
    all_to_all x1, waiting for transfers between devices, on_device(): lax.all_to_all(attention, 'dev', split_axis=0, concat_axis=0, tiled=True)  5.55 us
    all_to_all x1, starting transfers between devices, on_device(): lax.all_to_all(blocks, 'dev', split_axis=0, concat_axis=0, tiled=True)  4.82 us
  transfers between devices with their start and end apart: 36, of which 21 were waited for; matrix products, arithmetic and copies ran while one was open for 3% of the time, Pallas kernels for 7%

profile of v5, /device:TPU:0, one launch (start us, length us, event | category | flops | bytes accessed | tf_op | source)
XLA Modules:
  0.0 136.0 jit_solution(14209315464027687848)
XLA Ops:
  0.5 2.6 %collective-permute-start.1 = (bf16[32,2048]{1,0:T(8,128)(2,1)}, bf16[32,2048]{1,0:T(8,128)(2,1)S(1)}, u32[]{:S(2)}, u32[]{:S(2)}) collective-permute-start(bf16[32,2048]{1,0:T(8,128)(2,1)} %hidden_ref.1), channel_id=1, source_target_pairs={{0,4},{4,8},{8,12},{12,14},{14,10},{10,6},{6,2},{2,0},{1,5},{5,9},... | collective-permute-start | bytes 393224 | tf_op jit(solution)/shard_map/ppermute | solution.py:45
  3.0 1.0 constant_dynamic-update-slice_fusion.4
  4.1 3.3 %collective-permute-done.1 = bf16[32,2048]{1,0:T(8,128)(2,1)S(1)} collective-permute-done((bf16[32,2048]{1,0:T(8,128)(2,1)}, bf16[32,2048]{1,0:T(8,128)(2,1)S(1)}, u32[]{:S(2)}, u32[]{:S(2)}) %collective-permute-start.1) | collective-permute-done | bytes 131104 | tf_op jit(solution)/shard_map/ppermute | solution.py:45
  7.3 1.8 %collective-permute-start.3 = (bf16[32,2048]{1,0:T(8,128)(2,1)S(1)}, bf16[32,2048]{1,0:T(8,128)(2,1)S(1)}, u32[]{:S(2)}, u32[]{:S(2)}) collective-permute-start(bf16[32,2048]{1,0:T(8,128)(2,1)S(1)} %collective-permute-done.1), channel_id=1, source_target_pairs={{0,4},{4,8},{8,12},{12,14},{14,10},{10,6},{6,2},{2,0},{1,5},{5,9},... | collective-permute-start | bytes 393224 | tf_op jit(solution)/shard_map/ppermute | solution.py:45
  9.4 1.7 %load_project.1.weight_ref = bf16[2048,640]{1,0:T(8,128)(2,1)S(1)} custom-call(bf16[2048,640]{1,0:T(8,128)(2,1)} %refs_0_.2, bf16[32,2048]{1,0:T(8,128)(2,1)S(1)} %collective-permute-done.refs_1_), custom_call_target="tpu_custom_call" | custom-call | bytes 104857600 | tf_op jit(solution)/shard_map/load_project/pallas_call | solution.py:99
  11.2 1.5 %collective-permute-done.3 = bf16[32,2048]{1,0:T(8,128)(2,1)S(1)} collective-permute-done((bf16[32,2048]{1,0:T(8,128)(2,1)S(1)}, bf16[32,2048]{1,0:T(8,128)(2,1)S(1)}, u32[]{:S(2)}, u32[]{:S(2)}) %collective-permute-start.3) | collective-permute-done | bytes 131104 | tf_op jit(solution)/shard_map/ppermute | solution.py:45
  12.7 1.6 %collective-permute-start.5 = (bf16[32,2048]{1,0:T(8,128)(2,1)S(1)}, bf16[32,2048]{1,0:T(8,128)(2,1)S(1)}, u32[]{:S(2)}, u32[]{:S(2)}) collective-permute-start(bf16[32,2048]{1,0:T(8,128)(2,1)S(1)} %collective-permute-done.3), channel_id=1, source_target_pairs={{0,4},{4,8},{8,12},{12,14},{14,10},{10,6},{6,2},{2,0},{1,5},{5,9},... | collective-permute-start | bytes 393224 | tf_op jit(solution)/shard_map/ppermute | solution.py:45
  14.7 2.9 %collective-permute-done.5 = bf16[32,2048]{1,0:T(8,128)(2,1)S(1)} collective-permute-done((bf16[32,2048]{1,0:T(8,128)(2,1)S(1)}, bf16[32,2048]{1,0:T(8,128)(2,1)S(1)}, u32[]{:S(2)}, u32[]{:S(2)}) %collective-permute-start.5) | collective-permute-done | bytes 131104 | tf_op jit(solution)/shard_map/ppermute | solution.py:45
  17.7 1.6 %collective-permute-start.6 = (bf16[16,2048]{1,0:T(8,128)(2,1)S(1)}, bf16[16,2048]{1,0:T(8,128)(2,1)S(1)}, u32[]{:S(2)}, u32[]{:S(2)}) collective-permute-start(bf16[16,2048]{1,0:T(8,128)(2,1)S(1)} %slice.100), channel_id=1, source_target_pairs={{0,4},{4,8},{8,12},{12,14},{14,10},{10,6},{6,2},{2,0},{1,5},{5,9},... | collective-permute-start | bytes 196616 | tf_op jit(solution)/shard_map/ppermute | solution.py:45
  19.8 0.8 project_near.1.near_ref
  20.6 1.3 collective-permute-done.6
  21.9 1.7 %collective-permute-done.7 = bf16[16,2048]{1,0:T(8,128)(2,1)S(1)} collective-permute-done((bf16[16,2048]{1,0:T(8,128)(2,1)S(1)}, bf16[16,2048]{1,0:T(8,128)(2,1)S(1)}, u32[]{:S(2)}, u32[]{:S(2)}) %collective-permute-start.7) | collective-permute-done | bytes 65568 | tf_op jit(solution)/shard_map/ppermute | solution.py:48
  23.7 2.0 %project.1 = bf16[8,32,640]{2,1,0:T(8,128)(2,1)} custom-call(s32[1,8]{1,0:T(1,128)S(1)} %compare_select_fusion.4.owner_ref, bf16[160,640]{1,0:T(8,128)(2,1)S(1)} %project_near.1.near_ref, bf16[96,2048]{1,0:T(8,128)(2,1)S(1)} %pad_maximum_fusion.hidden_ref, f32[8,2048]{1,0:T(8,128)S(1)} %broadcast_in_dim.10.gain_ref, bf16[2048,640]{1,0:T(8,128)(2,1)S(1)} %load_project.1.weight_ref), custom_call_target="tpu_custom_call" | custom-call | bytes 104857600 | tf_op jit(solution)/shard_map/project/pallas_call | solution.py:99
  25.6 4.8 %all-to-all-start = ((bf16[8,32,640]{2,1,0:T(8,128)(2,1)}), bf16[8,32,640]{2,1,0:T(8,128)(2,1)S(1)}, u32[]{:S(2)}, u32[]{:S(2)}) async-start(bf16[8,32,640]{2,1,0:T(8,128)(2,1)} %project.1), calls=%async_computation | async-start | bytes 655360 | tf_op jit(solution)/shard_map/all_to_all | solution.py:492
  30.6 0.8 gate_digits.1.refs_0_.digit_ref
  31.4 0.6 copy-done.5
  32.1 0.7 pad_maximum_fusion.5
  32.8 6.3 %all-to-all-done.merged_ref = bf16[8,32,640]{2,1,0:T(8,128)(2,1)S(1)} async-done(((bf16[8,32,640]{2,1,0:T(8,128)(2,1)}), bf16[8,32,640]{2,1,0:T(8,128)(2,1)S(1)}, u32[]{:S(2)}, u32[]{:S(2)}) %all-to-all-start) | async-done | bytes 327712 | tf_op jit(solution)/shard_map/all_to_all | solution.py:492
  39.1 0.7 copy-done.8
  39.8 10.7 %ragged_attention.1.refs_1_ = bf16[8,32,512]{2,1,0:T(8,128)(2,1)} custom-call(s32[1,32]{1,0:T(1,128)} %length_ref.1, bf16[8,32,640]{2,1,0:T(8,128)(2,1)} %copy-done.8, f32[32,128]{1,0:T(8,128)} %get-tuple-element.36.cos_ref, f32[32,128]{1,0:T(8,128)} %get-tuple-element.37.sin_ref, f32[1,128]{1,0:T(1,128)} %bitcast.56, f32[1,128]{1,0:T(1,128)} %bitcast.57, ...), custom_call_target="tpu_custom_call" | custom-call | bytes 104857600 | tf_op jit(solution)/shard_map/ragged_attention/pallas_call | solution.py:99
  50.6 3.4 %all-to-all-start.1 = ((bf16[8,32,512]{2,1,0:T(8,128)(2,1)}), bf16[8,32,512]{2,1,0:T(8,128)(2,1)S(1)}, u32[]{:S(2)}, u32[]{:S(2)}) async-start(bf16[8,32,512]{2,1,0:T(8,128)(2,1)} %ragged_attention.1.refs_1_), calls=%async_computation.1 | async-start | bytes 524288 | tf_op jit(solution)/shard_map/all_to_all | solution.py:500
  54.0 1.0 copy-done.2
  55.0 1.6 %copy-done.3 = bf16[512,2048]{1,0:T(8,128)(2,1)S(1)} copy-done((bf16[512,2048]{1,0:T(8,128)(2,1)S(1)}, bf16[512,2048]{1,0:T(8,128)(2,1)}, u32[]{:S(2)}) %copy-start.3) | copy-done | bytes 2097176
  56.7 5.5 %all-to-all-done.1.feature_ref = bf16[8,32,512]{2,1,0:T(8,128)(2,1)S(1)} async-done(((bf16[8,32,512]{2,1,0:T(8,128)(2,1)}), bf16[8,32,512]{2,1,0:T(8,128)(2,1)S(1)}, u32[]{:S(2)}, u32[]{:S(2)}) %all-to-all-start.1) | async-done | bytes 262176 | tf_op jit(solution)/shard_map/all_to_all | solution.py:500
  62.3 1.2 output_projection.1
  63.5 0.6 collective-permute-start.9
  64.2 1.4 %collective-permute-start.13 = (bf16[32,1024]{1,0:T(8,128)(2,1)S(1)}, bf16[32,1024]{1,0:T(8,128)(2,1)S(1)}, u32[]{:S(2)}, u32[]{:S(2)}) collective-permute-start(bf16[32,1024]{1,0:T(8,128)(2,1)S(1)} %get-tuple-element.24), channel_id=1, source_target_pairs={{4,0},{8,4},{12,8},{14,12},{10,14},{6,10},{2,6},{0,2},{5,1},{9,5},... | collective-permute-start | bytes 196616 | tf_op jit(solution)/shard_map/ppermute | solution.py:48
  65.7 2.6 %collective-permute-done.9 = bf16[32,1024]{1,0:T(8,128)(2,1)S(1)} collective-permute-done((bf16[32,1024]{1,0:T(8,128)(2,1)S(1)}, bf16[32,1024]{1,0:T(8,128)(2,1)S(1)}, u32[]{:S(2)}, u32[]{:S(2)}) %collective-permute-start.9) | collective-permute-done | bytes 65568 | tf_op jit(solution)/shard_map/ppermute | solution.py:45
  68.4 0.9 collective-permute-start.10
  69.3 1.3 collective-permute-start.14
  70.6 3.6 %collective-permute-done.10 = bf16[32,2048]{1,0:T(8,128)(2,1)S(1)} collective-permute-done((bf16[32,2048]{1,0:T(8,128)(2,1)S(1)}, bf16[32,2048]{1,0:T(8,128)(2,1)S(1)}, u32[]{:S(2)}, u32[]{:S(2)}) %collective-permute-start.10) | collective-permute-done | bytes 131104 | tf_op jit(solution)/shard_map/ppermute | solution.py:45
  74.2 1.1 collective-permute-start.11
  75.4 1.0 collective-permute-start.15
  76.4 2.9 %collective-permute-done.11.refs_1_ = bf16[32,2048]{1,0:T(8,128)(2,1)S(1)} collective-permute-done((bf16[32,2048]{1,0:T(8,128)(2,1)S(1)}, bf16[32,2048]{1,0:T(8,128)(2,1)S(1)}, u32[]{:S(2)}, u32[]{:S(2)}) %collective-permute-start.11) | collective-permute-done | bytes 131104 | tf_op jit(solution)/shard_map/ppermute | solution.py:45
  79.3 0.7 fusion.7
  80.0 1.1 collective-permute-start.12
  81.0 0.7 fusion.5
  81.7 0.9 collective-permute-start.16
  82.7 2.8 %copy-done = bf16[1,2048,1536]{2,1,0:T(8,128)(2,1)S(1)} copy-done((bf16[1,2048,1536]{2,1,0:T(8,128)(2,1)S(1)}, bf16[1,2048,1536]{2,1,0:T(8,128)(2,1)}, u32[]{:S(2)}) %copy-start) | copy-done | bytes 6291480
  85.9 1.1 collective-permute-done.16.down_ref
  87.0 1.1 residual_norm.1
  88.2 0.5 collective-permute-start.18
  88.7 1.6 %collective-permute-start.17 = (bf16[32,2176]{1,0:T(8,128)(2,1)S(1)}, bf16[32,2176]{1,0:T(8,128)(2,1)S(1)}, u32[]{:S(2)}, u32[]{:S(2)}) collective-permute-start(bf16[32,2176]{1,0:T(8,128)(2,1)S(1)} %get-tuple-element.26), channel_id=1, source_target_pairs={{4,0},{8,4},{12,8},{14,12},{10,14},{6,10},{2,6},{0,2},{5,1},{9,5},... | collective-permute-start | bytes 417800 | tf_op jit(solution)/shard_map/ppermute | solution.py:48
  90.3 3.4 %collective-permute-done.18 = bf16[32,2176]{1,0:T(8,128)(2,1)S(1)} collective-permute-done((bf16[32,2176]{1,0:T(8,128)(2,1)S(1)}, bf16[32,2176]{1,0:T(8,128)(2,1)S(1)}, u32[]{:S(2)}, u32[]{:S(2)}) %collective-permute-start.18) | collective-permute-done | bytes 139296 | tf_op jit(solution)/shard_map/ppermute | solution.py:45
  93.7 1.1 collective-permute-start.20
  94.8 0.9 collective-permute-start.19
  95.7 2.8 %load_gate_up.3.refs_1_ = bf16[2048,1536]{1,0:T(8,128)(2,1)S(1)} custom-call(bf16[2048,1536]{1,0:T(8,128)(2,1)} %collective-permute-done.8.refs_1_.refs_0_, bf16[32,2176]{1,0:T(8,128)(2,1)S(1)} %collective-permute-done.17.refs_1_), custom_call_target="tpu_custom_call" | custom-call | bytes 104857600 | tf_op jit(solution)/shard_map/load_gate_up/pallas_call | solution.py:99
  98.7 1.3 collective-permute-start.22
  100.1 0.7 collective-permute-start.21
  101.0 2.9 %collective-permute-done.22 = bf16[32,2176]{1,0:T(8,128)(2,1)S(1)} collective-permute-done((bf16[32,2176]{1,0:T(8,128)(2,1)S(1)}, bf16[32,2176]{1,0:T(8,128)(2,1)S(1)}, u32[]{:S(2)}, u32[]{:S(2)}) %collective-permute-start.22) | collective-permute-done | bytes 139296 | tf_op jit(solution)/shard_map/ppermute | solution.py:45
  103.9 1.2 collective-permute-start.23
  105.1 1.0 collective-permute-start.24
  106.2 2.0 %collective-permute-done.23 = bf16[16,2176]{1,0:T(8,128)(2,1)S(1)} collective-permute-done((bf16[16,2176]{1,0:T(8,128)(2,1)S(1)}, bf16[16,2176]{1,0:T(8,128)(2,1)S(1)}, u32[]{:S(2)}, u32[]{:S(2)}) %collective-permute-start.23) | collective-permute-done | bytes 69664 | tf_op jit(solution)/shard_map/ppermute | solution.py:45
  108.2 1.5 %collective-permute-done.24 = bf16[16,2176]{1,0:T(8,128)(2,1)S(1)} collective-permute-done((bf16[16,2176]{1,0:T(8,128)(2,1)S(1)}, bf16[16,2176]{1,0:T(8,128)(2,1)S(1)}, u32[]{:S(2)}, u32[]{:S(2)}) %collective-permute-start.24) | collective-permute-done | bytes 69664 | tf_op jit(solution)/shard_map/ppermute | solution.py:48
  109.7 5.7 %experts.1 = (f32[32,2048]{1,0:T(8,128)S(1)}, bf16[32,1024]{1,0:T(8,128)(2,1)S(1)}, bf16[32,1024]{1,0:T(8,128)(2,1)S(1)}, f32[3,32,2048]{2,1,0:T(8,128)S(1)}, f32[3,32,2048]{2,1,0:T(8,128)S(1)}) custom-call(s32[1,2]{1,0:T(1,128)S(1)} %fusion.15.slot_ref, bf16[256,2176]{1,0:T(8,128)(2,1)S(1)} %constant_dynamic-update-slice_fusion.5.held, ...), custom_call_target="tpu_custom_call" | custom-call | bytes 104857600 | tf_op jit(solution)/shard_map/experts/pallas_call | solution.py:99
  115.7 1.7 %collective-permute-start.30 = (bf16[32,1024]{1,0:T(8,128)(2,1)S(1)}, bf16[32,1024]{1,0:T(8,128)(2,1)S(1)}, u32[]{:S(2)}, u32[]{:S(2)}) collective-permute-start(bf16[32,1024]{1,0:T(8,128)(2,1)S(1)} %get-tuple-element.32), channel_id=1, source_target_pairs={{4,0},{8,4},{12,8},{14,12},{10,14},{6,10},{2,6},{0,2},{5,1},{9,5},... | collective-permute-start | bytes 196616 | tf_op jit(solution)/shard_map/ppermute | solution.py:48
  117.5 2.2 %collective-permute-done.26 = bf16[32,1024]{1,0:T(8,128)(2,1)S(1)} collective-permute-done((bf16[32,1024]{1,0:T(8,128)(2,1)S(1)}, bf16[32,1024]{1,0:T(8,128)(2,1)S(1)}, u32[]{:S(2)}, u32[]{:S(2)}) %collective-permute-start.26) | collective-permute-done | bytes 65568 | tf_op jit(solution)/shard_map/ppermute | solution.py:45
  120.1 1.8 %collective-permute-start.31 = (bf16[32,2048]{1,0:T(8,128)(2,1)S(1)}, bf16[32,2048]{1,0:T(8,128)(2,1)S(1)}, u32[]{:S(2)}, u32[]{:S(2)}) collective-permute-start(bf16[32,2048]{1,0:T(8,128)(2,1)S(1)} %pad_maximum_fusion.4), channel_id=1, source_target_pairs={{4,0},{8,4},{12,8},{14,12},{10,14},{6,10},{2,6},{0,2},{5,1},{9,5},... | collective-permute-start | bytes 393224 | tf_op jit(solution)/shard_map/ppermute | solution.py:48
  121.9 2.8 %collective-permute-done.27 = bf16[32,2048]{1,0:T(8,128)(2,1)S(1)} collective-permute-done((bf16[32,2048]{1,0:T(8,128)(2,1)S(1)}, bf16[32,2048]{1,0:T(8,128)(2,1)S(1)}, u32[]{:S(2)}, u32[]{:S(2)}) %collective-permute-start.27) | collective-permute-done | bytes 131104 | tf_op jit(solution)/shard_map/ppermute | solution.py:45
  125.2 1.8 %collective-permute-start.32 = (bf16[32,2048]{1,0:T(8,128)(2,1)S(1)}, bf16[32,2048]{1,0:T(8,128)(2,1)S(1)}, u32[]{:S(2)}, u32[]{:S(2)}) collective-permute-start(bf16[32,2048]{1,0:T(8,128)(2,1)S(1)} %fusion), channel_id=1, source_target_pairs={{4,0},{8,4},{12,8},{14,12},{10,14},{6,10},{2,6},{0,2},{5,1},{9,5},... | collective-permute-start | bytes 393224 | tf_op jit(solution)/shard_map/ppermute | solution.py:48
  127.0 2.8 %collective-permute-done.28 = bf16[32,2048]{1,0:T(8,128)(2,1)S(1)} collective-permute-done((bf16[32,2048]{1,0:T(8,128)(2,1)S(1)}, bf16[32,2048]{1,0:T(8,128)(2,1)S(1)}, u32[]{:S(2)}, u32[]{:S(2)}) %collective-permute-start.28) | collective-permute-done | bytes 131104 | tf_op jit(solution)/shard_map/ppermute | solution.py:45
  130.2 1.8 %collective-permute-start.33 = (bf16[32,2048]{1,0:T(8,128)(2,1)S(1)}, bf16[32,2048]{1,0:T(8,128)(2,1)S(1)}, u32[]{:S(2)}, u32[]{:S(2)}) collective-permute-start(bf16[32,2048]{1,0:T(8,128)(2,1)S(1)} %fusion.1), channel_id=1, source_target_pairs={{4,0},{8,4},{12,8},{14,12},{10,14},{6,10},{2,6},{0,2},{5,1},{9,5},... | collective-permute-start | bytes 393224 | tf_op jit(solution)/shard_map/ppermute | solution.py:48
  132.0 2.8 %collective-permute-done.29 = bf16[32,2048]{1,0:T(8,128)(2,1)S(1)} collective-permute-done((bf16[32,2048]{1,0:T(8,128)(2,1)S(1)}, bf16[32,2048]{1,0:T(8,128)(2,1)S(1)}, u32[]{:S(2)}, u32[]{:S(2)}) %collective-permute-start.29) | collective-permute-done | bytes 131104 | tf_op jit(solution)/shard_map/ppermute | solution.py:45
  135.3 0.7 add_convert_fusion
  (102 shorter events, 5.4 us)
Async XLA Ops:
  0.0 39.1 %collective-permute-start.8 = (bf16[2048,1536]{1,0:T(8,128)(2,1)}, bf16[2048,1536]{1,0:T(8,128)(2,1)}, u32[]{:S(2)}, u32[]{:S(2)}) collective-permute-start(bf16[2048,1536]{1,0:T(8,128)(2,1)} %bitcast.49), channel_id=1, source_target_pairs={{0,1},{1,0},{2,3},{3,2},{4,5},{5,4},{6,7},{7,6},{8,9},{9,8},{10,11... | collective-permute-start | bytes 18874376 | tf_op jit(solution)/shard_map/ppermute | solution.py:450
  0.5 6.9 %collective-permute-start.1 = (bf16[32,2048]{1,0:T(8,128)(2,1)}, bf16[32,2048]{1,0:T(8,128)(2,1)S(1)}, u32[]{:S(2)}, u32[]{:S(2)}) collective-permute-start(bf16[32,2048]{1,0:T(8,128)(2,1)} %hidden_ref.1), channel_id=1, source_target_pairs={{0,4},{4,8},{8,12},{12,14},{14,10},{10,6},{6,2},{2,0},{1,5},{5,9},... | collective-permute-start | bytes 393224 | tf_op jit(solution)/shard_map/ppermute | solution.py:45
  3.0 6.1 %collective-permute-start = (bf16[32,2048]{1,0:T(8,128)(2,1)}, bf16[32,2048]{1,0:T(8,128)(2,1)S(1)}, u32[]{:S(2)}, u32[]{:S(2)}) collective-permute-start(bf16[32,2048]{1,0:T(8,128)(2,1)} %hidden_ref.1), channel_id=1, source_target_pairs={{4,0},{8,4},{12,8},{14,12},{10,14},{6,10},{2,6},{0,2},{5,1},{9,5},... | collective-permute-start | bytes 393224 | tf_op jit(solution)/shard_map/ppermute | solution.py:48
  7.3 5.3 %collective-permute-start.3 = (bf16[32,2048]{1,0:T(8,128)(2,1)S(1)}, bf16[32,2048]{1,0:T(8,128)(2,1)S(1)}, u32[]{:S(2)}, u32[]{:S(2)}) collective-permute-start(bf16[32,2048]{1,0:T(8,128)(2,1)S(1)} %collective-permute-done.1), channel_id=1, source_target_pairs={{0,4},{4,8},{8,12},{12,14},{14,10},{10,6},{6,2},{2,0},{1,5},{5,9},... | collective-permute-start | bytes 393224 | tf_op jit(solution)/shard_map/ppermute | solution.py:45
  9.2 5.1 %collective-permute-start.2 = (bf16[32,2048]{1,0:T(8,128)(2,1)S(1)}, bf16[32,2048]{1,0:T(8,128)(2,1)S(1)}, u32[]{:S(2)}, u32[]{:S(2)}) collective-permute-start(bf16[32,2048]{1,0:T(8,128)(2,1)S(1)} %collective-permute-done.refs_1_), channel_id=1, source_target_pairs={{4,0},{8,4},{12,8},{14,12},{10,14},{6,10},{2,6},{0,2},{5,1},{9,5},... | collective-permute-start | bytes 393224 | tf_op jit(solution)/shard_map/ppermute | solution.py:48
  11.1 8.6 %copy-start.9 = (f32[2048]{0:T(1024)S(1)}, f32[2048]{0:T(1024)}, u32[]{:S(2)}) copy-start(f32[2048]{0:T(1024)} %param.22) | copy-start | bytes 24580
  12.7 5.0 %collective-permute-start.5 = (bf16[32,2048]{1,0:T(8,128)(2,1)S(1)}, bf16[32,2048]{1,0:T(8,128)(2,1)S(1)}, u32[]{:S(2)}, u32[]{:S(2)}) collective-permute-start(bf16[32,2048]{1,0:T(8,128)(2,1)S(1)} %collective-permute-done.3), channel_id=1, source_target_pairs={{0,4},{4,8},{8,12},{12,14},{14,10},{10,6},{6,2},{2,0},{1,5},{5,9},... | collective-permute-start | bytes 393224 | tf_op jit(solution)/shard_map/ppermute | solution.py:45
  14.3 5.0 %collective-permute-start.4 = (bf16[32,2048]{1,0:T(8,128)(2,1)S(1)}, bf16[32,2048]{1,0:T(8,128)(2,1)S(1)}, u32[]{:S(2)}, u32[]{:S(2)}) collective-permute-start(bf16[32,2048]{1,0:T(8,128)(2,1)S(1)} %collective-permute-done.2), channel_id=1, source_target_pairs={{4,0},{8,4},{12,8},{14,12},{10,14},{6,10},{2,6},{0,2},{5,1},{9,5},... | collective-permute-start | bytes 393224 | tf_op jit(solution)/shard_map/ppermute | solution.py:48
  17.7 4.3 %collective-permute-start.6 = (bf16[16,2048]{1,0:T(8,128)(2,1)S(1)}, bf16[16,2048]{1,0:T(8,128)(2,1)S(1)}, u32[]{:S(2)}, u32[]{:S(2)}) collective-permute-start(bf16[16,2048]{1,0:T(8,128)(2,1)S(1)} %slice.100), channel_id=1, source_target_pairs={{0,4},{4,8},{8,12},{12,14},{14,10},{10,6},{6,2},{2,0},{1,5},{5,9},... | collective-permute-start | bytes 196616 | tf_op jit(solution)/shard_map/ppermute | solution.py:45
  19.3 4.3 %collective-permute-start.7 = (bf16[16,2048]{1,0:T(8,128)(2,1)S(1)}, bf16[16,2048]{1,0:T(8,128)(2,1)S(1)}, u32[]{:S(2)}, u32[]{:S(2)}) collective-permute-start(bf16[16,2048]{1,0:T(8,128)(2,1)S(1)} %slice.101), channel_id=1, source_target_pairs={{4,0},{8,4},{12,8},{14,12},{10,14},{6,10},{2,6},{0,2},{5,1},{9,5},... | collective-permute-start | bytes 196616 | tf_op jit(solution)/shard_map/ppermute | solution.py:48
  23.6 6.8 %copy-start.11 = (s32[32,8]{0,1:T(8,128)S(1)}, s32[32,8]{0,1:T(8,128)}, u32[]{:S(2)}) copy-start(s32[32,8]{0,1:T(8,128)} %param.19) | copy-start | bytes 3076
  23.6 6.9 %copy-start.12 = (s32[32,8]{0,1:T(8,128)S(1)}, s32[32,8]{0,1:T(8,128)}, u32[]{:S(2)}) copy-start(s32[32,8]{0,1:T(8,128)} %param.20) | copy-start | bytes 3076
  23.6 7.0 %copy-start.7 = (s32[16]{0:T(128)S(1)}, s32[16]{0:T(128)}, u32[]{:S(2)}) copy-start(s32[16]{0:T(128)} %param.21) | copy-start | bytes 196
  23.6 8.3 %copy-start.13 = (s32[1,32]{1,0:T(1,128)S(1)}, s32[1,32]{1,0:T(1,128)}, u32[]{:S(2)}) copy-start(s32[1,32]{1,0:T(1,128)} %length_ref.1) | copy-start | bytes 388
  25.6 13.5 %all-to-all-start = ((bf16[8,32,640]{2,1,0:T(8,128)(2,1)}), bf16[8,32,640]{2,1,0:T(8,128)(2,1)S(1)}, u32[]{:S(2)}, u32[]{:S(2)}) async-start(bf16[8,32,640]{2,1,0:T(8,128)(2,1)} %project.1), calls=%async_computation | async-start | bytes 655360 | tf_op jit(solution)/shard_map/all_to_all | solution.py:492
  31.4 0.6 copy-start.5
  39.1 0.7 copy-start.8
  50.6 11.7 %all-to-all-start.1 = ((bf16[8,32,512]{2,1,0:T(8,128)(2,1)}), bf16[8,32,512]{2,1,0:T(8,128)(2,1)S(1)}, u32[]{:S(2)}, u32[]{:S(2)}) async-start(bf16[8,32,512]{2,1,0:T(8,128)(2,1)} %ragged_attention.1.refs_1_), calls=%async_computation.1 | async-start | bytes 524288 | tf_op jit(solution)/shard_map/all_to_all | solution.py:500
  54.0 1.0 copy-start.2
  55.0 1.6 %copy-start.3 = (bf16[512,2048]{1,0:T(8,128)(2,1)S(1)}, bf16[512,2048]{1,0:T(8,128)(2,1)}, u32[]{:S(2)}) copy-start(bf16[512,2048]{1,0:T(8,128)(2,1)} %refs_0_.3) | copy-start | bytes 6291460
  63.5 4.8 %collective-permute-start.9 = (bf16[32,1024]{1,0:T(8,128)(2,1)S(1)}, bf16[32,1024]{1,0:T(8,128)(2,1)S(1)}, u32[]{:S(2)}, u32[]{:S(2)}) collective-permute-start(bf16[32,1024]{1,0:T(8,128)(2,1)S(1)} %get-tuple-element.22), channel_id=1, source_target_pairs={{0,4},{4,8},{8,12},{12,14},{14,10},{10,6},{6,2},{2,0},{1,5},{5,9},... | collective-permute-start | bytes 196616 | tf_op jit(solution)/shard_map/ppermute | solution.py:45
  64.2 5.1 %collective-permute-start.13 = (bf16[32,1024]{1,0:T(8,128)(2,1)S(1)}, bf16[32,1024]{1,0:T(8,128)(2,1)S(1)}, u32[]{:S(2)}, u32[]{:S(2)}) collective-permute-start(bf16[32,1024]{1,0:T(8,128)(2,1)S(1)} %get-tuple-element.24), channel_id=1, source_target_pairs={{4,0},{8,4},{12,8},{14,12},{10,14},{6,10},{2,6},{0,2},{5,1},{9,5},... | collective-permute-start | bytes 196616 | tf_op jit(solution)/shard_map/ppermute | solution.py:48
  68.3 14.3 %copy-start.1 = (bf16[1,768,2048]{2,1,0:T(8,128)(2,1)S(1)}, bf16[1,768,2048]{2,1,0:T(8,128)(2,1)}, u32[]{:S(2)}) copy-start(bf16[1,768,2048]{2,1,0:T(8,128)(2,1)} %param.29) | copy-start | bytes 9437188
  68.4 5.9 %collective-permute-start.10 = (bf16[32,2048]{1,0:T(8,128)(2,1)S(1)}, bf16[32,2048]{1,0:T(8,128)(2,1)S(1)}, u32[]{:S(2)}, u32[]{:S(2)}) collective-permute-start(bf16[32,2048]{1,0:T(8,128)(2,1)S(1)} %pad_maximum_fusion.1), channel_id=1, source_target_pairs={{0,4},{4,8},{8,12},{12,14},{14,10},{10,6},{6,2},{2,0},{1,5},{5,9},... | collective-permute-start | bytes 393224 | tf_op jit(solution)/shard_map/ppermute | solution.py:45
  69.3 6.1 %collective-permute-start.14 = (bf16[32,2048]{1,0:T(8,128)(2,1)S(1)}, bf16[32,2048]{1,0:T(8,128)(2,1)S(1)}, u32[]{:S(2)}, u32[]{:S(2)}) collective-permute-start(bf16[32,2048]{1,0:T(8,128)(2,1)S(1)} %pad_maximum_fusion.2), channel_id=1, source_target_pairs={{4,0},{8,4},{12,8},{14,12},{10,14},{6,10},{2,6},{0,2},{5,1},{9,5},... | collective-permute-start | bytes 393224 | tf_op jit(solution)/shard_map/ppermute | solution.py:48
  74.2 5.0 %collective-permute-start.11 = (bf16[32,2048]{1,0:T(8,128)(2,1)S(1)}, bf16[32,2048]{1,0:T(8,128)(2,1)S(1)}, u32[]{:S(2)}, u32[]{:S(2)}) collective-permute-start(bf16[32,2048]{1,0:T(8,128)(2,1)S(1)} %fusion.6), channel_id=1, source_target_pairs={{0,4},{4,8},{8,12},{12,14},{14,10},{10,6},{6,2},{2,0},{1,5},{5,9},... | collective-permute-start | bytes 393224 | tf_op jit(solution)/shard_map/ppermute | solution.py:45
  75.4 5.6 %collective-permute-start.15 = (bf16[32,2048]{1,0:T(8,128)(2,1)S(1)}, bf16[32,2048]{1,0:T(8,128)(2,1)S(1)}, u32[]{:S(2)}, u32[]{:S(2)}) collective-permute-start(bf16[32,2048]{1,0:T(8,128)(2,1)S(1)} %fusion.4), channel_id=1, source_target_pairs={{4,0},{8,4},{12,8},{14,12},{10,14},{6,10},{2,6},{0,2},{5,1},{9,5},... | collective-permute-start | bytes 393224 | tf_op jit(solution)/shard_map/ppermute | solution.py:48
  80.0 6.0 %collective-permute-start.12 = (bf16[32,2048]{1,0:T(8,128)(2,1)}, bf16[32,2048]{1,0:T(8,128)(2,1)}, u32[]{:S(2)}, u32[]{:S(2)}) collective-permute-start(bf16[32,2048]{1,0:T(8,128)(2,1)} %fusion.7), channel_id=1, source_target_pairs={{0,4},{4,8},{8,12},{12,14},{14,10},{10,6},{6,2},{2,0},{1,5},{5,9},... | collective-permute-start | bytes 393224 | tf_op jit(solution)/shard_map/ppermute | solution.py:45
  81.7 5.3 %collective-permute-start.16 = (bf16[32,2048]{1,0:T(8,128)(2,1)}, bf16[32,2048]{1,0:T(8,128)(2,1)}, u32[]{:S(2)}, u32[]{:S(2)}) collective-permute-start(bf16[32,2048]{1,0:T(8,128)(2,1)} %fusion.5), channel_id=1, source_target_pairs={{4,0},{8,4},{12,8},{14,12},{10,14},{6,10},{2,6},{0,2},{5,1},{9,5},... | collective-permute-start | bytes 393224 | tf_op jit(solution)/shard_map/ppermute | solution.py:48
  82.7 27.0 %collective-permute-start.25 = (bf16[768,2048]{1,0:T(8,128)(2,1)S(1)}, bf16[768,2048]{1,0:T(8,128)(2,1)S(1)}, u32[]{:S(2)}, u32[]{:S(2)}) collective-permute-start(bf16[768,2048]{1,0:T(8,128)(2,1)S(1)} %bitcast.51), channel_id=1, source_target_pairs={{0,1},{1,0},{2,3},{3,2},{4,5},{5,4},{6,7},{7,6},{8,9},{9,8},{10,11... | collective-permute-start | bytes 9437192 | tf_op jit(solution)/shard_map/ppermute | solution.py:450
  82.7 2.8 %copy-start = (bf16[1,2048,1536]{2,1,0:T(8,128)(2,1)S(1)}, bf16[1,2048,1536]{2,1,0:T(8,128)(2,1)}, u32[]{:S(2)}) copy-start(bf16[1,2048,1536]{2,1,0:T(8,128)(2,1)} %param.28) | copy-start | bytes 18874372
  85.5 1.5 %copy-start.10 = (f32[2048]{0:T(1024)S(1)}, f32[2048]{0:T(1024)}, u32[]{:S(2)}) copy-start(f32[2048]{0:T(1024)} %param.23) | copy-start | bytes 24580
  85.5 1.6 %copy-start.4 = (bf16[32,2048]{1,0:T(8,128)(2,1)S(1)}, bf16[32,2048]{1,0:T(8,128)(2,1)}, u32[]{:S(2)}) copy-start(bf16[32,2048]{1,0:T(8,128)(2,1)} %hidden_ref.1) | copy-start | bytes 393220
  85.5 1.6 %copy-start.6 = (bf16[32,128]{1,0:T(8,128)(2,1)S(1)}, bf16[32,128]{1,0:T(8,128)(2,1)}, u32[]{:S(2)}) copy-start(bf16[32,128]{1,0:T(8,128)(2,1)} %copy-done.5) | copy-start | bytes 24580
  88.2 5.5 %collective-permute-start.18 = (bf16[32,2176]{1,0:T(8,128)(2,1)S(1)}, bf16[32,2176]{1,0:T(8,128)(2,1)S(1)}, u32[]{:S(2)}, u32[]{:S(2)}) collective-permute-start(bf16[32,2176]{1,0:T(8,128)(2,1)S(1)} %get-tuple-element.26), channel_id=1, source_target_pairs={{0,4},{4,8},{8,12},{12,14},{14,10},{10,6},{6,2},{2,0},{1,5},{5,9},... | collective-permute-start | bytes 417800 | tf_op jit(solution)/shard_map/ppermute | solution.py:45
  88.7 6.1 %collective-permute-start.17 = (bf16[32,2176]{1,0:T(8,128)(2,1)S(1)}, bf16[32,2176]{1,0:T(8,128)(2,1)S(1)}, u32[]{:S(2)}, u32[]{:S(2)}) collective-permute-start(bf16[32,2176]{1,0:T(8,128)(2,1)S(1)} %get-tuple-element.26), channel_id=1, source_target_pairs={{4,0},{8,4},{12,8},{14,12},{10,14},{6,10},{2,6},{0,2},{5,1},{9,5},... | collective-permute-start | bytes 417800 | tf_op jit(solution)/shard_map/ppermute | solution.py:48
  93.7 5.1 %collective-permute-start.20 = (bf16[32,2176]{1,0:T(8,128)(2,1)S(1)}, bf16[32,2176]{1,0:T(8,128)(2,1)S(1)}, u32[]{:S(2)}, u32[]{:S(2)}) collective-permute-start(bf16[32,2176]{1,0:T(8,128)(2,1)S(1)} %collective-permute-done.18), channel_id=1, source_target_pairs={{0,4},{4,8},{8,12},{12,14},{14,10},{10,6},{6,2},{2,0},{1,5},{5,9},... | collective-permute-start | bytes 417800 | tf_op jit(solution)/shard_map/ppermute | solution.py:45
  94.8 5.3 %collective-permute-start.19 = (bf16[32,2176]{1,0:T(8,128)(2,1)S(1)}, bf16[32,2176]{1,0:T(8,128)(2,1)S(1)}, u32[]{:S(2)}, u32[]{:S(2)}) collective-permute-start(bf16[32,2176]{1,0:T(8,128)(2,1)S(1)} %collective-permute-done.17.refs_1_), channel_id=1, source_target_pairs={{4,0},{8,4},{12,8},{14,12},{10,14},{6,10},{2,6},{0,2},{5,1},{9,5},... | collective-permute-start | bytes 417800 | tf_op jit(solution)/shard_map/ppermute | solution.py:48
  98.7 5.2 %collective-permute-start.22 = (bf16[32,2176]{1,0:T(8,128)(2,1)S(1)}, bf16[32,2176]{1,0:T(8,128)(2,1)S(1)}, u32[]{:S(2)}, u32[]{:S(2)}) collective-permute-start(bf16[32,2176]{1,0:T(8,128)(2,1)S(1)} %collective-permute-done.20), channel_id=1, source_target_pairs={{0,4},{4,8},{8,12},{12,14},{14,10},{10,6},{6,2},{2,0},{1,5},{5,9},... | collective-permute-start | bytes 417800 | tf_op jit(solution)/shard_map/ppermute | solution.py:45
  100.1 5.1 %collective-permute-start.21 = (bf16[32,2176]{1,0:T(8,128)(2,1)S(1)}, bf16[32,2176]{1,0:T(8,128)(2,1)S(1)}, u32[]{:S(2)}, u32[]{:S(2)}) collective-permute-start(bf16[32,2176]{1,0:T(8,128)(2,1)S(1)} %collective-permute-done.19.refs_1_), channel_id=1, source_target_pairs={{4,0},{8,4},{12,8},{14,12},{10,14},{6,10},{2,6},{0,2},{5,1},{9,5},... | collective-permute-start | bytes 417800 | tf_op jit(solution)/shard_map/ppermute | solution.py:48
  103.9 4.3 %collective-permute-start.23 = (bf16[16,2176]{1,0:T(8,128)(2,1)S(1)}, bf16[16,2176]{1,0:T(8,128)(2,1)S(1)}, u32[]{:S(2)}, u32[]{:S(2)}) collective-permute-start(bf16[16,2176]{1,0:T(8,128)(2,1)S(1)} %slice.106), channel_id=1, source_target_pairs={{0,4},{4,8},{8,12},{12,14},{14,10},{10,6},{6,2},{2,0},{1,5},{5,9},... | collective-permute-start | bytes 208904 | tf_op jit(solution)/shard_map/ppermute | solution.py:45
  105.1 4.5 %collective-permute-start.24 = (bf16[16,2176]{1,0:T(8,128)(2,1)S(1)}, bf16[16,2176]{1,0:T(8,128)(2,1)S(1)}, u32[]{:S(2)}, u32[]{:S(2)}) collective-permute-start(bf16[16,2176]{1,0:T(8,128)(2,1)S(1)} %slice.107), channel_id=1, source_target_pairs={{4,0},{8,4},{12,8},{14,12},{10,14},{6,10},{2,6},{0,2},{5,1},{9,5},... | collective-permute-start | bytes 208904 | tf_op jit(solution)/shard_map/ppermute | solution.py:48
  115.4 4.3 %collective-permute-start.26 = (bf16[32,1024]{1,0:T(8,128)(2,1)S(1)}, bf16[32,1024]{1,0:T(8,128)(2,1)S(1)}, u32[]{:S(2)}, u32[]{:S(2)}) collective-permute-start(bf16[32,1024]{1,0:T(8,128)(2,1)S(1)} %get-tuple-element.30), channel_id=1, source_target_pairs={{0,4},{4,8},{8,12},{12,14},{14,10},{10,6},{6,2},{2,0},{1,5},{5,9},... | collective-permute-start | bytes 196616 | tf_op jit(solution)/shard_map/ppermute | solution.py:45
  115.7 4.4 %collective-permute-start.30 = (bf16[32,1024]{1,0:T(8,128)(2,1)S(1)}, bf16[32,1024]{1,0:T(8,128)(2,1)S(1)}, u32[]{:S(2)}, u32[]{:S(2)}) collective-permute-start(bf16[32,1024]{1,0:T(8,128)(2,1)S(1)} %get-tuple-element.32), channel_id=1, source_target_pairs={{4,0},{8,4},{12,8},{14,12},{10,14},{6,10},{2,6},{0,2},{5,1},{9,5},... | collective-permute-start | bytes 196616 | tf_op jit(solution)/shard_map/ppermute | solution.py:48
  119.8 5.0 %collective-permute-start.27 = (bf16[32,2048]{1,0:T(8,128)(2,1)S(1)}, bf16[32,2048]{1,0:T(8,128)(2,1)S(1)}, u32[]{:S(2)}, u32[]{:S(2)}) collective-permute-start(bf16[32,2048]{1,0:T(8,128)(2,1)S(1)} %pad_maximum_fusion.3), channel_id=1, source_target_pairs={{0,4},{4,8},{8,12},{12,14},{14,10},{10,6},{6,2},{2,0},{1,5},{5,9},... | collective-permute-start | bytes 393224 | tf_op jit(solution)/shard_map/ppermute | solution.py:45
  120.1 5.0 %collective-permute-start.31 = (bf16[32,2048]{1,0:T(8,128)(2,1)S(1)}, bf16[32,2048]{1,0:T(8,128)(2,1)S(1)}, u32[]{:S(2)}, u32[]{:S(2)}) collective-permute-start(bf16[32,2048]{1,0:T(8,128)(2,1)S(1)} %pad_maximum_fusion.4), channel_id=1, source_target_pairs={{4,0},{8,4},{12,8},{14,12},{10,14},{6,10},{2,6},{0,2},{5,1},{9,5},... | collective-permute-start | bytes 393224 | tf_op jit(solution)/shard_map/ppermute | solution.py:48
  124.8 5.0 %collective-permute-start.28 = (bf16[32,2048]{1,0:T(8,128)(2,1)S(1)}, bf16[32,2048]{1,0:T(8,128)(2,1)S(1)}, u32[]{:S(2)}, u32[]{:S(2)}) collective-permute-start(bf16[32,2048]{1,0:T(8,128)(2,1)S(1)} %fusion.2), channel_id=1, source_target_pairs={{0,4},{4,8},{8,12},{12,14},{14,10},{10,6},{6,2},{2,0},{1,5},{5,9},... | collective-permute-start | bytes 393224 | tf_op jit(solution)/shard_map/ppermute | solution.py:45
  125.2 5.0 %collective-permute-start.32 = (bf16[32,2048]{1,0:T(8,128)(2,1)S(1)}, bf16[32,2048]{1,0:T(8,128)(2,1)S(1)}, u32[]{:S(2)}, u32[]{:S(2)}) collective-permute-start(bf16[32,2048]{1,0:T(8,128)(2,1)S(1)} %fusion), channel_id=1, source_target_pairs={{4,0},{8,4},{12,8},{14,12},{10,14},{6,10},{2,6},{0,2},{5,1},{9,5},... | collective-permute-start | bytes 393224 | tf_op jit(solution)/shard_map/ppermute | solution.py:48
  129.9 5.0 %collective-permute-start.29 = (bf16[32,2048]{1,0:T(8,128)(2,1)S(1)}, bf16[32,2048]{1,0:T(8,128)(2,1)S(1)}, u32[]{:S(2)}, u32[]{:S(2)}) collective-permute-start(bf16[32,2048]{1,0:T(8,128)(2,1)S(1)} %fusion.3), channel_id=1, source_target_pairs={{0,4},{4,8},{8,12},{12,14},{14,10},{10,6},{6,2},{2,0},{1,5},{5,9},... | collective-permute-start | bytes 393224 | tf_op jit(solution)/shard_map/ppermute | solution.py:45
  130.2 5.0 %collective-permute-start.33 = (bf16[32,2048]{1,0:T(8,128)(2,1)S(1)}, bf16[32,2048]{1,0:T(8,128)(2,1)S(1)}, u32[]{:S(2)}, u32[]{:S(2)}) collective-permute-start(bf16[32,2048]{1,0:T(8,128)(2,1)S(1)} %fusion.1), channel_id=1, source_target_pairs={{4,0},{8,4},{12,8},{14,12},{10,14},{6,10},{2,6},{0,2},{5,1},{9,5},... | collective-permute-start | bytes 393224 | tf_op jit(solution)/shard_map/ppermute | solution.py:48
